TPU v7x, 128 devices: a whole 4x4x4 slice. The times are simulated.
128 devices in a mesh: sa: 8 (over x_lo, y), sb: 16 (over z, x_hi, core).
Axes of the slice: x: 4 (x_hi: 2, x_lo: 2; x = x_hi * 2 + x_lo), y: 4, z: 4, core: 2. Of those that a mesh axis runs over, the one named last changes fastest.
Arguments:
- gate_signal: bfloat16 [8192, 4096], P(('sa', 'sb')), may hold values from -6 to 6
- key_signal: bfloat16 [8192, 4096], P(('sa', 'sb')), may hold values from -6 to 6
- value_signal: bfloat16 [8192, 4096], P(('sa', 'sb')), may hold values from -6 to 6
- long_filter: bfloat16 [8192, 4096], P(('sa', 'sb')), may hold values from -2 to 2
- skip_gain: float32 [4096], replicated, may hold values from 0.5 to 1.5
- head_weight: bfloat16 [4096, 32, 384], P(None, 'sb'), may hold values from -0.5 to 0.5
Outputs:
- mixed: bfloat16 [8192, 4096], P(('sa', 'sb'))
- attended: bfloat16 [8192, 4096], P(('sa', 'sb'))
All inputs are finite; a program needn't handle non-finite values.
Results may differ from a plain program's by a relative error of at most 0.025.
The roundings to bfloat16 on the way count: a program that leaves them out, or rounds other values in their place, can miss the bound.
Values may be sent and summed in bfloat16 or wider, within the bound.
No kernel may reach another device: no remote copies, remote signals or barrier semaphores. Data moves between devices by JAX's collectives and lax.ppermute only.
A program may use at most 192 MiB of HBM per device.

v0:
```python
import math

import jax
import jax.numpy as jnp
from jax import lax
from jax.sharding import PartitionSpec as P

HIGH = lax.Precision.HIGHEST


def fourier_table(left_count, right_count, period):
    left_index = jnp.arange(left_count, dtype=jnp.int32)[:, None]
    right_index = jnp.arange(right_count, dtype=jnp.int32)[None, :]
    phase = (left_index * right_index % period).astype(jnp.float32) * (2.0 * math.pi / period)
    return (jnp.cos(phase), jnp.sin(phase))


def to_channels(stacked, tok_rows, chan_block, devices):
    items = stacked.shape[0]
    shaped = stacked.reshape(items, devices, chan_block, 1, tok_rows)
    moved = lax.all_to_all(shaped, ("sa", "sb"), split_axis=1, concat_axis=3, tiled=True)
    return moved.reshape(items, chan_block, devices * tok_rows)


def to_positions(layer_out, tok_rows, chan_block, devices):
    shaped = layer_out.reshape(1, chan_block, devices, tok_rows)
    moved = lax.all_to_all(shaped, ("sa", "sb"), split_axis=2, concat_axis=0, tiled=True)
    return moved.reshape(devices * chan_block, tok_rows).T


def per_device(gate_signal, key_signal, value_signal, long_filter, skip_gain, head_weight):
    tok_rows, chan_count = gate_signal.shape
    devices = lax.axis_size(("sa", "sb"))
    inner_count = lax.axis_size("sb")
    chan_block = chan_count // devices
    head_local = head_weight.shape[1]
    head_size = head_weight.shape[2] // 3
    product = (key_signal.astype(jnp.float32) * value_signal.astype(jnp.float32)).astype(
        jnp.bfloat16
    )
    stacked = jnp.transpose(jnp.stack([product, long_filter, gate_signal], axis=0), (0, 2, 1))
    columns = to_channels(stacked, tok_rows, chan_block, devices)
    first_len = 2 * tok_rows
    total_len = first_len * devices
    cos_first, sin_first = fourier_table(tok_rows, first_len, first_len)
    cos_second, sin_second = fourier_table(devices, devices, devices)
    twist_cos, twist_sin = fourier_table(first_len, devices, total_len)

    def forward(signal):
        real_a = jnp.einsum("cnm,nk->ckm", signal, cos_first, precision=HIGH)
        imag_a = -jnp.einsum("cnm,nk->ckm", signal, sin_first, precision=HIGH)
        real_b = real_a * twist_cos + imag_a * twist_sin
        imag_b = imag_a * twist_cos - real_a * twist_sin
        real_x = jnp.einsum("ckm,mj->ckj", real_b, cos_second, precision=HIGH) + jnp.einsum(
            "ckm,mj->ckj", imag_b, sin_second, precision=HIGH
        )
        imag_x = jnp.einsum("ckm,mj->ckj", imag_b, cos_second, precision=HIGH) - jnp.einsum(
            "ckm,mj->ckj", real_b, sin_second, precision=HIGH
        )
        return (real_x, imag_x)

    signal = columns[0].astype(jnp.float32)
    shaped_signal = signal.reshape(chan_block, tok_rows, devices)
    shaped_taps = columns[1].astype(jnp.float32).reshape(chan_block, tok_rows, devices)
    real_s, imag_s = forward(shaped_signal)
    real_h, imag_h = forward(shaped_taps)
    real_y = real_s * real_h - imag_s * imag_h
    imag_y = real_s * imag_h + imag_s * real_h
    real_c = jnp.einsum("ckj,mj->ckm", real_y, cos_second, precision=HIGH) - jnp.einsum(
        "ckj,mj->ckm", imag_y, sin_second, precision=HIGH
    )
    imag_c = jnp.einsum("ckj,mj->ckm", imag_y, cos_second, precision=HIGH) + jnp.einsum(
        "ckj,mj->ckm", real_y, sin_second, precision=HIGH
    )
    real_d = real_c * twist_cos - imag_c * twist_sin
    imag_d = imag_c * twist_cos + real_c * twist_sin
    conv = (
        jnp.einsum("ckm,nk->cnm", real_d, cos_first, precision=HIGH)
        - jnp.einsum("ckm,nk->cnm", imag_d, sin_first, precision=HIGH)
    ) * (1.0 / total_len)
    conv = conv.reshape(chan_block, tok_rows * devices)
    my_block = lax.axis_index(("sa", "sb"))
    local_gain = lax.dynamic_slice_in_dim(skip_gain, my_block * chan_block, chan_block, 0)
    filtered = lax.optimization_barrier((conv + local_gain[:, None] * signal).astype(jnp.bfloat16))
    layer_out = (columns[2].astype(jnp.float32) * filtered.astype(jnp.float32)).astype(jnp.bfloat16)
    mixed = to_positions(layer_out, tok_rows, chan_block, devices)
    flat_weight = head_weight.reshape(chan_count, head_local * 3 * head_size)
    projected = jnp.dot(
        lax.all_gather(mixed, "sb", axis=0, tiled=True),
        flat_weight,
        preferred_element_type=jnp.float32,
    )
    group_rows = projected.shape[0]
    projected = projected.reshape(group_rows, head_local, 3 * head_size)
    queries = projected[:, :, :head_size].astype(jnp.bfloat16)
    keys = projected[:, :, head_size : 2 * head_size].astype(jnp.bfloat16)
    values = projected[:, :, 2 * head_size :].astype(jnp.bfloat16)
    query_pos = lax.axis_index("sa") * group_rows + jnp.arange(group_rows, dtype=jnp.int32)
    score_scale = 1.0 / math.sqrt(head_size)
    best = jnp.full((head_local, group_rows), -1e30, jnp.float32)
    piece_keys = lax.all_gather(keys, "sa", axis=0, tiled=True)
    piece_values = lax.all_gather(values, "sa", axis=0, tiled=True)
    scores = (
        jnp.einsum("qhd,khd->hqk", queries, piece_keys, preferred_element_type=jnp.float32)
        * score_scale
    )
    key_pos = jnp.arange(piece_keys.shape[0], dtype=jnp.int32)
    allowed = (key_pos[None, :] <= query_pos[:, None])[None, :, :]
    masked = jnp.where(allowed, scores, jnp.float32(-1e30))
    new_best = jnp.maximum(best, jnp.max(masked, axis=2))
    weights = jnp.where(allowed, jnp.exp(masked - new_best[:, :, None]), jnp.float32(0.0))
    total = jnp.sum(weights, axis=2)
    accum = jnp.einsum("hqk,khd->hqd", weights, piece_values.astype(jnp.float32), precision=HIGH)
    best, total, accum = (new_best, total, accum)
    head_out = (accum / total[:, :, None]).astype(jnp.bfloat16)
    head_out = jnp.transpose(head_out, (1, 0, 2)).reshape(
        inner_count, tok_rows, head_local * head_size
    )
    returned_heads = lax.all_to_all(head_out, "sb", split_axis=0, concat_axis=2, tiled=True)
    attended = returned_heads.reshape(tok_rows, inner_count * head_local * head_size)
    return (mixed, attended)


def solution(mesh):
    placed = (
        P(("sa", "sb"), None),
        P(("sa", "sb"), None),
        P(("sa", "sb"), None),
        P(("sa", "sb"), None),
        P(),
        P(None, "sb", None),
    )
    return jax.shard_map(
        per_device,
        mesh=mesh,
        in_specs=placed,
        out_specs=(P(("sa", "sb"), None), P(("sa", "sb"), None)),
        check_vma=False,
    )
```

profile of v0, /device:TPU:0, one launch (start us, length us, event | category | flops | bytes accessed | tf_op | source)
XLA Modules:
  0.0 410.1 jit_solution(3420438997320833095)
XLA Ops:
  7.2 1.3 fusion.61
  8.5 2.5 maximum_bitcast_fusion
  11.0 3.1 copy.41
  14.1 2.2 copy.60
  16.2 6.1 %reshape.129 = bf16[128,2,3072]{2,1,0:T(2,128)(2,1)} reshape(bf16[128,1,3,32,64]{4,3,2,1,0:T(8,128)(2,1)} %bitcast.154) | data formatting | bytes 3145728
  22.3 11.6 %all-to-all-start = ((bf16[128,2,3072]{2,1,0:T(2,128)(2,1)}), bf16[128,2,3072]{2,1,0:T(2,128)(2,1)}, u32[]{:S(2)}, u32[]{:S(2)}) async-start(bf16[128,2,3072]{2,1,0:T(2,128)(2,1)} %reshape.129), calls=%async_computation | async-start | bytes 3145728 | tf_op jit(solution)/shard_map/all_to_all | solution.py:21
  35.0 22.1 %all-to-all-done = bf16[128,2,3072]{2,1,0:T(2,128)(2,1)} async-done(((bf16[128,2,3072]{2,1,0:T(2,128)(2,1)}), bf16[128,2,3072]{2,1,0:T(2,128)(2,1)}, u32[]{:S(2)}, u32[]{:S(2)}) %all-to-all-start) | async-done | bytes 1572896 | tf_op jit(solution)/shard_map/all_to_all | solution.py:21
  57.1 4.9 %reshape.130 = bf16[128,1,3,32,64]{4,3,2,1,0:T(8,128)(2,1)S(1)} reshape(bf16[128,2,3072]{2,1,0:T(2,128)(2,1)} %all-to-all-done) | data formatting | bytes 3145728
  62.0 4.0 copy.43
  66.0 3.1 slice_convert_fusion.1
  70.1 1.2 fusion.93
  71.3 2.5 fusion.98
  73.7 1.3 copy.45
  75.1 2.2 reshape.114
  77.3 1.2 fusion.100
  78.5 1.2 fusion.95
  79.7 2.2 fusion.10
  81.9 2.2 fusion.12
  84.1 2.2 fusion.20
  86.4 2.2 fusion.18
  88.6 2.4 fusion.46
  91.0 2.3 fusion.37
  93.3 2.3 fusion.43
  95.6 2.7 multiply_add_fusion
  98.3 2.1 fusion.74
  100.4 2.5 fusion.76
  103.0 2.1 convolution_add_fusion
  105.1 2.1 convolution_subtract_fusion
  107.2 1.6 fusion.26
  108.9 1.6 fusion.52
  110.5 1.8 copy.47
  112.4 1.6 reshape.123
  114.0 2.6 fusion.56
  116.6 1.8 copy.44
  119.1 1.1 multiply_convert_fusion
  122.8 18.7 %all_to_all.45 = bf16[128,2,1024]{2,1,0:T(2,128)(2,1)S(1)} all-to-all(bf16[128,2,1024]{2,1,0:T(2,128)(2,1)S(1)} %reshape.131), channel_id=1, replica_groups=mesh['sa'=8,'sb'=16] {'sa','sb'}, dimensions={0} | all-to-all | bytes 1048576 | tf_op jit(solution)/shard_map/all_to_all | solution.py:27
  142.2 1.1 copy.49
  143.4 6.4 %copy.54 = bf16[512,8,2,384]{3,1,2,0:T(8,128)(2,1)} copy(bf16[512,8,2,384]{3,2,1,0:T(2,128)(2,1)} %bitcast.156) | data formatting | bytes 12582912
  149.8 8.8 %copy.50 = bf16[768,4096]{1,0:T(8,128)(2,1)} copy(bf16[768,4096]{0,1:T(8,128)(2,1)} %bitcast.152) | data formatting | bytes 12582912 | tf_op jit(solution)/shard_map/dot_general | solution.py:88
  158.6 54.4 %all-gather.4.cloned.1.call-done = bf16[1024,4096]{1,0:T(8,128)(2,1)} async-done(((bf16[64,4096]{1,0:T(8,128)(2,1)}), bf16[1024,4096]{1,0:T(8,128)(2,1)}) %all-gather.4.cloned.1.call-update) | async-done | bytes 8388624 | tf_op jit(solution)/shard_map/all_gather | solution.py:89
  213.0 11.0 %fusion.34 = bf16[1024,2,384]{2,0,1:T(8,128)(2,1)S(1)} fusion(bf16[2,384,4096]{2,1,0:T(8,128)(2,1)} %bitcast.157, bf16[1024,4096]{1,0:T(8,128)(2,1)} %all-gather.4.cloned.1.call-done), kind=kOutput, calls=%fused_computation.43 | convolution fusion | flops 6443237376 | bytes 16252928 | tf_op jit(solution)/shard_map/dot_general | solution.py:88
  224.0 1.2 fusion.204
  225.2 9.9 %iota_compare_fusion = pred[1024,8192]{1,0:T(8,128)(4,1)} fusion(s32[1024]{0:T(1024)S(1)} %iota_add_fusion), kind=kLoop, calls=%fused_computation.9 | loop fusion | flops 8388608 | bytes 8392704 | tf_op jit(solution)/shard_map/le | solution.py:108
  235.2 40.5 %all-gather.6.cloned.1.call-done = bf16[8192,2,128]{2,0,1:T(8,128)(2,1)} async-done(((bf16[1024,2,128]{2,0,1:T(8,128)(2,1)}), bf16[8192,2,128]{2,0,1:T(8,128)(2,1)}) %all-gather.6.cloned.1.call-update) | async-done | bytes 4194320 | tf_op jit(solution)/shard_map/all_gather | solution.py:101
  275.6 29.9 %fusion = (f32[2,1024]{1,0:T(2,128)S(1)}, f32[2,1024,8192]{2,1,0:T(8,128)}) fusion(pred[1024,8192]{1,0:T(8,128)(4,1)} %iota_compare_fusion, bf16[8192,2,128]{2,0,1:T(8,128)(2,1)} %all-gather.6.cloned.1.call-done, bf16[1024,2,384]{2,0,1:T(8,128)(2,1)S(1)} %fusion.34), kind=kOutput, calls=%fused_computation.2 | convolution fusion | flops 4345296896 | bytes 80224256 | tf_op jit(solution)/shard_map/qhd,khd->hqk/dot_general | solution.py:104
  305.6 24.6 %fusion.1 = f32[2,1024]{1,0:T(2,128)S(1)} fusion(f32[2,1024,8192]{2,1,0:T(8,128)} %get-tuple-element.11, f32[2,1024]{1,0:T(2,128)S(1)} %broadcast_maximum_fusion, pred[1024,8192]{1,0:T(8,128)(4,1)} %iota_compare_fusion), kind=kLoop, calls=%fused_computation.3 | loop fusion | flops 83884032 | bytes 75513856 | tf_op jit(solution)/shard_map/reduce_sum | solution.py:112
  330.2 52.3 %divide_convert_fusion = bf16[1024,2,128]{2,0,1:T(8,128)(2,1)S(1)} fusion(bf16[8192,2,128]{2,0,1:T(8,128)(2,1)} %all-gather.8.cloned.1.call-done, f32[2,1024,8192]{2,1,0:T(8,128)} %get-tuple-element.11, f32[2,1024]{1,0:T(2,128)S(1)} %broadcast_maximum_fusion, pred[1024,8192]{1,0:T(8,128)(4,1)} %iota_compare_fusion, f32[1024,2]{0,1:T(2,128)S(1)} %bitcast.168), kind=kOutput, calls=%fused_computation.56 | convolution fusion | flops 25837436928 | bytes 80232448 | tf_op jit(solution)/shard_map/hqk,khd->hqd/dot_general | solution.py:113
  383.4 18.9 %all_to_all.46 = bf16[16,64,256]{2,1,0:T(8,128)(2,1)S(1)} all-to-all(bf16[16,64,256]{2,1,0:T(8,128)(2,1)S(1)} %reshape.120), channel_id=1, replica_groups=mesh['sa'=8,'sb'=16] {'sb'}, dimensions={0} | all-to-all | bytes 1048576 | tf_op jit(solution)/shard_map/all_to_all | solution.py:119
  (23 shorter events, 7.7 us)
Async XLA Ops:
  22.3 34.8 %all-to-all-start = ((bf16[128,2,3072]{2,1,0:T(2,128)(2,1)}), bf16[128,2,3072]{2,1,0:T(2,128)(2,1)}, u32[]{:S(2)}, u32[]{:S(2)}) async-start(bf16[128,2,3072]{2,1,0:T(2,128)(2,1)} %reshape.129), calls=%async_computation | async-start | bytes 3145728 | tf_op jit(solution)/shard_map/all_to_all | solution.py:21
  34.0 179.0 %all-gather.4.cloned.1.call-start = ((), (), s32[]{:S(2)}) async-start(), calls=%async_computation.3 | async-start | bytes 8912896 | tf_op jit(solution)/shard_map/all_gather | solution.py:89
  77.3 2.4 copy-start
  143.3 132.3 %all-gather.6.cloned.1.call-start = ((), (), s32[]{:S(2)}) async-start(), calls=%async_computation.4 | async-start | bytes 4718592 | tf_op jit(solution)/shard_map/all_gather | solution.py:101
  225.2 105.0 %all-gather.8.cloned.1.call-start = ((), (), s32[]{:S(2)}) async-start(), calls=%async_computation.5 | async-start | bytes 4718592 | tf_op jit(solution)/shard_map/all_gather | solution.py:102
Sparse Core Ops, SparseCore 0:
  143.5 69.4 all-gather.3
  225.3 50.2 all-gather.5
  277.3 51.3 all-gather.7
where the time goes:
time: 418 us; the launch traced here: 410 us
  matrix products  130 us (31%)
  waiting for transfers between devices  117 us (28%)
  local copies, waits for them, and re-layouts  53.8 us (13%)
  other arithmetic  45.5 us (11%)
  blocking collectives  37.6 us (9%)
  between operations  14.4 us (3%)
  starting transfers between devices  11.7 us (3%)
    all_gather x1, waiting for transfers between devices, per_device(): lax.all_gather(mixed, 'sb', axis=0, tiled=True)  54.4 us
    dot_general x1, matrix products, per_device(): jnp.einsum('hqk,khd->hqd', weights, piece_values.astype(jnp.float32), pre...  52.3 us
    all_gather x1, waiting for transfers between devices, per_device(): piece_keys = lax.all_gather(keys, 'sa', axis=0, tiled=True)  40.5 us
    dot_general x1, matrix products, per_device(): jnp.einsum('qhd,khd->hqk', queries, piece_keys, preferred_element_type=jn...  29.9 us
    reduce_sum x1, other arithmetic, per_device(): total = jnp.sum(weights, axis=2)  24.6 us
    all_to_all x1, waiting for transfers between devices, to_channels(): lax.all_to_all(shaped, ('sa', 'sb'), split_axis=1, concat_axis=3, tiled=T...  22.1 us
    unnamed x8, local copies, waits for them, and re-layouts  19.6 us
    all_to_all x1, blocking collectives, per_device(): lax.all_to_all(head_out, 'sb', split_axis=0, concat_axis=2, tiled=True)  18.9 us
  transfers between devices with their start and end apart: 4, of which 3 were waited for; matrix products, arithmetic and copies ran while one was open for 20% of the time, Pallas kernels for 0%

commit v1 on v0

v1 whole, which is shorter than its diff:
```python
import itertools
import math

import jax
import jax.numpy as jnp
import ml_dtypes
import numpy as np
from jax import lax
from jax.experimental import pallas as pl
from jax.experimental.pallas import tpu as pltpu
from jax.sharding import Mesh, PartitionSpec as P

BF = jnp.bfloat16
F32 = jnp.float32
NAMES = ("xl", "yh", "yl", "z", "xh", "c")
SIZES = (2, 2, 2, 4, 2, 2)
ROWS = 64
DEVS = 128
SEQ = ROWS * DEVS
CHANS = 4096
HALF = CHANS // 2
HD = 128
VMEM_LIMIT = 56 * 1024 * 1024


def split16(table):
    table = np.asarray(table, np.float64)
    high = table.astype(np.float32).astype(ml_dtypes.bfloat16)
    low = (table - high.astype(np.float64)).astype(np.float32).astype(ml_dtypes.bfloat16)
    return high, low


def conv_tables():
    d = np.arange(DEVS)
    k1 = np.arange(DEVS) + 0.25
    r = np.arange(ROWS)
    outer = 2 * math.pi * np.outer(k1, d) / DEVS
    first = np.concatenate([np.cos(outer), -np.sin(outer)], axis=0)
    twist = 2 * math.pi * np.outer(k1, r) / SEQ
    twist_cos = np.tile(np.cos(twist), (1, 2)).astype(np.float32)
    twist_sin = np.tile(np.sin(twist), (1, 2)).astype(np.float32)
    inner = 2 * math.pi * np.outer(r, r) / ROWS
    eye = np.eye(2)
    cos, sin = np.kron(eye, np.cos(inner)), np.kron(eye, np.sin(inner))
    second = np.block([[cos, -sin], [sin, cos]])
    third = np.block([[cos, sin], [-sin, cos]])
    last = np.concatenate([np.cos(outer).T, -np.sin(outer).T], axis=1) / SEQ
    return (*split16(first), twist_cos, twist_sin, *split16(second), *split16(third), *split16(last))


def whole(shape):
    return pl.BlockSpec(shape, lambda *_: (0,) * len(shape), memory_space=pltpu.VMEM)


def params(**more):
    return pltpu.CompilerParams(vmem_limit_bytes=VMEM_LIMIT, **more)


def pack_kernel(key_ref, value_ref, taps_ref, out_ref):
    def both(ref, start):
        return jnp.concatenate(
            [ref[:, pl.ds(start, 128)].astype(F32), ref[:, pl.ds(start + HALF, 128)].astype(F32)], axis=0
        )

    for block in range(HALF // 128):
        start = block * 128
        product = (both(key_ref, start) * both(value_ref, start)).astype(BF).astype(F32)
        for which, tile in enumerate((product, both(taps_ref, start))):
            out_ref[block * 8 : block * 8 + 8, which] = tile.T.astype(BF).reshape(8, 16, 128)


def pack(key_signal, value_signal, long_filter):
    return pl.pallas_call(
        pack_kernel,
        out_shape=jax.ShapeDtypeStruct((DEVS, 2, 16, 128), BF),
        in_specs=[whole((ROWS, CHANS))] * 3,
        out_specs=whole((DEVS, 2, 16, 128)),
        compiler_params=params(),
        name="pack",
    )(key_signal, value_signal, long_filter)


def dot(a, b):
    return jnp.dot(a, b, preferred_element_type=F32)


def cut(x):
    high = x.astype(BF)
    return high, (x - high.astype(F32)).astype(BF)


def conv_kernel(
    recv_ref, gain_ref, w1h, w1l, tc_ref, ts_ref, m2h, m2l, m3h, m3l, w3h, w3l, out_ref, x_s, h_s, y_s
):
    x_s[...] = recv_ref[:, 0].astype(F32).reshape(DEVS * 16, 128)
    h_s[...] = recv_ref[:, 1].astype(F32).reshape(DEVS * 16, 128)
    tc = tc_ref[...]
    ts = ts_ref[...]

    def three(a, bh, bl):
        ah, al = cut(a)
        return dot(ah, bh) + (dot(al, bh) + dot(ah, bl))

    def step(it, carry):
        rows = [pl.ds(it * 2 + u, DEVS, stride=16) for u in range(2)]
        xs = [x_s[row, :] for row in rows]
        hs = [h_s[row, :] for row in rows]
        signal = jnp.concatenate([v.astype(BF) for v in xs + hs], axis=1)
        first = dot(w1h[...], signal) + dot(w1l[...], signal)
        stacked = []
        for u in range(4):
            re = first[:DEVS, u * 128 : u * 128 + 128]
            im = first[DEVS:, u * 128 : u * 128 + 128]
            stacked.append(jnp.concatenate([re * tc + im * ts, im * tc - re * ts], axis=1))
        spectrum = three(jnp.concatenate(stacked, axis=0), m2h[...], m2l[...])
        prods = []
        for u in range(2):
            s = spectrum[u * 128 : u * 128 + 128]
            h = spectrum[256 + u * 128 : 256 + u * 128 + 128]
            sr, si, hr, hi = s[:, :128], s[:, 128:], h[:, :128], h[:, 128:]
            prods.append(jnp.concatenate([sr * hr - si * hi, sr * hi + si * hr], axis=1))
        back = three(jnp.concatenate(prods, axis=0), m3h[...], m3l[...])
        outs = []
        for u in range(2):
            re = back[u * 128 : u * 128 + 128, :128]
            im = back[u * 128 : u * 128 + 128, 128:]
            outs.append(jnp.concatenate([re * tc - im * ts, im * tc + re * ts], axis=0))
        vh, vl = cut(jnp.concatenate(outs, axis=1))
        conv = dot(w3h[...], vh) + (dot(w3l[...], vh) + dot(w3h[...], vl))
        for u in range(2):
            gain = gain_ref[pl.ds(it * 2 + u, 1), :]
            y_s[rows[u], :] = conv[:, u * 128 : u * 128 + 128] + gain * xs[u]
        return carry

    lax.fori_loop(0, 8, step, 0)
    out_ref[...] = y_s[...].reshape(DEVS, 16, 128).astype(BF)


def convolve(recv, gain):
    tables = conv_tables()
    args = (recv, gain, *[jnp.asarray(t) for t in tables])
    return pl.pallas_call(
        conv_kernel,
        out_shape=jax.ShapeDtypeStruct((DEVS, 16, 128), BF),
        in_specs=[whole(a.shape) for a in args],
        out_specs=whole((DEVS, 16, 128)),
        scratch_shapes=[pltpu.VMEM((DEVS * 16, 128), F32)] * 3,
        compiler_params=params(),
        name="convolve",
    )(*args)


def gate_kernel(recv_ref, gate_ref, out_ref):
    for block in range(HALF // 128):
        tile = recv_ref[block * 8 : block * 8 + 8].astype(F32).reshape(128, 128).T
        for half in range(2):
            cols = pl.ds(half * HALF + block * 128, 128)
            part = tile[half * ROWS : half * ROWS + ROWS]
            out_ref[:, cols] = (gate_ref[:, cols].astype(F32) * part).astype(BF)


def apply_gate(recv, gate_signal):
    return pl.pallas_call(
        gate_kernel,
        out_shape=jax.ShapeDtypeStruct((ROWS, CHANS), BF),
        in_specs=[whole((DEVS, 16, 128)), whole((ROWS, CHANS))],
        out_specs=whole((ROWS, CHANS)),
        compiler_params=params(),
        name="apply_gate",
    )(recv, gate_signal)


def project_kernel(place_ref, *refs):
    shards = refs[:8]
    w_ref, out_ref, x_s, sems = refs[8:]

    @pl.when(pl.program_id(0) == 0)
    def _():
        copies = [
            pltpu.make_async_copy(shard, x_s.at[pl.ds(i * ROWS, ROWS), :], sems.at[i])
            for i, shard in enumerate(shards)
        ]
        for copy in copies:
            copy.start()
        for copy in copies:
            copy.wait()

    result = dot(x_s[...], w_ref[0])
    for slot, part in enumerate((1, 2, 0)):
        out_ref[0, slot] = result[:, part * HD : part * HD + HD].astype(BF)


def project(place, shards, weights):
    rows = 8 * ROWS
    return pl.pallas_call(
        project_kernel,
        out_shape=jax.ShapeDtypeStruct((4, 3, rows, HD), BF),
        grid_spec=pltpu.PrefetchScalarGridSpec(
            num_scalar_prefetch=1,
            grid=(4,),
            in_specs=[pl.BlockSpec(memory_space=pl.ANY)] * 8
            + [pl.BlockSpec((1, CHANS, 3 * HD), lambda i, place: (i // 2, 0, i % 2))],
            out_specs=pl.BlockSpec((1, 3, rows, HD), lambda i, place: (place[i], 0, 0, 0)),
            scratch_shapes=[pltpu.VMEM((rows, CHANS), BF), pltpu.SemaphoreType.DMA((8,))],
        ),
        compiler_params=params(),
        name="project",
    )(place, *shards, weights)


GROUP = 8 * ROWS
TILE = 256
SCALE = math.log2(math.e) / math.sqrt(HD)
EXTRA = 16


def attend_kernel(me_ref, q_ref, own_ref, sib_ref, out_ref, vt_s):
    me, my_z, my_xh, my_c = me_ref[0], me_ref[1], me_ref[2], me_ref[3]
    ones = jnp.ones((EXTRA, GROUP), BF)
    for side, ref in enumerate((own_ref, sib_ref)):
        for rel in range(8):
            vt_s[side, rel, :HD] = ref[rel, 1].astype(F32).T.astype(BF)
            vt_s[side, rel, HD:] = ones

    def inner_pos(index, core):
        z = (my_z + (index >> 7)) & 3
        xh = my_xh ^ ((index >> 6) & 1)
        return z * 256 + xh * 128 + core * 64 + (index & 63)

    row = lax.broadcasted_iota(jnp.int32, (GROUP, TILE), 0)
    col = lax.broadcasted_iota(jnp.int32, (GROUP, TILE), 1)

    for qrel in range(4):
        group = me ^ (qrel * 2)
        queries = [q_ref[qrel, t * TILE : t * TILE + TILE] for t in range(2)]

        def visit(rel, carry, masked):
            done = []
            for t in range(2):
                best, acc = carry[t]
                scores = []
                for side, ref in enumerate((own_ref, sib_ref)):
                    s = lax.dot_general(
                        ref[rel, 0], queries[t], (((1,), (1,)), ((), ())), preferred_element_type=F32
                    )
                    if masked:
                        key_pos = inner_pos(row, my_c ^ side)
                        query_pos = inner_pos(col + t * TILE, my_c)
                        s = jnp.where(key_pos <= query_pos, s, -1e30)
                    scores.append(s)
                top = jnp.maximum(
                    jnp.max(scores[0], axis=0, keepdims=True), jnp.max(scores[1], axis=0, keepdims=True)
                )
                new = jnp.maximum(best, top)
                shrink = jnp.exp2((best - new) * SCALE)
                acc = acc * shrink
                for side in range(2):
                    weight = jnp.exp2((scores[side] - new) * SCALE).astype(BF)
                    acc = acc + dot(vt_s[side, rel], weight)
                done.append((new, acc))
            return tuple(done)

        start = tuple(
            (jnp.full((1, TILE), -1e30, F32), jnp.zeros((HD + EXTRA, TILE), F32)) for _ in range(2)
        )
        carry = visit(qrel * 2, start, True)
        carry = lax.fori_loop(0, group, lambda g, cr: visit(g ^ me, cr, False), carry)
        for t in range(2):
            acc = carry[t][1]
            out = (acc[:HD] / acc[HD : HD + 1]).T.astype(BF)
            for part in range(TILE // ROWS):
                shard = t * (TILE // ROWS) + part
                z = (my_z + (shard >> 1)) & 3
                xh = my_xh ^ (shard & 1)
                out_ref[(group >> 1) * 8 + z * 2 + xh] = out[part * ROWS : part * ROWS + ROWS]


def attend(place, queries, own, sib):
    return pl.pallas_call(
        attend_kernel,
        out_shape=jax.ShapeDtypeStruct((32, ROWS, HD), BF),
        in_specs=[pl.BlockSpec(memory_space=pltpu.SMEM)]
        + [whole((4, GROUP, HD)), whole((8, 2, GROUP, HD)), whole((8, 2, GROUP, HD))],
        out_specs=whole((32, ROWS, HD)),
        scratch_shapes=[pltpu.VMEM((2, 8, HD + EXTRA, GROUP), BF)],
        compiler_params=params(),
        name="attend",
    )(place, queries, own, sib)


def shift(x, move):
    pairs = []
    for spot in itertools.product(*[range(n) for n in SIZES]):
        target = dict(zip(NAMES, spot))
        move(target)
        goal = [target[n] % size for n, size in zip(NAMES, SIZES)]
        pairs.append((int(np.ravel_multi_index(spot, SIZES)), int(np.ravel_multi_index(goal, SIZES))))
    return lax.ppermute(x, NAMES, pairs)


def along_z(x, step):
    def move(t):
        t["z"] = (t["z"] + step) % 4

    return shift(x, move)


def flip(x, **bits):
    def move(t):
        for name, bit in bits.items():
            t[name] ^= bit

    return shift(x, move)


def per_device(gate_signal, key_signal, value_signal, long_filter, skip_gain, head_weight):
    at = {name: lax.axis_index(name) for name in NAMES}
    device = lax.axis_index(NAMES)

    packed = pack(key_signal, value_signal, long_filter)
    recv = lax.all_to_all(packed, NAMES, split_axis=0, concat_axis=0, tiled=True)

    own_weight = head_weight.reshape(CHANS, 6 * HD)
    weights = jnp.stack([own_weight, flip(own_weight, c=1)])

    gain = lax.dynamic_slice_in_dim(skip_gain.reshape(2, HALF), device * 16, 16, 1)
    gain = jnp.repeat(gain.T, ROWS, axis=1)
    filtered = convolve(recv, gain)
    returned = lax.all_to_all(filtered, NAMES, split_axis=0, concat_axis=0, tiled=True)
    mixed = apply_gate(returned, gate_signal)

    from_z = [mixed, along_z(mixed, -1), along_z(mixed, -2), along_z(mixed, -3)]
    shards = []
    for part in from_z:
        shards += [part, flip(part, xh=1)]

    places = []
    for side in range(2):
        for i in range(2):
            places.append((at["xl"] ^ at["c"] ^ side) * 2 + (at["yh"] ^ i))
    projected = project(jnp.stack(places).astype(jnp.int32), shards, weights)

    kv, queries = [], []
    for rel in range(8):
        xl, yh, yl = rel >> 2, (rel >> 1) & 1, rel & 1
        part = projected[rel >> 1]
        part = part if yl == 0 else part[:2]
        got = part if rel == 0 else flip(part, xl=xl, yh=yh, yl=yl)
        kv.append(got[:2])
        if yl == 0:
            queries.append(got[2])
    own = jnp.stack(kv)
    sib = flip(own, c=1)
    group = at["xl"] * 4 + at["yh"] * 2 + at["yl"]
    place = jnp.stack([group, at["z"], at["xh"], at["c"]]).astype(jnp.int32)
    heads = attend(place, jnp.stack(queries), own, sib)

    out = lax.all_to_all(heads, ("xl", "yh", "z", "xh"), split_axis=0, concat_axis=0, tiled=True)
    out = out.reshape(2, 2, 4, 2, ROWS, HD).transpose(4, 2, 3, 0, 1, 5)
    return mixed, out.reshape(ROWS, CHANS)


def solution(mesh):
    fine = Mesh(mesh.devices.reshape(SIZES), NAMES)
    rows = P(NAMES, None)
    return jax.shard_map(
        per_device,
        mesh=fine,
        in_specs=(rows, rows, rows, rows, P(), P(None, ("z", "xh", "c"), None)),
        out_specs=(rows, rows),
        check_vma=False,
    )
```

time: 418 us -> 249 us (0.60)
  matrix products: 130 us -> 0 us
  Pallas kernels: 0 us -> 53.7 us
  waiting for transfers between devices: 117 us -> 77.3 us
  other arithmetic: 45.5 us -> 12.8 us
  local copies, waits for them, and re-layouts: 53.8 us -> 33.1 us
  starting transfers between devices: 11.7 us -> 28.6 us
  between operations: 14.4 us -> 0.79 us
    dot_general x21 -> x0, matrix products: 130 us -> none  [the longest x1 52.3 us: per_device(): jnp.einsum('hqk,khd->hqd', weights, piece_values.astype(jnp.float32), pre...]
    all_gather x3 -> x0, waiting for transfers between devices: 94.9 us -> none  [the longest x1 54.4 us: per_device(): lax.all_gather(mixed, 'sb', axis=0, tiled=True)]
    ppermute x0 -> x16, waiting for transfers between devices: none -> 60 us  [shift(): return lax.ppermute(x, NAMES, pairs)]
    pallas_call x0 -> x5, Pallas kernels: none -> 53.7 us  [the longest x1 20.5 us: attend(): pl.pallas_call(attend_kernel, out_shape=jax.ShapeDtypeStruct((32, ROWS, H...]
    reduce_sum x1 -> x0, other arithmetic: 24.6 us -> none  [per_device(): total = jnp.sum(weights, axis=2)]
    ppermute x0 -> x16, starting transfers between devices: none -> 17.4 us  [shift(): return lax.ppermute(x, NAMES, pairs)]
    another operation x0 -> x2, local copies, waits for them, and re-layouts: none -> 15.4 us  [the longest x1 14.7 us: per_device(): weights = jnp.stack([own_weight, flip(own_weight, c=1)])]
    another operation x2 -> x4, other arithmetic: 1.33 us -> 12.8 us  [the longest x1 10.7 us: per_device(): weights = jnp.stack([own_weight, flip(own_weight, c=1)])]
  transfers between devices with their start and end apart: 4 -> 17, of which waited for: 3 -> 10; matrix products, arithmetic and copies ran while one was open for 20% -> 13% of each run, Pallas kernels for 0% -> 7%
where the time goes in v1:
time: 249 us; the launch traced here: 244 us
  waiting for transfers between devices  77.3 us (31%)
  Pallas kernels  53.7 us (22%)
  blocking collectives  38 us (15%)
  local copies, waits for them, and re-layouts  33.1 us (13%)
  starting transfers between devices  28.6 us (11%)
  other arithmetic  12.8 us (5%)
    ppermute x16, waiting for transfers between devices, shift(): return lax.ppermute(x, NAMES, pairs)  60 us
    pallas_call x1, Pallas kernels, attend(): pl.pallas_call(attend_kernel, out_shape=jax.ShapeDtypeStruct((32, ROWS, H...  20.5 us
    all_to_all x1, blocking collectives, per_device(): lax.all_to_all(heads, ('xl', 'yh', 'z', 'xh'), split_axis=0, concat_axis=...  19.2 us
    all_to_all x1, blocking collectives, per_device(): lax.all_to_all(filtered, NAMES, split_axis=0, concat_axis=0, tiled=True)  18.8 us
    ppermute x16, starting transfers between devices, shift(): return lax.ppermute(x, NAMES, pairs)  17.4 us
    all_to_all x1, waiting for transfers between devices, per_device(): lax.all_to_all(packed, NAMES, split_axis=0, concat_axis=0, tiled=True)  17.3 us
    pallas_call x1, Pallas kernels, project(): pl.pallas_call(project_kernel, out_shape=jax.ShapeDtypeStruct((4, 3, rows...  15.2 us
    another operation x1, local copies, waits for them, and re-layouts, per_device(): weights = jnp.stack([own_weight, flip(own_weight, c=1)])  14.7 us
  transfers between devices with their start and end apart: 17, of which 10 were waited for; matrix products, arithmetic and copies ran while one was open for 13% of the time, Pallas kernels for 7%

profile of v1, /device:TPU:0, one launch (start us, length us, event | category | flops | bytes accessed | tf_op | source)
XLA Modules:
  0.0 244.4 jit_solution(9654742002639746177)
XLA Ops:
  0.6 6.5 %copy.21 = bf16[512,8,2,384]{3,1,2,0:T(8,128)(2,1)} copy(bf16[512,8,2,384]{3,2,1,0:T(2,128)(2,1)} %bitcast.52) | data formatting | bytes 12582912
  7.1 2.7 %pack.1 = bf16[128,2,16,128]{3,2,1,0:T(8,128)(2,1)} custom-call(bf16[64,4096]{1,0:T(8,128)(2,1)} %key_ref.1, bf16[64,4096]{1,0:T(8,128)(2,1)} %value_ref.1, bf16[64,4096]{1,0:T(8,128)(2,1)} %taps_ref.1), custom_call_target="tpu_custom_call" | custom-call | tf_op jit(solution)/shard_map/pack/pallas_call | solution.py:73
  9.8 11.2 %all-to-all-start = ((bf16[128,2,16,128]{3,2,1,0:T(8,128)(2,1)}), bf16[128,2,16,128]{3,2,1,0:T(8,128)(2,1)S(1)}, u32[]{:S(2)}, u32[]{:S(2)}) async-start(bf16[128,2,16,128]{3,2,1,0:T(8,128)(2,1)} %pack.1), calls=%async_computation | async-start | bytes 2097152 | tf_op jit(solution)/shard_map/all_to_all | solution.py:321
  21.4 0.7 reshape.26.gain_ref
  22.0 17.3 %all-to-all-done.recv_ref = bf16[128,2,16,128]{3,2,1,0:T(8,128)(2,1)S(1)} async-done(((bf16[128,2,16,128]{3,2,1,0:T(8,128)(2,1)}), bf16[128,2,16,128]{3,2,1,0:T(8,128)(2,1)S(1)}, u32[]{:S(2)}, u32[]{:S(2)}) %all-to-all-start) | async-done | bytes 1048608 | tf_op jit(solution)/shard_map/all_to_all | solution.py:321
  39.3 1.0 copy-done.1
  40.3 13.1 %convolve.1 = bf16[128,16,128]{2,1,0:T(8,128)(2,1)} custom-call(bf16[128,2,16,128]{3,2,1,0:T(8,128)(2,1)} %copy-done.1, f32[16,128]{1,0:T(8,128)} %reshape.26.gain_ref, bf16[256,128]{1,0:T(8,128)(2,1)} %constant.59.clone.w1h, bf16[256,128]{1,0:T(8,128)(2,1)} %constant.60.clone.w1l, f32[128,128]{1,0:T(8,128)} %constant.61.clone.tc_ref, ...), custom_call_target="tpu_custom_call" | custom-call | tf_op jit(solution)/shard_map/convolve/pallas_call | solution.py:142
  53.4 18.8 %all_to_all.15.recv_ref = bf16[128,16,128]{2,1,0:T(8,128)(2,1)} all-to-all(bf16[128,16,128]{2,1,0:T(8,128)(2,1)} %convolve.1), channel_id=1, replica_groups=mesh['xl'=2,'yh'=2,'yl'=2,'z'=4,'xh'=2,'c'=2] {'xl','yh','yl','z','xh','c'}, dimensions={0} | all-to-all | bytes 1048576 | tf_op jit(solution)/shard_map/all_to_all | solution.py:329
  72.2 2.2 apply_gate.1.refs_0_
  74.4 1.8 collective-permute-start.3
  76.2 2.0 collective-permute-start.1
  78.3 14.7 %stack_reshape.3 = bf16[1,4096,768]{2,1,0:T(8,128)(2,1)} reshape(bf16[4096,2,384]{2,1,0:T(2,128)(2,1)} %param.21) | data formatting | bytes 12582912 | tf_op jit(solution)/shard_map/stack;reshape | solution.py:324
  93.0 0.6 pad_add_fusion.1.place_ref
  93.6 1.8 collective-permute-start
  95.4 5.6 %collective-permute-done.5.refs_6_ = bf16[64,4096]{1,0:T(8,128)(2,1)S(1)} collective-permute-done((bf16[64,4096]{1,0:T(8,128)(2,1)}, bf16[64,4096]{1,0:T(8,128)(2,1)S(1)}, u32[]{:S(2)}, u32[]{:S(2)}) %collective-permute-start.5) | collective-permute-done | bytes 524320 | tf_op jit(solution)/shard_map/ppermute | solution.py:298
  101.0 0.8 collective-permute-start.6
  101.8 2.8 %collective-permute-start.4 = (bf16[64,4096]{1,0:T(8,128)(2,1)S(1)}, bf16[64,4096]{1,0:T(8,128)(2,1)S(1)}, u32[]{:S(2)}, u32[]{:S(2)}) collective-permute-start(bf16[64,4096]{1,0:T(8,128)(2,1)S(1)} %collective-permute-done.3.refs_4_), channel_id=1, source_target_pairs={{0,2},{1,3},{2,0},{3,1},{4,6},{5,7},{6,4},{7,5},{8,10},{9,11},{10,... | collective-permute-start | bytes 1572872 | tf_op jit(solution)/shard_map/ppermute | solution.py:298
  104.6 0.8 collective-permute-start.2
  105.3 10.7 %pad_maximum_fusion.refs_8_ = bf16[2,4096,768]{2,1,0:T(8,128)(2,1)} fusion(bf16[1,4096,768]{2,1,0:T(8,128)(2,1)} %bitcast.9, bf16[1,4096,768]{2,1,0:T(8,128)(2,1)} %stack_reshape.3), kind=kLoop, calls=%fused_computation | loop fusion | flops 6291456 | bytes 25165824 | tf_op jit(solution)/shard_map/stack | solution.py:324
  116.1 5.1 %collective-permute-done.6.refs_7_ = bf16[64,4096]{1,0:T(8,128)(2,1)S(1)} collective-permute-done((bf16[64,4096]{1,0:T(8,128)(2,1)S(1)}, bf16[64,4096]{1,0:T(8,128)(2,1)S(1)}, u32[]{:S(2)}, u32[]{:S(2)}) %collective-permute-start.6) | collective-permute-done | bytes 524320 | tf_op jit(solution)/shard_map/ppermute | solution.py:298
  121.2 11.2 %collective-permute-done.4.refs_5_ = bf16[64,4096]{1,0:T(8,128)(2,1)S(1)} collective-permute-done((bf16[64,4096]{1,0:T(8,128)(2,1)S(1)}, bf16[64,4096]{1,0:T(8,128)(2,1)S(1)}, u32[]{:S(2)}, u32[]{:S(2)}) %collective-permute-start.4) | collective-permute-done | bytes 524320 | tf_op jit(solution)/shard_map/ppermute | solution.py:298
  132.4 9.7 %collective-permute-done.2.refs_3_ = bf16[64,4096]{1,0:T(8,128)(2,1)S(1)} collective-permute-done((bf16[64,4096]{1,0:T(8,128)(2,1)S(1)}, bf16[64,4096]{1,0:T(8,128)(2,1)S(1)}, u32[]{:S(2)}, u32[]{:S(2)}) %collective-permute-start.2) | collective-permute-done | bytes 524320 | tf_op jit(solution)/shard_map/ppermute | solution.py:298
  142.1 0.8 copy-done.9
  143.0 15.2 %project.1 = bf16[4,3,512,128]{3,2,1,0:T(8,128)(2,1)} custom-call(s32[4]{0:T(128)} %pad_add_fusion.1.place_ref, bf16[64,4096]{1,0:T(8,128)(2,1)} %apply_gate.1.refs_0_, bf16[64,4096]{1,0:T(8,128)(2,1)} %copy-done.6, bf16[64,4096]{1,0:T(8,128)(2,1)} %copy-done.5, bf16[64,4096]{1,0:T(8,128)(2,1)} %copy-done.9, bf16[64,4096]{1,0:T(8,128)(2,1)} %copy-done.4, ...), custom_call_target="tpu_custom_call" | custom-call | tf_op jit(solution)/shard_map/project/pallas_call | solution.py:195
  158.2 2.2 slice_bitcast_fusion.3
  160.9 2.1 collective-permute-start.8
  163.0 1.6 collective-permute-start.10
  164.6 1.4 collective-permute-start.9
  166.0 0.8 collective-permute-start.14
  166.8 11.2 %collective-permute-done.11 = bf16[2,512,128]{2,1,0:T(8,128)(2,1)S(1)} collective-permute-done((bf16[2,512,128]{2,1,0:T(8,128)(2,1)S(1)}, bf16[2,512,128]{2,1,0:T(8,128)(2,1)S(1)}, u32[]{:S(2)}, u32[]{:S(2)}) %collective-permute-start.11) | collective-permute-done | bytes 262176 | tf_op jit(solution)/shard_map/ppermute | solution.py:298
  178.1 1.0 collective-permute-start.12
  179.1 0.7 bitcast_dynamic-update-slice_fusion.3
  179.8 9.1 %collective-permute-done.8 = bf16[3,512,128]{2,1,0:T(8,128)(2,1)S(1)} collective-permute-done((bf16[3,512,128]{2,1,0:T(8,128)(2,1)S(1)}, bf16[3,512,128]{2,1,0:T(8,128)(2,1)S(1)}, u32[]{:S(2)}, u32[]{:S(2)}) %collective-permute-start.8) | collective-permute-done | bytes 393248 | tf_op jit(solution)/shard_map/ppermute | solution.py:298
  188.9 0.7 fusion.2
  189.7 4.2 %collective-permute-done.12 = bf16[2,512,128]{2,1,0:T(8,128)(2,1)S(1)} collective-permute-done((bf16[2,512,128]{2,1,0:T(8,128)(2,1)S(1)}, bf16[2,512,128]{2,1,0:T(8,128)(2,1)S(1)}, u32[]{:S(2)}, u32[]{:S(2)}) %collective-permute-start.12) | collective-permute-done | bytes 262176 | tf_op jit(solution)/shard_map/ppermute | solution.py:298
  193.8 0.7 bitcast_dynamic-update-slice_fusion.2
  194.5 0.7 fusion.1
  195.3 0.9 collective-permute-done.13
  196.2 0.8 bitcast_dynamic-update-slice_fusion.1
  196.9 0.7 fusion
  197.7 0.7 bitcast_dynamic-update-slice_fusion.own_ref
  198.4 0.6 pad_add_fusion.me_ref
  199.1 0.9 pad_maximum_fusion.1.q_ref
  199.9 3.0 %collective-permute-done.15.sib_ref = bf16[8,2,512,128]{3,2,1,0:T(8,128)(2,1)} collective-permute-done((bf16[8,2,512,128]{3,2,1,0:T(8,128)(2,1)}, bf16[8,2,512,128]{3,2,1,0:T(8,128)(2,1)}, u32[]{:S(2)}, u32[]{:S(2)}) %collective-permute-start.15) | collective-permute-done | bytes 2097184 | tf_op jit(solution)/shard_map/ppermute | solution.py:298
  202.9 20.5 %attend.1 = bf16[32,64,128]{2,1,0:T(8,128)(2,1)} custom-call(s32[4]{0:T(128)} %pad_add_fusion.me_ref, bf16[4,512,128]{2,1,0:T(8,128)(2,1)} %pad_maximum_fusion.1.q_ref, bf16[8,2,512,128]{3,2,1,0:T(8,128)(2,1)} %bitcast_dynamic-update-slice_fusion.own_ref, bf16[8,2,512,128]{3,2,1,0:T(8,128)(2,1)} %collective-permute-done.15.sib_ref), custom_call_target="tpu_custom_call" | custom-call | tf_op jit(solution)/shard_map/attend/pallas_call | solution.py:279
  223.4 19.2 %all_to_all.16 = bf16[32,64,128]{2,1,0:T(8,128)(2,1)S(1)} all-to-all(bf16[32,64,128]{2,1,0:T(8,128)(2,1)} %attend.1), channel_id=1, replica_groups=mesh['xl'=2,'yh'=2,'yl'=2,'z'=4,'xh'=2,'c'=2] {'xl','yh','z','xh'}, dimensions={0} | all-to-all | bytes 1048576 | tf_op jit(solution)/shard_map/all_to_all | solution.py:358
  242.6 0.5 copy.20
  243.2 1.2 reshape.29
  (41 shorter events, 1.0 us)
Async XLA Ops:
  7.1 14.0 %copy-start.10 = (f32[4096]{0:T(1024)S(1)}, f32[4096]{0:T(1024)}, u32[]{:S(2)}) copy-start(f32[4096]{0:T(1024)} %param.20) | copy-start | bytes 49156
  7.1 98.2 %collective-permute-start.7 = (bf16[4096,768]{1,0:T(8,128)(2,1)}, bf16[4096,768]{1,0:T(8,128)(2,1)}, u32[]{:S(2)}, u32[]{:S(2)}) collective-permute-start(bf16[4096,768]{1,0:T(8,128)(2,1)} %bitcast.29), channel_id=1, source_target_pairs={{0,1},{1,0},{2,3},{3,2},{4,5},{5,4},{6,7},{7,6},{8,9},{9,8},{10,11... | collective-permute-start | bytes 18874376 | tf_op jit(solution)/shard_map/ppermute | solution.py:298
  9.8 29.5 %all-to-all-start = ((bf16[128,2,16,128]{3,2,1,0:T(8,128)(2,1)}), bf16[128,2,16,128]{3,2,1,0:T(8,128)(2,1)S(1)}, u32[]{:S(2)}, u32[]{:S(2)}) async-start(bf16[128,2,16,128]{3,2,1,0:T(8,128)(2,1)} %pack.1), calls=%async_computation | async-start | bytes 2097152 | tf_op jit(solution)/shard_map/all_to_all | solution.py:321
  39.3 1.0 copy-start.1
  74.4 26.6 %collective-permute-start.5 = (bf16[64,4096]{1,0:T(8,128)(2,1)}, bf16[64,4096]{1,0:T(8,128)(2,1)S(1)}, u32[]{:S(2)}, u32[]{:S(2)}) collective-permute-start(bf16[64,4096]{1,0:T(8,128)(2,1)} %apply_gate.1.refs_0_), channel_id=1, source_target_pairs={{0,4},{1,5},{2,6},{3,7},{4,8},{5,9},{6,10},{7,11},{8,12},{9,13},{1... | collective-permute-start | bytes 1572872 | tf_op jit(solution)/shard_map/ppermute | solution.py:298
  74.4 27.4 %collective-permute-start.3 = (bf16[64,4096]{1,0:T(8,128)(2,1)}, bf16[64,4096]{1,0:T(8,128)(2,1)S(1)}, u32[]{:S(2)}, u32[]{:S(2)}) collective-permute-start(bf16[64,4096]{1,0:T(8,128)(2,1)} %apply_gate.1.refs_0_), channel_id=1, source_target_pairs={{0,8},{1,9},{2,10},{3,11},{4,12},{5,13},{6,14},{7,15},{8,0},{9,1},... | collective-permute-start | bytes 1572872 | tf_op jit(solution)/shard_map/ppermute | solution.py:298
  76.2 28.3 %collective-permute-start.1 = (bf16[64,4096]{1,0:T(8,128)(2,1)}, bf16[64,4096]{1,0:T(8,128)(2,1)S(1)}, u32[]{:S(2)}, u32[]{:S(2)}) collective-permute-start(bf16[64,4096]{1,0:T(8,128)(2,1)} %apply_gate.1.refs_0_), channel_id=1, source_target_pairs={{0,12},{1,13},{2,14},{3,15},{4,0},{5,1},{6,2},{7,3},{8,4},{9,5},{1... | collective-permute-start | bytes 1572872 | tf_op jit(solution)/shard_map/ppermute | solution.py:298
  78.3 15.3 %copy-start.2 = (bf16[64,4096]{1,0:T(8,128)(2,1)S(1)}, bf16[64,4096]{1,0:T(8,128)(2,1)}, u32[]{:S(2)}) copy-start(bf16[64,4096]{1,0:T(8,128)(2,1)} %apply_gate.1.refs_0_) | copy-start | bytes 1572868
  93.6 22.5 %collective-permute-start = (bf16[64,4096]{1,0:T(8,128)(2,1)S(1)}, bf16[64,4096]{1,0:T(8,128)(2,1)S(1)}, u32[]{:S(2)}, u32[]{:S(2)}) collective-permute-start(bf16[64,4096]{1,0:T(8,128)(2,1)S(1)} %copy-done.2), channel_id=1, source_target_pairs={{0,2},{1,3},{2,0},{3,1},{4,6},{5,7},{6,4},{7,5},{8,10},{9,11},{10,... | collective-permute-start | bytes 1572872 | tf_op jit(solution)/shard_map/ppermute | solution.py:298
  101.0 15.1 %copy-start.3 = (bf16[64,4096]{1,0:T(8,128)(2,1)}, bf16[64,4096]{1,0:T(8,128)(2,1)S(1)}, u32[]{:S(2)}) copy-start(bf16[64,4096]{1,0:T(8,128)(2,1)S(1)} %collective-permute-done.5.refs_6_) | copy-start | bytes 1572868
  101.0 20.1 %collective-permute-start.6 = (bf16[64,4096]{1,0:T(8,128)(2,1)S(1)}, bf16[64,4096]{1,0:T(8,128)(2,1)S(1)}, u32[]{:S(2)}, u32[]{:S(2)}) collective-permute-start(bf16[64,4096]{1,0:T(8,128)(2,1)S(1)} %collective-permute-done.5.refs_6_), channel_id=1, source_target_pairs={{0,2},{1,3},{2,0},{3,1},{4,6},{5,7},{6,4},{7,5},{8,10},{9,11},{10,... | collective-permute-start | bytes 1572872 | tf_op jit(solution)/shard_map/ppermute | solution.py:298
  101.8 14.3 %copy-start.4 = (bf16[64,4096]{1,0:T(8,128)(2,1)}, bf16[64,4096]{1,0:T(8,128)(2,1)S(1)}, u32[]{:S(2)}) copy-start(bf16[64,4096]{1,0:T(8,128)(2,1)S(1)} %collective-permute-done.3.refs_4_) | copy-start | bytes 1572868
  101.8 30.6 %collective-permute-start.4 = (bf16[64,4096]{1,0:T(8,128)(2,1)S(1)}, bf16[64,4096]{1,0:T(8,128)(2,1)S(1)}, u32[]{:S(2)}, u32[]{:S(2)}) collective-permute-start(bf16[64,4096]{1,0:T(8,128)(2,1)S(1)} %collective-permute-done.3.refs_4_), channel_id=1, source_target_pairs={{0,2},{1,3},{2,0},{3,1},{4,6},{5,7},{6,4},{7,5},{8,10},{9,11},{10,... | collective-permute-start | bytes 1572872 | tf_op jit(solution)/shard_map/ppermute | solution.py:298
  104.6 11.5 %copy-start.5 = (bf16[64,4096]{1,0:T(8,128)(2,1)}, bf16[64,4096]{1,0:T(8,128)(2,1)S(1)}, u32[]{:S(2)}) copy-start(bf16[64,4096]{1,0:T(8,128)(2,1)S(1)} %collective-permute-done.1.refs_2_) | copy-start | bytes 1572868
  104.6 37.6 %collective-permute-start.2 = (bf16[64,4096]{1,0:T(8,128)(2,1)S(1)}, bf16[64,4096]{1,0:T(8,128)(2,1)S(1)}, u32[]{:S(2)}, u32[]{:S(2)}) collective-permute-start(bf16[64,4096]{1,0:T(8,128)(2,1)S(1)} %collective-permute-done.1.refs_2_), channel_id=1, source_target_pairs={{0,2},{1,3},{2,0},{3,1},{4,6},{5,7},{6,4},{7,5},{8,10},{9,11},{10,... | collective-permute-start | bytes 1572872 | tf_op jit(solution)/shard_map/ppermute | solution.py:298
  116.1 26.0 %copy-start.6 = (bf16[64,4096]{1,0:T(8,128)(2,1)}, bf16[64,4096]{1,0:T(8,128)(2,1)S(1)}, u32[]{:S(2)}) copy-start(bf16[64,4096]{1,0:T(8,128)(2,1)S(1)} %collective-permute-done.refs_1_) | copy-start | bytes 1572868
  121.2 21.0 %copy-start.7 = (bf16[64,4096]{1,0:T(8,128)(2,1)}, bf16[64,4096]{1,0:T(8,128)(2,1)S(1)}, u32[]{:S(2)}) copy-start(bf16[64,4096]{1,0:T(8,128)(2,1)S(1)} %collective-permute-done.6.refs_7_) | copy-start | bytes 1572868
  132.4 9.7 %copy-start.8 = (bf16[64,4096]{1,0:T(8,128)(2,1)}, bf16[64,4096]{1,0:T(8,128)(2,1)S(1)}, u32[]{:S(2)}) copy-start(bf16[64,4096]{1,0:T(8,128)(2,1)S(1)} %collective-permute-done.4.refs_5_) | copy-start | bytes 1572868
  142.1 0.8 copy-start.9
  158.1 2.7 %copy-start = (bf16[4,3,512,128]{3,2,1,0:T(8,128)(2,1)S(1)}, bf16[4,3,512,128]{3,2,1,0:T(8,128)(2,1)}, u32[]{:S(2)}) copy-start(bf16[4,3,512,128]{3,2,1,0:T(8,128)(2,1)} %project.1) | copy-start | bytes 4718596
  160.3 17.7 %collective-permute-start.11 = (bf16[2,512,128]{2,1,0:T(8,128)(2,1)S(1)}, bf16[2,512,128]{2,1,0:T(8,128)(2,1)S(1)}, u32[]{:S(2)}, u32[]{:S(2)}) collective-permute-start(bf16[2,512,128]{2,1,0:T(8,128)(2,1)S(1)} %get-tuple-element.6), channel_id=1, source_target_pairs={{0,16},{1,17},{2,18},{3,19},{4,20},{5,21},{6,22},{7,23},{8,24},{9,... | collective-permute-start | bytes 786440 | tf_op jit(solution)/shard_map/ppermute | solution.py:298
  160.9 28.0 %collective-permute-start.8 = (bf16[3,512,128]{2,1,0:T(8,128)(2,1)S(1)}, bf16[3,512,128]{2,1,0:T(8,128)(2,1)S(1)}, u32[]{:S(2)}, u32[]{:S(2)}) collective-permute-start(bf16[3,512,128]{2,1,0:T(8,128)(2,1)S(1)} %get-tuple-element.7), channel_id=1, source_target_pairs={{0,32},{1,33},{2,34},{3,35},{4,36},{5,37},{6,38},{7,39},{8,40},{9,... | collective-permute-start | bytes 1179656 | tf_op jit(solution)/shard_map/ppermute | solution.py:298
  163.0 33.9 %collective-permute-start.10 = (bf16[3,512,128]{2,1,0:T(8,128)(2,1)S(1)}, bf16[3,512,128]{2,1,0:T(8,128)(2,1)S(1)}, u32[]{:S(2)}, u32[]{:S(2)}) collective-permute-start(bf16[3,512,128]{2,1,0:T(8,128)(2,1)S(1)} %get-tuple-element.8), channel_id=1, source_target_pairs={{0,96},{1,97},{2,98},{3,99},{4,100},{5,101},{6,102},{7,103},{8,104... | collective-permute-start | bytes 1179656 | tf_op jit(solution)/shard_map/ppermute | solution.py:298
  164.6 30.0 %collective-permute-start.9 = (bf16[3,512,128]{2,1,0:T(8,128)(2,1)S(1)}, bf16[3,512,128]{2,1,0:T(8,128)(2,1)S(1)}, u32[]{:S(2)}, u32[]{:S(2)}) collective-permute-start(bf16[3,512,128]{2,1,0:T(8,128)(2,1)S(1)} %get-tuple-element.9), channel_id=1, source_target_pairs={{0,64},{1,65},{2,66},{3,67},{4,68},{5,69},{6,70},{7,71},{8,72},{9,... | collective-permute-start | bytes 1179656 | tf_op jit(solution)/shard_map/ppermute | solution.py:298
  166.0 31.7 %collective-permute-start.14 = (bf16[2,512,128]{2,1,0:T(8,128)(2,1)S(1)}, bf16[2,512,128]{2,1,0:T(8,128)(2,1)S(1)}, u32[]{:S(2)}, u32[]{:S(2)}) collective-permute-start(bf16[2,512,128]{2,1,0:T(8,128)(2,1)S(1)} %get-tuple-element.2), channel_id=1, source_target_pairs={{0,112},{1,113},{2,114},{3,115},{4,116},{5,117},{6,118},{7,119},{8... | collective-permute-start | bytes 786440 | tf_op jit(solution)/shard_map/ppermute | solution.py:298
  178.1 15.8 %collective-permute-start.12 = (bf16[2,512,128]{2,1,0:T(8,128)(2,1)S(1)}, bf16[2,512,128]{2,1,0:T(8,128)(2,1)S(1)}, u32[]{:S(2)}, u32[]{:S(2)}) collective-permute-start(bf16[2,512,128]{2,1,0:T(8,128)(2,1)S(1)} %get-tuple-element.5), channel_id=1, source_target_pairs={{0,48},{1,49},{2,50},{3,51},{4,52},{5,53},{6,54},{7,55},{8,56},{9,... | collective-permute-start | bytes 786440 | tf_op jit(solution)/shard_map/ppermute | solution.py:298
  188.9 7.3 %collective-permute-start.13 = (bf16[2,512,128]{2,1,0:T(8,128)(2,1)S(1)}, bf16[2,512,128]{2,1,0:T(8,128)(2,1)S(1)}, u32[]{:S(2)}, u32[]{:S(2)}) collective-permute-start(bf16[2,512,128]{2,1,0:T(8,128)(2,1)S(1)} %get-tuple-element.4), channel_id=1, source_target_pairs={{0,80},{1,81},{2,82},{3,83},{4,84},{5,85},{6,86},{7,87},{8,88},{9,... | collective-permute-start | bytes 786440 | tf_op jit(solution)/shard_map/ppermute | solution.py:298
  198.4 4.5 %collective-permute-start.15 = (bf16[8,2,512,128]{3,2,1,0:T(8,128)(2,1)}, bf16[8,2,512,128]{3,2,1,0:T(8,128)(2,1)}, u32[]{:S(2)}, u32[]{:S(2)}) collective-permute-start(bf16[8,2,512,128]{3,2,1,0:T(8,128)(2,1)} %bitcast_dynamic-update-slice_fusion.own_ref), channel_id=1, source_target_pairs={{0,1},{1,0},{2,3},{3,2},{4,5},{5,4},{6,7},{7,6},{8,9},{9,8},{10,11... | collective-permute-start | bytes 6291464 | tf_op jit(solution)/shard_map/ppermute | solution.py:298

commit v2 on v1

--- a/solution.py
+++ b/solution.py
@@ -1,3 +1,4 @@
+import functools
 import itertools
 import math
 
@@ -150,142 +151,238 @@
     )(*args)
 
 
-def gate_kernel(recv_ref, gate_ref, out_ref):
+PART = ROWS // 2
+
+
+def gate_kernel(recv_ref, gate_ref, out_ref, upper_ref, lower_ref):
     for block in range(HALF // 128):
         tile = recv_ref[block * 8 : block * 8 + 8].astype(F32).reshape(128, 128).T
         for half in range(2):
             cols = pl.ds(half * HALF + block * 128, 128)
             part = tile[half * ROWS : half * ROWS + ROWS]
-            out_ref[:, cols] = (gate_ref[:, cols].astype(F32) * part).astype(BF)
+            mixed = (gate_ref[:, cols].astype(F32) * part).astype(BF)
+            out_ref[:, cols] = mixed
+            upper_ref[:, cols] = mixed[:PART]
+            lower_ref[:, cols] = mixed[PART:]
 
 
 def apply_gate(recv, gate_signal):
+    shapes = [(ROWS, CHANS), (PART, CHANS), (PART, CHANS)]
     return pl.pallas_call(
         gate_kernel,
-        out_shape=jax.ShapeDtypeStruct((ROWS, CHANS), BF),
+        out_shape=[jax.ShapeDtypeStruct(shape, BF) for shape in shapes],
         in_specs=[whole((DEVS, 16, 128)), whole((ROWS, CHANS))],
-        out_specs=whole((ROWS, CHANS)),
+        out_specs=[whole(shape) for shape in shapes],
         compiler_params=params(),
         name="apply_gate",
     )(recv, gate_signal)
 
 
-def project_kernel(place_ref, *refs):
-    shards = refs[:8]
-    w_ref, out_ref, x_s, sems = refs[8:]
-
-    @pl.when(pl.program_id(0) == 0)
+BLOCK = 8 * PART
+ASKED = BLOCK // 2
+MESSAGE = 2 * BLOCK + ASKED
+DEPTH = 1024
+
+
+def project_kernel(core_ref, *refs):
+    shards = refs[:16]
+    weights = refs[16:18]
+    out_ref, acc = refs[18:]
+    step = pl.program_id(0)
+    x = jnp.concatenate([shard[...] for shard in shards], axis=0)
+
+    for side in range(2):
+        part = dot(x, weights[side][...])
+
+        @pl.when(step == 0)
+        def _():
+            acc[side] = part
+
+        @pl.when(step > 0)
+        def _():
+            acc[side] += part
+
+    @pl.when(step == pl.num_programs(0) - 1)
     def _():
-        copies = [
-            pltpu.make_async_copy(shard, x_s.at[pl.ds(i * ROWS, ROWS), :], sems.at[i])
-            for i, shard in enumerate(shards)
-        ]
-        for copy in copies:
-            copy.start()
-        for copy in copies:
-            copy.wait()
-
-    result = dot(x_s[...], w_ref[0])
-    for slot, part in enumerate((1, 2, 0)):
-        out_ref[0, slot] = result[:, part * HD : part * HD + HD].astype(BF)
-
-
-def project(place, shards, weights):
-    rows = 8 * ROWS
+        for xl in range(2):
+            for yh in range(2):
+                start = yh * 3 * HD
+                side = core_ref[0] ^ xl
+                queries = acc[side, :, start : start + HD].astype(BF).reshape(2, 8, 2, PART // 2, HD)
+                keys = acc[side, :, start + HD : start + 2 * HD].astype(BF)
+                values = acc[side, :, start + 2 * HD : start + 3 * HD]
+                flipped = [values[n * HD : n * HD + HD].T.astype(BF) for n in range(2 * BLOCK // HD)]
+                for yl in range(2):
+                    goal = xl * 4 + yh * 2 + yl
+                    for part in range(2):
+                        out_ref[goal, part, :BLOCK] = keys[part * BLOCK : part * BLOCK + BLOCK]
+                        for n in range(BLOCK // HD):
+                            first = BLOCK + n * HD
+                            out_ref[goal, part, first : first + HD] = flipped[part * (BLOCK // HD) + n]
+                        out_ref[goal, part, 2 * BLOCK :] = queries[part, :, yl].reshape(ASKED, HD)
+
+
+def project(core, shards, own, sib, depth=DEPTH):
     return pl.pallas_call(
         project_kernel,
-        out_shape=jax.ShapeDtypeStruct((4, 3, rows, HD), BF),
+        out_shape=jax.ShapeDtypeStruct((8, 2, MESSAGE, HD), BF),
         grid_spec=pltpu.PrefetchScalarGridSpec(
             num_scalar_prefetch=1,
-            grid=(4,),
-            in_specs=[pl.BlockSpec(memory_space=pl.ANY)] * 8
-            + [pl.BlockSpec((1, CHANS, 3 * HD), lambda i, place: (i // 2, 0, i % 2))],
-            out_specs=pl.BlockSpec((1, 3, rows, HD), lambda i, place: (place[i], 0, 0, 0)),
-            scratch_shapes=[pltpu.VMEM((rows, CHANS), BF), pltpu.SemaphoreType.DMA((8,))],
+            grid=(CHANS // depth,),
+            in_specs=[pl.BlockSpec((PART, depth), lambda i, core: (0, i))] * 16
+            + [pl.BlockSpec((depth, 6 * HD), lambda i, core: (i, 0))] * 2,
+            out_specs=whole((8, 2, MESSAGE, HD)),
+            scratch_shapes=[pltpu.VMEM((2, 2 * BLOCK, 6 * HD), F32)],
+        ),
+        cost_estimate=pl.CostEstimate(
+            flops=4 * BLOCK * CHANS * 12 * HD, bytes_accessed=CHANS * 12 * HD * 2, transcendentals=0
         ),
         compiler_params=params(),
         name="project",
-    )(place, *shards, weights)
-
-
-GROUP = 8 * ROWS
-TILE = 256
+    )(core, *shards, own, sib)
+
+
 SCALE = math.log2(math.e) / math.sqrt(HD)
 EXTRA = 16
-
-
-def attend_kernel(me_ref, q_ref, own_ref, sib_ref, out_ref, vt_s):
-    me, my_z, my_xh, my_c = me_ref[0], me_ref[1], me_ref[2], me_ref[3]
-    ones = jnp.ones((EXTRA, GROUP), BF)
-    for side, ref in enumerate((own_ref, sib_ref)):
-        for rel in range(8):
-            vt_s[side, rel, :HD] = ref[rel, 1].astype(F32).T.astype(BF)
-            vt_s[side, rel, HD:] = ones
-
-    def inner_pos(index, core):
-        z = (my_z + (index >> 7)) & 3
-        xh = my_xh ^ ((index >> 6) & 1)
-        return z * 256 + xh * 128 + core * 64 + (index & 63)
-
-    row = lax.broadcasted_iota(jnp.int32, (GROUP, TILE), 0)
-    col = lax.broadcasted_iota(jnp.int32, (GROUP, TILE), 1)
-
-    for qrel in range(4):
-        group = me ^ (qrel * 2)
-        queries = [q_ref[qrel, t * TILE : t * TILE + TILE] for t in range(2)]
-
-        def visit(rel, carry, masked):
-            done = []
-            for t in range(2):
-                best, acc = carry[t]
-                scores = []
-                for side, ref in enumerate((own_ref, sib_ref)):
-                    s = lax.dot_general(
-                        ref[rel, 0], queries[t], (((1,), (1,)), ((), ())), preferred_element_type=F32
-                    )
-                    if masked:
-                        key_pos = inner_pos(row, my_c ^ side)
-                        query_pos = inner_pos(col + t * TILE, my_c)
-                        s = jnp.where(key_pos <= query_pos, s, -1e30)
-                    scores.append(s)
-                top = jnp.maximum(
-                    jnp.max(scores[0], axis=0, keepdims=True), jnp.max(scores[1], axis=0, keepdims=True)
+KEYS = 4 * BLOCK
+QUERIES = 2 * ASKED
+
+
+PAIR = 2 * QUERIES
+ROOM = 80.0
+REACH = 170.0
+
+
+def attend_kernel(me_ref, *refs):
+    own_hbm, sib_hbm, out_ref, k_s, v_s, q_s, acc_s, sems = refs
+    my_yl, my_z, my_xh, my_c = me_ref[0], me_ref[1], me_ref[2], me_ref[3]
+
+    def fetch(group):
+        copies = []
+
+        def add(source, target):
+            copies.append(pltpu.make_async_copy(source, target, sems.at[group, len(copies)]))
+
+        for n in range(4):
+            source = (own_hbm, sib_hbm)[n // 2].at[:, n % 2]
+            add(source.at[group, pl.ds(0, BLOCK)], k_s.at[group, pl.ds(n * BLOCK, BLOCK)])
+            for tile in range(BLOCK // HD):
+                add(
+                    source.at[group, pl.ds(BLOCK + tile * HD, HD)],
+                    v_s.at[group, pl.ds(0, HD), pl.ds(n * BLOCK + tile * HD, HD)],
                 )
-                new = jnp.maximum(best, top)
-                shrink = jnp.exp2((best - new) * SCALE)
-                acc = acc * shrink
-                for side in range(2):
-                    weight = jnp.exp2((scores[side] - new) * SCALE).astype(BF)
-                    acc = acc + dot(vt_s[side, rel], weight)
-                done.append((new, acc))
-            return tuple(done)
-
-        start = tuple(
-            (jnp.full((1, TILE), -1e30, F32), jnp.zeros((HD + EXTRA, TILE), F32)) for _ in range(2)
+            if n < 2:
+                add(source.at[group, pl.ds(2 * BLOCK, ASKED)], q_s.at[group, pl.ds(n * ASKED, ASKED)])
+        return copies
+
+    for group in range(8):
+        for copy in fetch(group):
+            copy.start()
+    for group in range(8):
+        v_s[group, HD:] = jnp.ones((EXTRA, KEYS), BF)
+
+    def inner_pos(shard, core, r):
+        return ((my_z + (shard >> 1)) & 3) * 256 + (my_xh ^ (shard & 1)) * 128 + core * ROWS + r
+
+    row = lax.broadcasted_iota(jnp.int32, (KEYS, 1), 0)
+    col = lax.broadcasted_iota(jnp.int32, (1, PAIR), 1)
+    key_pos = inner_pos((row >> 5) & 7, my_c ^ (row >> 9), ((row >> 8) & 1) * PART + (row & 31))
+    query_pos = inner_pos(
+        (col >> 4) & 7, my_c, ((col >> 7) & 1) * PART + my_yl * (PART // 2) + (col & 15)
+    ) + (col >> 8) * 1024
+
+    def nt(a, b):
+        return lax.dot_general(a, b, (((1,), (1,)), ((), ())), preferred_element_type=F32)
+
+    def score(group, queries, which):
+        s = nt(k_s[group], queries)
+        if which is not None:
+            s = jnp.where(key_pos + which * 1024 <= query_pos, s, -1e30)
+        return s
+
+    def pair(k, tallest):
+        groups = (2 * k, 2 * k + 1)
+        for group in groups:
+            for copy in fetch(group):
+                copy.wait()
+        queries = jnp.concatenate([q_s[group] for group in groups], axis=0)
+        itself = jnp.concatenate(
+            [
+                k_s[group, pl.ds(pl.multiple_of(part * BLOCK + shard * PART + my_yl * 16, 16), 16)]
+                for group in groups
+                for part in range(2)
+                for shard in range(8)
+            ],
+            axis=0,
         )
-        carry = visit(qrel * 2, start, True)
-        carry = lax.fori_loop(0, group, lambda g, cr: visit(g ^ me, cr, False), carry)
-        for t in range(2):
-            acc = carry[t][1]
-            out = (acc[:HD] / acc[HD : HD + 1]).T.astype(BF)
-            for part in range(TILE // ROWS):
-                shard = t * (TILE // ROWS) + part
+        ones = jnp.ones((16, HD), BF)
+        for group in groups:
+            square = nt(ones, jnp.square(k_s[group].astype(F32)).astype(BF))
+            tallest = jnp.maximum(tallest, jnp.max(square[:8], axis=1, keepdims=True))
+        size = nt(ones, jnp.square(queries.astype(F32)).astype(BF))[:1]
+        bound = jnp.sqrt(size * tallest[:1]) * (SCALE * 1.02)
+        product = (queries.astype(F32) * itself.astype(F32)).astype(BF)
+        own = nt(ones, product)[:1] * SCALE
+        safe = jnp.max(bound * 1.01 - own) <= REACH
+        acc_s[...] = jnp.zeros(acc_s.shape, F32)
+
+        @pl.when(safe)
+        def _():
+            offset = bound - ROOM
+
+            def visit(group, which=None):
+                weight = jnp.exp2(score(group, queries, which) * SCALE - offset).astype(BF)
+                acc_s[...] += dot(v_s[group], weight)
+
+            visit(groups[0], 0)
+            visit(groups[1], 1)
+
+            @pl.loop(0, 2 * k)
+            def _(group):
+                visit(group)
+
+        @pl.when(jnp.logical_not(safe))
+        def _():
+            def visit(group, best, which=None):
+                s = score(group, queries, which)
+                new = jnp.maximum(best, jnp.max(s, axis=0, keepdims=True))
+                weight = jnp.exp2((s - new) * SCALE).astype(BF)
+                acc_s[...] = acc_s[...] * jnp.exp2((best - new) * SCALE) + dot(v_s[group], weight)
+                return new
+
+            best = visit(groups[0], jnp.full((1, PAIR), -1e30, F32), 0)
+            best = visit(groups[1], best, 1)
+            lax.fori_loop(0, 2 * k, visit, best)
+
+        out = (acc_s[:HD] / acc_s[HD : HD + 1]).T.astype(BF)
+        for n, group in enumerate(groups):
+            for shard in range(8):
                 z = (my_z + (shard >> 1)) & 3
                 xh = my_xh ^ (shard & 1)
-                out_ref[(group >> 1) * 8 + z * 2 + xh] = out[part * ROWS : part * ROWS + ROWS]
-
-
-def attend(place, queries, own, sib):
+                for part in range(2):
+                    first = n * QUERIES + part * ASKED + shard * 16
+                    out_ref[group * 8 + z * 2 + xh, part * 16 : part * 16 + 16] = out[first : first + 16]
+        return tallest
+
+    lax.fori_loop(0, 4, pair, jnp.zeros((8, 1), F32))
+
+
+def attend(place, own, sib):
     return pl.pallas_call(
         attend_kernel,
-        out_shape=jax.ShapeDtypeStruct((32, ROWS, HD), BF),
-        in_specs=[pl.BlockSpec(memory_space=pltpu.SMEM)]
-        + [whole((4, GROUP, HD)), whole((8, 2, GROUP, HD)), whole((8, 2, GROUP, HD))],
-        out_specs=whole((32, ROWS, HD)),
-        scratch_shapes=[pltpu.VMEM((2, 8, HD + EXTRA, GROUP), BF)],
+        out_shape=jax.ShapeDtypeStruct((64, PART, HD), BF),
+        in_specs=[pl.BlockSpec(memory_space=pltpu.SMEM)] + [pl.BlockSpec(memory_space=pl.ANY)] * 2,
+        out_specs=whole((64, PART, HD)),
+        scratch_shapes=[
+            pltpu.VMEM((8, KEYS, HD), BF),
+            pltpu.VMEM((8, HD + EXTRA, KEYS), BF),
+            pltpu.VMEM((8, QUERIES, HD), BF),
+            pltpu.VMEM((HD + EXTRA, PAIR), F32),
+            pltpu.SemaphoreType.DMA((8, 14)),
+        ],
         compiler_params=params(),
         name="attend",
-    )(place, queries, own, sib)
+    )(place, own, sib)
 
 
 def shift(x, move):
@@ -321,42 +418,30 @@
     recv = lax.all_to_all(packed, NAMES, split_axis=0, concat_axis=0, tiled=True)
 
     own_weight = head_weight.reshape(CHANS, 6 * HD)
-    weights = jnp.stack([own_weight, flip(own_weight, c=1)])
+    sib_weight = flip(head_weight, c=1).reshape(CHANS, 6 * HD)
 
     gain = lax.dynamic_slice_in_dim(skip_gain.reshape(2, HALF), device * 16, 16, 1)
     gain = jnp.repeat(gain.T, ROWS, axis=1)
+    recv, own_weight, sib_weight = lax.optimization_barrier((recv, own_weight, sib_weight))
     filtered = convolve(recv, gain)
     returned = lax.all_to_all(filtered, NAMES, split_axis=0, concat_axis=0, tiled=True)
-    mixed = apply_gate(returned, gate_signal)
-
-    from_z = [mixed, along_z(mixed, -1), along_z(mixed, -2), along_z(mixed, -3)]
-    shards = []
-    for part in from_z:
-        shards += [part, flip(part, xh=1)]
-
-    places = []
-    for side in range(2):
-        for i in range(2):
-            places.append((at["xl"] ^ at["c"] ^ side) * 2 + (at["yh"] ^ i))
-    projected = project(jnp.stack(places).astype(jnp.int32), shards, weights)
-
-    kv, queries = [], []
-    for rel in range(8):
-        xl, yh, yl = rel >> 2, (rel >> 1) & 1, rel & 1
-        part = projected[rel >> 1]
-        part = part if yl == 0 else part[:2]
-        got = part if rel == 0 else flip(part, xl=xl, yh=yh, yl=yl)
-        kv.append(got[:2])
-        if yl == 0:
-            queries.append(got[2])
-    own = jnp.stack(kv)
+    mixed, upper, lower = apply_gate(returned, gate_signal)
+
+    upper_z = [upper] + [along_z(upper, -step) for step in (1, 2, 3)]
+    lower_x = [lower, flip(lower, xh=1)]
+    uppers = [[part, flip(part, xh=1)] for part in upper_z]
+    lowers = [lower_x] + [[along_z(part, -step) for part in lower_x] for step in (1, 2, 3)]
+
+    core = at["c"].astype(jnp.int32).reshape(1)
+    shards = [half[z][xh] for half in (uppers, lowers) for z in range(4) for xh in range(2)]
+    messages = project(core, shards, own_weight, sib_weight)
+    own = lax.all_to_all(messages, ("xl", "yh", "yl"), split_axis=0, concat_axis=0, tiled=True)
     sib = flip(own, c=1)
-    group = at["xl"] * 4 + at["yh"] * 2 + at["yl"]
-    place = jnp.stack([group, at["z"], at["xh"], at["c"]]).astype(jnp.int32)
-    heads = attend(place, jnp.stack(queries), own, sib)
-
-    out = lax.all_to_all(heads, ("xl", "yh", "z", "xh"), split_axis=0, concat_axis=0, tiled=True)
-    out = out.reshape(2, 2, 4, 2, ROWS, HD).transpose(4, 2, 3, 0, 1, 5)
+    place = jnp.stack([at["yl"], at["z"], at["xh"], at["c"]]).astype(jnp.int32)
+    heads = attend(place, own, sib)
+
+    out = lax.all_to_all(heads, ("xl", "yh", "yl", "z", "xh"), split_axis=0, concat_axis=0, tiled=True)
+    out = out.reshape(2, 2, 2, 4, 2, 2, PART // 2, HD).transpose(5, 2, 6, 3, 4, 0, 1, 7)
     return mixed, out.reshape(ROWS, CHANS)
 
 

time: 249 us -> 219 us (0.88); the launches traced: 244 us -> 218 us
  waiting for transfers between devices: 77.3 us -> 29.2 us
  blocking collectives: 38 us -> 74.2 us
  local copies, waits for them, and re-layouts: 33.1 us -> 18.9 us
  other arithmetic: 12.8 us -> 0.7 us
  Pallas kernels: 53.7 us -> 60.1 us
  starting transfers between devices: 28.6 us -> 34.4 us
    all_to_all x1 -> x2, blocking collectives: 19.2 us -> 55.4 us  [the longest x1 36.5 us: per_device(): lax.all_to_all(messages, ('xl', 'yh', 'yl'), split_axis=0, concat_axis=0,...]
    ppermute x16, waiting for transfers between devices: 60 us -> 25 us  [shift(): return lax.ppermute(x, NAMES, pairs)]
    another operation x2 -> x0, local copies, waits for them, and re-layouts: 15.4 us -> none  [the longest x1 14.7 us: per_device(): weights = jnp.stack([own_weight, flip(own_weight, c=1)])]
    all_to_all x1, waiting for transfers between devices: 17.3 us -> 4.24 us  [per_device(): lax.all_to_all(packed, NAMES, split_axis=0, concat_axis=0, tiled=True)]
    another operation x4 -> x1, other arithmetic: 12.8 us -> 0.7 us  [per_device(): place = jnp.stack([at['yl'], at['z'], at['xh'], at['c']]).astype(jnp.int32)]
    pallas_call x3, Pallas kernels: 37.9 us -> 44.2 us  [the longest x1 26.6 us: attend(): pl.pallas_call(attend_kernel, out_shape=jax.ShapeDtypeStruct((64, PART, H...]
    ppermute x16, starting transfers between devices: 17.4 us -> 23.1 us  [shift(): return lax.ppermute(x, NAMES, pairs)]
    unnamed x29 -> x38, local copies, waits for them, and re-layouts: 12.7 us -> 16.2 us
  transfers between devices with their start and end apart: 17 -> 17, of which waited for: 10 -> 9; matrix products, arithmetic and copies ran while one was open for 13% -> 7% of each run, Pallas kernels for 7% -> 1%
where the time goes in v2:
time: 219 us; the launch traced here: 218 us
  blocking collectives  74.2 us (34%)
  Pallas kernels  60.1 us (27%)
  starting transfers between devices  34.4 us (16%)
  waiting for transfers between devices  29.2 us (13%)
  local copies, waits for them, and re-layouts  18.9 us (9%)
    all_to_all x1, blocking collectives, per_device(): lax.all_to_all(messages, ('xl', 'yh', 'yl'), split_axis=0, concat_axis=0,...  36.5 us
    pallas_call x1, Pallas kernels, attend(): pl.pallas_call(attend_kernel, out_shape=jax.ShapeDtypeStruct((64, PART, H...  26.6 us
    ppermute x16, waiting for transfers between devices, shift(): return lax.ppermute(x, NAMES, pairs)  25 us
    ppermute x16, starting transfers between devices, shift(): return lax.ppermute(x, NAMES, pairs)  23.1 us
    all_to_all x1, blocking collectives, per_device(): lax.all_to_all(heads, ('xl', 'yh', 'yl', 'z', 'xh'), split_axis=0, concat...  18.9 us
    all_to_all x1, blocking collectives, per_device(): lax.all_to_all(filtered, NAMES, split_axis=0, concat_axis=0, tiled=True)  18.8 us
    unnamed x38, local copies, waits for them, and re-layouts  16.2 us
    pallas_call x1, Pallas kernels, project(): pl.pallas_call(project_kernel, out_shape=jax.ShapeDtypeStruct((8, 2, MESS...  15.3 us
  transfers between devices with their start and end apart: 17, of which 9 were waited for; matrix products, arithmetic and copies ran while one was open for 7% of the time, Pallas kernels for 1%

profile of v2, /device:TPU:0, one launch (start us, length us, event | category | flops | bytes accessed | tf_op | source)
XLA Modules:
  0.0 218.2 jit_solution(10954631261538171281)
XLA Ops:
  0.6 0.1 collective-permute-start
  0.7 2.7 %pack.1 = bf16[128,2,16,128]{3,2,1,0:T(8,128)(2,1)} custom-call(bf16[64,4096]{1,0:T(8,128)(2,1)} %key_ref.1, bf16[64,4096]{1,0:T(8,128)(2,1)} %value_ref.1, bf16[64,4096]{1,0:T(8,128)(2,1)} %taps_ref.1), custom_call_target="tpu_custom_call" | custom-call | tf_op jit(solution)/shard_map/pack/pallas_call | solution.py:74
  3.4 11.2 %all-to-all-start = ((bf16[128,2,16,128]{3,2,1,0:T(8,128)(2,1)}), bf16[128,2,16,128]{3,2,1,0:T(8,128)(2,1)S(1)}, u32[]{:S(2)}, u32[]{:S(2)}) async-start(bf16[128,2,16,128]{3,2,1,0:T(8,128)(2,1)} %pack.1), calls=%async_computation | async-start | bytes 2097152 | tf_op jit(solution)/shard_map/all_to_all | solution.py:418
  14.7 0.0 copy-start.3
  14.7 6.5 %copy.21 = bf16[512,8,2,384]{3,1,2,0:T(8,128)(2,1)} copy(bf16[512,8,2,384]{3,2,1,0:T(2,128)(2,1)} %bitcast.13) | data formatting | bytes 12582912
  21.2 0.1 dynamic-slice_bitcast_fusion
  21.3 0.1 copy.19
  21.4 0.1 broadcast_in_dim.3
  21.5 0.7 reshape.26.gain_ref
  22.2 0.0 collective-permute-done
  22.2 6.5 %copy.22 = bf16[512,8,2,384]{3,1,2,0:T(8,128)(2,1)} copy(bf16[512,8,2,384]{3,2,1,0:T(2,128)(2,1)} %bitcast.10) | data formatting | bytes 12582912
  28.7 4.2 %all-to-all-done.recv_ref = bf16[128,2,16,128]{3,2,1,0:T(8,128)(2,1)S(1)} async-done(((bf16[128,2,16,128]{3,2,1,0:T(8,128)(2,1)}), bf16[128,2,16,128]{3,2,1,0:T(8,128)(2,1)S(1)}, u32[]{:S(2)}, u32[]{:S(2)}) %all-to-all-start) | async-done | bytes 1048608 | tf_op jit(solution)/shard_map/all_to_all | solution.py:418
  32.9 1.0 copy-done.1
  33.9 13.2 %convolve.1 = bf16[128,16,128]{2,1,0:T(8,128)(2,1)} custom-call(bf16[128,2,16,128]{3,2,1,0:T(8,128)(2,1)} %copy-done.1, f32[16,128]{1,0:T(8,128)} %reshape.26.gain_ref, bf16[256,128]{1,0:T(8,128)(2,1)} %constant.57.clone.w1h, bf16[256,128]{1,0:T(8,128)(2,1)} %constant.58.clone.w1l, f32[128,128]{1,0:T(8,128)} %constant.59.clone.tc_ref, ...), custom_call_target="tpu_custom_call" | custom-call | tf_op jit(solution)/shard_map/convolve/pallas_call | solution.py:143
  47.1 18.8 %all_to_all.20.recv_ref = bf16[128,16,128]{2,1,0:T(8,128)(2,1)} all-to-all(bf16[128,16,128]{2,1,0:T(8,128)(2,1)} %convolve.1), channel_id=1, replica_groups=mesh['xl'=2,'yh'=2,'yl'=2,'z'=4,'xh'=2,'c'=2] {'xl','yh','yl','z','xh','c'}, dimensions={0} | all-to-all | bytes 1048576 | tf_op jit(solution)/shard_map/all_to_all | solution.py:427
  65.9 2.4 %apply_gate.1 = (bf16[64,4096]{1,0:T(8,128)(2,1)}, bf16[32,4096]{1,0:T(8,128)(2,1)}, bf16[32,4096]{1,0:T(8,128)(2,1)}) custom-call(bf16[128,16,128]{2,1,0:T(8,128)(2,1)} %all_to_all.20.recv_ref, bf16[64,4096]{1,0:T(8,128)(2,1)} %gate_ref.1), custom_call_target="tpu_custom_call" | custom-call | tf_op jit(solution)/shard_map/apply_gate/pallas_call | solution.py:171
  68.2 1.6 collective-permute-start.1
  69.8 0.7 collective-permute-start.2
  70.5 1.4 collective-permute-start.4
  71.8 0.9 collective-permute-start.6
  72.7 1.7 collective-permute-start.8
  74.4 4.7 %collective-permute-done.1.refs_1_ = bf16[32,4096]{1,0:T(8,128)(2,1)S(1)} collective-permute-done((bf16[32,4096]{1,0:T(8,128)(2,1)}, bf16[32,4096]{1,0:T(8,128)(2,1)S(1)}, u32[]{:S(2)}, u32[]{:S(2)}) %collective-permute-start.1) | collective-permute-done | bytes 262176 | tf_op jit(solution)/shard_map/ppermute | solution.py:395
  79.1 0.3 collective-permute-start.9
  79.4 1.5 collective-permute-start.11
  80.9 0.6 collective-permute-done.4.refs_4_
  81.5 4.3 %collective-permute-start.13 = (bf16[32,4096]{1,0:T(8,128)(2,1)}, bf16[32,4096]{1,0:T(8,128)(2,1)S(1)}, u32[]{:S(2)}, u32[]{:S(2)}) collective-permute-start(bf16[32,4096]{1,0:T(8,128)(2,1)} %get-tuple-element.11.refs_8_), channel_id=1, source_target_pairs={{0,4},{1,5},{2,6},{3,7},{4,8},{5,9},{6,10},{7,11},{8,12},{9,13},{1... | collective-permute-start | bytes 786440 | tf_op jit(solution)/shard_map/ppermute | solution.py:395
  85.7 1.4 collective-permute-done.6.refs_6_
  87.1 1.5 collective-permute-start.3
  88.7 2.0 collective-permute-start.5
  90.7 1.8 collective-permute-start.7
  92.4 0.3 collective-permute-done.11.refs_12_
  92.8 4.1 %collective-permute-start.10 = (bf16[32,4096]{1,0:T(8,128)(2,1)S(1)}, bf16[32,4096]{1,0:T(8,128)(2,1)S(1)}, u32[]{:S(2)}, u32[]{:S(2)}) collective-permute-start(bf16[32,4096]{1,0:T(8,128)(2,1)S(1)} %collective-permute-done.8.refs_9_), channel_id=1, source_target_pairs={{0,12},{1,13},{2,14},{3,15},{4,0},{5,1},{6,2},{7,3},{8,4},{9,5},{1... | collective-permute-start | bytes 786440 | tf_op jit(solution)/shard_map/ppermute | solution.py:395
  96.8 0.0 collective-permute-done.13.refs_14_
  96.8 1.3 collective-permute-start.12
  98.2 0.2 collective-permute-start.14
  98.3 5.1 %collective-permute-done.5.refs_5_ = bf16[32,4096]{1,0:T(8,128)(2,1)S(1)} collective-permute-done((bf16[32,4096]{1,0:T(8,128)(2,1)S(1)}, bf16[32,4096]{1,0:T(8,128)(2,1)S(1)}, u32[]{:S(2)}, u32[]{:S(2)}) %collective-permute-start.5) | collective-permute-done | bytes 262176 | tf_op jit(solution)/shard_map/ppermute | solution.py:395
  103.5 4.4 %collective-permute-done.7.refs_7_ = bf16[32,4096]{1,0:T(8,128)(2,1)S(1)} collective-permute-done((bf16[32,4096]{1,0:T(8,128)(2,1)S(1)}, bf16[32,4096]{1,0:T(8,128)(2,1)S(1)}, u32[]{:S(2)}, u32[]{:S(2)}) %collective-permute-start.7) | collective-permute-done | bytes 262176 | tf_op jit(solution)/shard_map/ppermute | solution.py:395
  107.9 4.2 %collective-permute-done.14.refs_15_ = bf16[32,4096]{1,0:T(8,128)(2,1)S(1)} collective-permute-done((bf16[32,4096]{1,0:T(8,128)(2,1)S(1)}, bf16[32,4096]{1,0:T(8,128)(2,1)S(1)}, u32[]{:S(2)}, u32[]{:S(2)}) %collective-permute-start.14) | collective-permute-done | bytes 262176 | tf_op jit(solution)/shard_map/ppermute | solution.py:395
  112.2 0.6 copy-done.17
  112.8 15.3 %project.1 = bf16[8,2,640,128]{3,2,1,0:T(8,128)(2,1)} custom-call(s32[1]{0:T(128)} %bitcast.4.core_ref, bf16[32,4096]{1,0:T(8,128)(2,1)} %get-tuple-element.10.refs_0_, bf16[32,4096]{1,0:T(8,128)(2,1)} %copy-done.4, bf16[32,4096]{1,0:T(8,128)(2,1)} %copy-done.5, bf16[32,4096]{1,0:T(8,128)(2,1)} %copy-done.12, bf16[32,4096]{1,0:T(8,128)(2,1)} %copy-done.6, ...), custom_call_target="tpu_custom_call" | custom-call | flops 6442450944 | bytes 12582912 | tf_op jit(solution)/shard_map/project/pallas_call | solution.py:226
  128.1 36.5 %all_to_all.21.refs_0_ = bf16[8,2,640,128]{3,2,1,0:T(8,128)(2,1)S(1)} all-to-all(bf16[8,2,640,128]{3,2,1,0:T(8,128)(2,1)} %project.1), channel_id=1, replica_groups=mesh['xl'=2,'yh'=2,'yl'=2,'z'=4,'xh'=2,'c'=2] {'xl','yh','yl'}, dimensions={0} | all-to-all | bytes 5242880 | tf_op jit(solution)/shard_map/all_to_all | solution.py:438
  164.5 0.7 pad_add_fusion.me_ref
  165.2 4.2 %collective-permute-done.15.refs_1_ = bf16[8,2,640,128]{3,2,1,0:T(8,128)(2,1)S(1)} collective-permute-done((bf16[8,2,640,128]{3,2,1,0:T(8,128)(2,1)S(1)}, bf16[8,2,640,128]{3,2,1,0:T(8,128)(2,1)S(1)}, u32[]{:S(2)}, u32[]{:S(2)}) %collective-permute-start.15) | collective-permute-done | bytes 2621472 | tf_op jit(solution)/shard_map/ppermute | solution.py:395
  169.4 1.5 copy-done.2
  171.0 26.6 %attend.1 = bf16[64,32,128]{2,1,0:T(8,128)(2,1)} custom-call(s32[4]{0:T(128)} %pad_add_fusion.me_ref, bf16[8,2,640,128]{3,2,1,0:T(8,128)(2,1)} %copy-done, bf16[8,2,640,128]{3,2,1,0:T(8,128)(2,1)} %copy-done.2), custom_call_target="tpu_custom_call" | custom-call | tf_op jit(solution)/shard_map/attend/pallas_call | solution.py:371
  197.6 18.9 %all_to_all.22 = bf16[64,32,128]{2,1,0:T(8,128)(2,1)S(1)} all-to-all(bf16[64,32,128]{2,1,0:T(8,128)(2,1)} %attend.1), channel_id=1, replica_groups=mesh['xl'=2,'yh'=2,'yl'=2,'z'=4,'xh'=2,'c'=2] {'xl','yh','yl','z','xh'}, dimensions={0} | all-to-all | bytes 1048576 | tf_op jit(solution)/shard_map/all_to_all | solution.py:443
  216.5 0.5 copy.20
  217.0 1.2 reshape.28
  (40 shorter events, 0.1 us)
Async XLA Ops:
  0.6 21.6 %collective-permute-start = (bf16[4096,2,384]{2,1,0:T(2,128)(2,1)}, bf16[4096,2,384]{2,1,0:T(2,128)(2,1)}, u32[]{:S(2)}, u32[]{:S(2)}) collective-permute-start(bf16[4096,2,384]{2,1,0:T(2,128)(2,1)} %param.21), channel_id=1, source_target_pairs={{0,1},{1,0},{2,3},{3,2},{4,5},{5,4},{6,7},{7,6},{8,9},{9,8},{10,11... | collective-permute-start | bytes 18874376 | tf_op jit(solution)/shard_map/ppermute | solution.py:395
  3.4 29.5 %all-to-all-start = ((bf16[128,2,16,128]{3,2,1,0:T(8,128)(2,1)}), bf16[128,2,16,128]{3,2,1,0:T(8,128)(2,1)S(1)}, u32[]{:S(2)}, u32[]{:S(2)}) async-start(bf16[128,2,16,128]{3,2,1,0:T(8,128)(2,1)} %pack.1), calls=%async_computation | async-start | bytes 2097152 | tf_op jit(solution)/shard_map/all_to_all | solution.py:418
  14.7 6.5 %copy-start.3 = (f32[4096]{0:T(1024)S(1)}, f32[4096]{0:T(1024)}, u32[]{:S(2)}) copy-start(f32[4096]{0:T(1024)} %param.20) | copy-start | bytes 49156
  32.9 1.0 copy-start.1
  68.2 10.9 %collective-permute-start.1 = (bf16[32,4096]{1,0:T(8,128)(2,1)}, bf16[32,4096]{1,0:T(8,128)(2,1)S(1)}, u32[]{:S(2)}, u32[]{:S(2)}) collective-permute-start(bf16[32,4096]{1,0:T(8,128)(2,1)} %get-tuple-element.10.refs_0_), channel_id=1, source_target_pairs={{0,2},{1,3},{2,0},{3,1},{4,6},{5,7},{6,4},{7,5},{8,10},{9,11},{10,... | collective-permute-start | bytes 786440 | tf_op jit(solution)/shard_map/ppermute | solution.py:395
  69.8 9.6 %collective-permute-start.2 = (bf16[32,4096]{1,0:T(8,128)(2,1)}, bf16[32,4096]{1,0:T(8,128)(2,1)S(1)}, u32[]{:S(2)}, u32[]{:S(2)}) collective-permute-start(bf16[32,4096]{1,0:T(8,128)(2,1)} %get-tuple-element.10.refs_0_), channel_id=1, source_target_pairs={{0,12},{1,13},{2,14},{3,15},{4,0},{5,1},{6,2},{7,3},{8,4},{9,5},{1... | collective-permute-start | bytes 786440 | tf_op jit(solution)/shard_map/ppermute | solution.py:395
  70.5 11.0 %collective-permute-start.4 = (bf16[32,4096]{1,0:T(8,128)(2,1)}, bf16[32,4096]{1,0:T(8,128)(2,1)S(1)}, u32[]{:S(2)}, u32[]{:S(2)}) collective-permute-start(bf16[32,4096]{1,0:T(8,128)(2,1)} %get-tuple-element.10.refs_0_), channel_id=1, source_target_pairs={{0,8},{1,9},{2,10},{3,11},{4,12},{5,13},{6,14},{7,15},{8,0},{9,1},... | collective-permute-start | bytes 786440 | tf_op jit(solution)/shard_map/ppermute | solution.py:395
  71.8 15.3 %collective-permute-start.6 = (bf16[32,4096]{1,0:T(8,128)(2,1)}, bf16[32,4096]{1,0:T(8,128)(2,1)S(1)}, u32[]{:S(2)}, u32[]{:S(2)}) collective-permute-start(bf16[32,4096]{1,0:T(8,128)(2,1)} %get-tuple-element.10.refs_0_), channel_id=1, source_target_pairs={{0,4},{1,5},{2,6},{3,7},{4,8},{5,9},{6,10},{7,11},{8,12},{9,13},{1... | collective-permute-start | bytes 786440 | tf_op jit(solution)/shard_map/ppermute | solution.py:395
  72.7 16.0 %collective-permute-start.8 = (bf16[32,4096]{1,0:T(8,128)(2,1)}, bf16[32,4096]{1,0:T(8,128)(2,1)S(1)}, u32[]{:S(2)}, u32[]{:S(2)}) collective-permute-start(bf16[32,4096]{1,0:T(8,128)(2,1)} %get-tuple-element.11.refs_8_), channel_id=1, source_target_pairs={{0,2},{1,3},{2,0},{3,1},{4,6},{5,7},{6,4},{7,5},{8,10},{9,11},{10,... | collective-permute-start | bytes 786440 | tf_op jit(solution)/shard_map/ppermute | solution.py:395
  79.1 33.0 %copy-start.4 = (bf16[32,4096]{1,0:T(8,128)(2,1)}, bf16[32,4096]{1,0:T(8,128)(2,1)S(1)}, u32[]{:S(2)}) copy-start(bf16[32,4096]{1,0:T(8,128)(2,1)S(1)} %collective-permute-done.1.refs_1_) | copy-start | bytes 786436
  79.1 11.6 %collective-permute-start.9 = (bf16[32,4096]{1,0:T(8,128)(2,1)}, bf16[32,4096]{1,0:T(8,128)(2,1)S(1)}, u32[]{:S(2)}, u32[]{:S(2)}) collective-permute-start(bf16[32,4096]{1,0:T(8,128)(2,1)} %get-tuple-element.11.refs_8_), channel_id=1, source_target_pairs={{0,12},{1,13},{2,14},{3,15},{4,0},{5,1},{6,2},{7,3},{8,4},{9,5},{1... | collective-permute-start | bytes 786440 | tf_op jit(solution)/shard_map/ppermute | solution.py:395
  79.4 32.7 %copy-start.5 = (bf16[32,4096]{1,0:T(8,128)(2,1)}, bf16[32,4096]{1,0:T(8,128)(2,1)S(1)}, u32[]{:S(2)}) copy-start(bf16[32,4096]{1,0:T(8,128)(2,1)S(1)} %collective-permute-done.2.refs_2_) | copy-start | bytes 786436
  79.4 13.3 %collective-permute-start.11 = (bf16[32,4096]{1,0:T(8,128)(2,1)}, bf16[32,4096]{1,0:T(8,128)(2,1)S(1)}, u32[]{:S(2)}, u32[]{:S(2)}) collective-permute-start(bf16[32,4096]{1,0:T(8,128)(2,1)} %get-tuple-element.11.refs_8_), channel_id=1, source_target_pairs={{0,8},{1,9},{2,10},{3,11},{4,12},{5,13},{6,14},{7,15},{8,0},{9,1},... | collective-permute-start | bytes 786440 | tf_op jit(solution)/shard_map/ppermute | solution.py:395
  81.5 30.6 %copy-start.6 = (bf16[32,4096]{1,0:T(8,128)(2,1)}, bf16[32,4096]{1,0:T(8,128)(2,1)S(1)}, u32[]{:S(2)}) copy-start(bf16[32,4096]{1,0:T(8,128)(2,1)S(1)} %collective-permute-done.4.refs_4_) | copy-start | bytes 786436
  81.5 15.3 %collective-permute-start.13 = (bf16[32,4096]{1,0:T(8,128)(2,1)}, bf16[32,4096]{1,0:T(8,128)(2,1)S(1)}, u32[]{:S(2)}, u32[]{:S(2)}) collective-permute-start(bf16[32,4096]{1,0:T(8,128)(2,1)} %get-tuple-element.11.refs_8_), channel_id=1, source_target_pairs={{0,4},{1,5},{2,6},{3,7},{4,8},{5,9},{6,10},{7,11},{8,12},{9,13},{1... | collective-permute-start | bytes 786440 | tf_op jit(solution)/shard_map/ppermute | solution.py:395
  87.1 24.9 %copy-start.7 = (bf16[32,4096]{1,0:T(8,128)(2,1)}, bf16[32,4096]{1,0:T(8,128)(2,1)S(1)}, u32[]{:S(2)}) copy-start(bf16[32,4096]{1,0:T(8,128)(2,1)S(1)} %collective-permute-done.6.refs_6_) | copy-start | bytes 786436
  87.1 11.0 %collective-permute-start.3 = (bf16[32,4096]{1,0:T(8,128)(2,1)S(1)}, bf16[32,4096]{1,0:T(8,128)(2,1)S(1)}, u32[]{:S(2)}, u32[]{:S(2)}) collective-permute-start(bf16[32,4096]{1,0:T(8,128)(2,1)S(1)} %collective-permute-done.2.refs_2_), channel_id=1, source_target_pairs={{0,2},{1,3},{2,0},{3,1},{4,6},{5,7},{6,4},{7,5},{8,10},{9,11},{10,... | collective-permute-start | bytes 786440 | tf_op jit(solution)/shard_map/ppermute | solution.py:395
  88.6 23.4 %copy-start.8 = (bf16[32,4096]{1,0:T(8,128)(2,1)}, bf16[32,4096]{1,0:T(8,128)(2,1)S(1)}, u32[]{:S(2)}) copy-start(bf16[32,4096]{1,0:T(8,128)(2,1)S(1)} %collective-permute-done.8.refs_9_) | copy-start | bytes 786436
  88.7 14.8 %collective-permute-start.5 = (bf16[32,4096]{1,0:T(8,128)(2,1)S(1)}, bf16[32,4096]{1,0:T(8,128)(2,1)S(1)}, u32[]{:S(2)}, u32[]{:S(2)}) collective-permute-start(bf16[32,4096]{1,0:T(8,128)(2,1)S(1)} %collective-permute-done.4.refs_4_), channel_id=1, source_target_pairs={{0,2},{1,3},{2,0},{3,1},{4,6},{5,7},{6,4},{7,5},{8,10},{9,11},{10,... | collective-permute-start | bytes 786440 | tf_op jit(solution)/shard_map/ppermute | solution.py:395
  90.7 21.4 %copy-start.9 = (bf16[32,4096]{1,0:T(8,128)(2,1)}, bf16[32,4096]{1,0:T(8,128)(2,1)S(1)}, u32[]{:S(2)}) copy-start(bf16[32,4096]{1,0:T(8,128)(2,1)S(1)} %collective-permute-done.9.refs_10_) | copy-start | bytes 786436
  90.7 17.2 %collective-permute-start.7 = (bf16[32,4096]{1,0:T(8,128)(2,1)S(1)}, bf16[32,4096]{1,0:T(8,128)(2,1)S(1)}, u32[]{:S(2)}, u32[]{:S(2)}) collective-permute-start(bf16[32,4096]{1,0:T(8,128)(2,1)S(1)} %collective-permute-done.6.refs_6_), channel_id=1, source_target_pairs={{0,2},{1,3},{2,0},{3,1},{4,6},{5,7},{6,4},{7,5},{8,10},{9,11},{10,... | collective-permute-start | bytes 786440 | tf_op jit(solution)/shard_map/ppermute | solution.py:395
  92.7 19.4 %copy-start.10 = (bf16[32,4096]{1,0:T(8,128)(2,1)}, bf16[32,4096]{1,0:T(8,128)(2,1)S(1)}, u32[]{:S(2)}) copy-start(bf16[32,4096]{1,0:T(8,128)(2,1)S(1)} %collective-permute-done.11.refs_12_) | copy-start | bytes 786436
  92.8 15.1 %collective-permute-start.10 = (bf16[32,4096]{1,0:T(8,128)(2,1)S(1)}, bf16[32,4096]{1,0:T(8,128)(2,1)S(1)}, u32[]{:S(2)}, u32[]{:S(2)}) collective-permute-start(bf16[32,4096]{1,0:T(8,128)(2,1)S(1)} %collective-permute-done.8.refs_9_), channel_id=1, source_target_pairs={{0,12},{1,13},{2,14},{3,15},{4,0},{5,1},{6,2},{7,3},{8,4},{9,5},{1... | collective-permute-start | bytes 786440 | tf_op jit(solution)/shard_map/ppermute | solution.py:395
  96.8 15.3 %copy-start.11 = (bf16[32,4096]{1,0:T(8,128)(2,1)}, bf16[32,4096]{1,0:T(8,128)(2,1)S(1)}, u32[]{:S(2)}) copy-start(bf16[32,4096]{1,0:T(8,128)(2,1)S(1)} %collective-permute-done.13.refs_14_) | copy-start | bytes 786436
  96.8 11.1 %collective-permute-start.12 = (bf16[32,4096]{1,0:T(8,128)(2,1)S(1)}, bf16[32,4096]{1,0:T(8,128)(2,1)S(1)}, u32[]{:S(2)}, u32[]{:S(2)}) collective-permute-start(bf16[32,4096]{1,0:T(8,128)(2,1)S(1)} %collective-permute-done.8.refs_9_), channel_id=1, source_target_pairs={{0,8},{1,9},{2,10},{3,11},{4,12},{5,13},{6,14},{7,15},{8,0},{9,1},... | collective-permute-start | bytes 786440 | tf_op jit(solution)/shard_map/ppermute | solution.py:395
  98.2 14.0 %copy-start.12 = (bf16[32,4096]{1,0:T(8,128)(2,1)}, bf16[32,4096]{1,0:T(8,128)(2,1)S(1)}, u32[]{:S(2)}) copy-start(bf16[32,4096]{1,0:T(8,128)(2,1)S(1)} %collective-permute-done.3.refs_3_) | copy-start | bytes 786436
  98.2 13.9 %collective-permute-start.14 = (bf16[32,4096]{1,0:T(8,128)(2,1)S(1)}, bf16[32,4096]{1,0:T(8,128)(2,1)S(1)}, u32[]{:S(2)}, u32[]{:S(2)}) collective-permute-start(bf16[32,4096]{1,0:T(8,128)(2,1)S(1)} %collective-permute-done.8.refs_9_), channel_id=1, source_target_pairs={{0,4},{1,5},{2,6},{3,7},{4,8},{5,9},{6,10},{7,11},{8,12},{9,13},{1... | collective-permute-start | bytes 786440 | tf_op jit(solution)/shard_map/ppermute | solution.py:395
  103.5 8.7 %copy-start.13 = (bf16[32,4096]{1,0:T(8,128)(2,1)}, bf16[32,4096]{1,0:T(8,128)(2,1)S(1)}, u32[]{:S(2)}) copy-start(bf16[32,4096]{1,0:T(8,128)(2,1)S(1)} %collective-permute-done.5.refs_5_) | copy-start | bytes 786436
  107.9 4.3 %copy-start.14 = (bf16[32,4096]{1,0:T(8,128)(2,1)}, bf16[32,4096]{1,0:T(8,128)(2,1)S(1)}, u32[]{:S(2)}) copy-start(bf16[32,4096]{1,0:T(8,128)(2,1)S(1)} %collective-permute-done.7.refs_7_) | copy-start | bytes 786436
  107.9 4.3 %copy-start.15 = (bf16[32,4096]{1,0:T(8,128)(2,1)}, bf16[32,4096]{1,0:T(8,128)(2,1)S(1)}, u32[]{:S(2)}) copy-start(bf16[32,4096]{1,0:T(8,128)(2,1)S(1)} %collective-permute-done.10.refs_11_) | copy-start | bytes 786436
  107.9 4.3 %copy-start.16 = (bf16[32,4096]{1,0:T(8,128)(2,1)}, bf16[32,4096]{1,0:T(8,128)(2,1)S(1)}, u32[]{:S(2)}) copy-start(bf16[32,4096]{1,0:T(8,128)(2,1)S(1)} %collective-permute-done.12.refs_13_) | copy-start | bytes 786436
  112.1 0.7 copy-start.17
  164.5 4.9 %copy-start = (bf16[8,2,640,128]{3,2,1,0:T(8,128)(2,1)}, bf16[8,2,640,128]{3,2,1,0:T(8,128)(2,1)S(1)}, u32[]{:S(2)}) copy-start(bf16[8,2,640,128]{3,2,1,0:T(8,128)(2,1)S(1)} %all_to_all.21.refs_0_) | copy-start | bytes 7864324
  164.5 4.9 %collective-permute-start.15 = (bf16[8,2,640,128]{3,2,1,0:T(8,128)(2,1)S(1)}, bf16[8,2,640,128]{3,2,1,0:T(8,128)(2,1)S(1)}, u32[]{:S(2)}, u32[]{:S(2)}) collective-permute-start(bf16[8,2,640,128]{3,2,1,0:T(8,128)(2,1)S(1)} %all_to_all.21.refs_0_), channel_id=1, source_target_pairs={{0,1},{1,0},{2,3},{3,2},{4,5},{5,4},{6,7},{7,6},{8,9},{9,8},{10,11... | collective-permute-start | bytes 7864328 | tf_op jit(solution)/shard_map/ppermute | solution.py:395
  169.4 1.5 copy-start.2

commit v3 on v2

v3 whole, which is shorter than its diff:
```python
import functools
import itertools
import math

import jax
import jax.numpy as jnp
import ml_dtypes
import numpy as np
from jax import lax
from jax.experimental import pallas as pl
from jax.experimental.pallas import tpu as pltpu
from jax.sharding import Mesh, PartitionSpec as P

BF = jnp.bfloat16
F32 = jnp.float32
NAMES = ("xl", "yh", "yl", "z", "xh", "c")
SIZES = (2, 2, 2, 4, 2, 2)
ROWS = 64
DEVS = 128
SEQ = ROWS * DEVS
CHANS = 4096
HALF = CHANS // 2
HD = 128
VMEM_LIMIT = 60 * 1024 * 1024


def split16(table):
    table = np.asarray(table, np.float64)
    high = table.astype(np.float32).astype(ml_dtypes.bfloat16)
    low = (table - high.astype(np.float64)).astype(np.float32).astype(ml_dtypes.bfloat16)
    return high, low


def conv_tables():
    d = np.arange(DEVS)
    k1 = np.arange(DEVS) + 0.25
    r = np.arange(ROWS)
    outer = 2 * math.pi * np.outer(k1, d) / DEVS
    first = np.concatenate([np.cos(outer), -np.sin(outer)], axis=0)
    twist = 2 * math.pi * np.outer(k1, r) / SEQ
    twist_cos = np.tile(np.cos(twist), (1, 2)).astype(np.float32)
    twist_sin = np.tile(np.sin(twist), (1, 2)).astype(np.float32)
    inner = 2 * math.pi * np.outer(r, r) / ROWS
    eye = np.eye(2)
    cos, sin = np.kron(eye, np.cos(inner)), np.kron(eye, np.sin(inner))
    second = np.block([[cos, -sin], [sin, cos]])
    third = np.block([[cos, sin], [-sin, cos]])
    last = np.concatenate([np.cos(outer).T, -np.sin(outer).T], axis=1) / SEQ
    return (*split16(first), twist_cos, twist_sin, *split16(second), *split16(third), *split16(last))


def whole(shape):
    return pl.BlockSpec(shape, lambda *_: (0,) * len(shape), memory_space=pltpu.VMEM)


def params(**more):
    return pltpu.CompilerParams(vmem_limit_bytes=VMEM_LIMIT, **more)


WIDE = CHANS // 16


def pack_kernel(key_ref, value_ref, taps_ref, gate_ref, out_ref, gate_out_ref):
    def both(ref, start):
        return jnp.concatenate(
            [ref[:, pl.ds(start + half * 128, 128)].astype(F32) for half in range(2)], axis=0
        )

    for block in range(16):
        start = block * WIDE
        product = (both(key_ref, start) * both(value_ref, start)).astype(BF).astype(F32)
        for which, tile in enumerate((product, both(taps_ref, start))):
            out_ref[:, block, which] = tile.T.astype(BF).reshape(8, 16, 128)
        gate_out_ref[block] = gate_ref[:, pl.ds(start, WIDE)]


def pack(key_signal, value_signal, long_filter, gate_signal):
    shapes = [(8, 16, 2, 16, 128), (16, ROWS, WIDE)]
    return pl.pallas_call(
        pack_kernel,
        out_shape=[jax.ShapeDtypeStruct(shape, BF) for shape in shapes],
        in_specs=[whole((ROWS, CHANS))] * 4,
        out_specs=[whole(shape) for shape in shapes],
        compiler_params=params(),
        name="pack",
    )(key_signal, value_signal, long_filter, gate_signal)


def dot(a, b):
    return jnp.dot(a, b, preferred_element_type=F32)


def cut(x):
    high = x.astype(BF)
    return high, (x - high.astype(F32)).astype(BF)


def conv_kernel(
    batch, recv_ref, gain_ref, w1h, w1l, tc_ref, ts_ref, m2h, m2l, m3h, m3l, w3h, w3l, out_ref, x_s, h_s, y_s
):
    x_s[...] = recv_ref[:, 0].astype(F32).reshape(DEVS * 16, 128)
    h_s[...] = recv_ref[:, 1].astype(F32).reshape(DEVS * 16, 128)
    tc = tc_ref[...]
    ts = ts_ref[...]

    def three(a, bh, bl):
        ah, al = cut(a)
        return dot(ah, bh) + (dot(al, bh) + dot(ah, bl))

    def step(it, carry):
        rows = [pl.ds(it * batch + u, DEVS, stride=16) for u in range(batch)]
        xs = [x_s[row, :] for row in rows]
        hs = [h_s[row, :] for row in rows]
        signal = jnp.concatenate([v.astype(BF) for v in xs + hs], axis=1)
        first = dot(w1h[...], signal) + dot(w1l[...], signal)
        stacked = []
        for u in range(2 * batch):
            re = first[:DEVS, u * 128 : u * 128 + 128]
            im = first[DEVS:, u * 128 : u * 128 + 128]
            stacked.append(jnp.concatenate([re * tc + im * ts, im * tc - re * ts], axis=1))
        spectrum = three(jnp.concatenate(stacked, axis=0), m2h[...], m2l[...])
        prods = []
        for u in range(batch):
            s = spectrum[u * 128 : u * 128 + 128]
            h = spectrum[(batch + u) * 128 : (batch + u) * 128 + 128]
            sr, si, hr, hi = s[:, :128], s[:, 128:], h[:, :128], h[:, 128:]
            prods.append(jnp.concatenate([sr * hr - si * hi, sr * hi + si * hr], axis=1))
        back = three(jnp.concatenate(prods, axis=0), m3h[...], m3l[...])
        outs = []
        for u in range(batch):
            re = back[u * 128 : u * 128 + 128, :128]
            im = back[u * 128 : u * 128 + 128, 128:]
            outs.append(jnp.concatenate([re * tc - im * ts, im * tc + re * ts], axis=0))
        vh, vl = cut(jnp.concatenate(outs, axis=1))
        conv = dot(w3h[...], vh) + (dot(w3l[...], vh) + dot(w3h[...], vl))
        for u in range(batch):
            gain = gain_ref[pl.ds(it * batch + u, 1), :]
            y_s[rows[u], :] = conv[:, u * 128 : u * 128 + 128] + gain * xs[u]
        return carry

    lax.fori_loop(0, 16 // batch, step, 0)
    out_ref[...] = y_s[...].reshape(DEVS, 16, 128).astype(BF)


def convolve(recv, gain, batch=16):
    tables = conv_tables()
    args = (recv, gain, *[jnp.asarray(t) for t in tables])
    return pl.pallas_call(
        functools.partial(conv_kernel, batch),
        out_shape=jax.ShapeDtypeStruct((DEVS, 16, 128), BF),
        in_specs=[whole(a.shape) for a in args],
        out_specs=whole((DEVS, 16, 128)),
        scratch_shapes=[pltpu.VMEM((DEVS * 16, 128), F32)] * 3,
        compiler_params=params(),
        name="convolve",
    )(*args)


PART = ROWS // 2
GROUP = 8 * ROWS
ASKED = GROUP // 2
MESSAGE = 2 * GROUP + ASKED


SPOTS = [(half, z, xh) for z in range(4) for xh in range(2) for half in range(2)]
EARLY = [(0, 0, 0), (1, 0, 0), (0, 0, 1), (0, 1, 0), (0, 3, 0), (0, 2, 0), (1, 0, 1), (1, 1, 0)]
LATE = [spot for spot in SPOTS if spot not in EARLY]


def place(at_ref, spot):
    half, z, xh = spot
    return ((at_ref[3] + z) & 3) * 4 + (at_ref[4] ^ xh) * 2 + (at_ref[5] ^ half)


def gate_kernel(at_ref, recv_ref, gate_ref, keep_ref, send_ref):
    for spot in range(16):
        tile = recv_ref[:, spot].astype(F32).reshape(128, 128).T
        wide = jnp.concatenate([tile[:ROWS], tile[ROWS:]], axis=1)
        mixed = (gate_ref[spot].astype(F32) * wide).astype(BF)
        first = spot // 2 * ROWS

        @pl.when(at_ref[5] == spot % 2)
        def _():
            keep_ref[first : first + ROWS] = mixed

        @pl.when(at_ref[5] != spot % 2)
        def _():
            send_ref[first : first + ROWS] = mixed


def apply_gate(at, recv, gate):
    return pl.pallas_call(
        gate_kernel,
        out_shape=[jax.ShapeDtypeStruct((GROUP, WIDE), BF)] * 2,
        in_specs=[pl.BlockSpec(memory_space=pltpu.SMEM), whole((8, 16, 16, 128)), whole((16, ROWS, WIDE))],
        out_specs=[whole((GROUP, WIDE))] * 2,
        compiler_params=params(),
        name="apply_gate",
    )(at, recv, gate)


def collect_kernel(at_ref, *refs):
    blocks, out_ref, sems = refs[:16], refs[16], refs[17]
    copies = []
    for n, block in enumerate(blocks):
        mine = pl.ds(pl.multiple_of((at_ref[3] * 2 + at_ref[4]) * ROWS, ROWS), ROWS)
        there = pl.ds(pl.multiple_of(place(at_ref, SPOTS[n]) * WIDE, WIDE), WIDE)
        copies.append(pltpu.make_async_copy(block.at[mine, :], out_ref.at[:, there], sems.at[n]))
    for copy in copies:
        copy.start()
    for copy in copies:
        copy.wait()


def collect(at, blocks):
    return pl.pallas_call(
        collect_kernel,
        out_shape=jax.ShapeDtypeStruct((ROWS, CHANS), BF),
        in_specs=[pl.BlockSpec(memory_space=pltpu.SMEM)] + [pl.BlockSpec(memory_space=pl.ANY)] * 16,
        out_specs=whole((ROWS, CHANS)),
        scratch_shapes=[pltpu.SemaphoreType.DMA((16,))],
        compiler_params=params(),
        name="collect",
    )(at, *blocks)


def project_kernel(final, at_ref, *refs):
    blocks = refs[:8]
    weights = refs[8:10]
    before = refs[10] if final else None
    out_ref, w_s, sems = refs[-3:]
    copies = []
    for n in range(8):
        for side in range(2):
            first = place(at_ref, (LATE if final else EARLY)[n]) * WIDE
            source = weights[side].at[pl.ds(pl.multiple_of(first, WIDE), WIDE), :]
            target = w_s.at[side, pl.ds(n * WIDE, WIDE), :]
            copies.append(pltpu.make_async_copy(source, target, sems.at[n, side]))
    for copy in copies:
        copy.start()
    total = [None, None]
    for chunk in range(2):
        x = jnp.concatenate([block[...] for block in blocks[chunk * 4 : chunk * 4 + 4]], axis=1)
        for copy in copies[chunk * 8 : chunk * 8 + 8]:
            copy.wait()
        for side in range(2):
            part = dot(x, w_s[side, chunk * 4 * WIDE : chunk * 4 * WIDE + 4 * WIDE])
            total[side] = part if chunk == 0 else total[side] + part
    if not final:
        for side in range(2):
            out_ref[side] = total[side]
        return
    for side in range(2):
        done = total[side] + before[side]
        for yh in range(2):
            start = yh * 3 * HD
            queries = done[:, start : start + HD].astype(BF).reshape(8, 2, PART, HD)
            keys = done[:, start + HD : start + 2 * HD].astype(BF)
            values = done[:, start + 2 * HD : start + 3 * HD]
            flipped = [values[n * HD : n * HD + HD].T.astype(BF) for n in range(GROUP // HD)]
            for yl in range(2):
                goal = (at_ref[5] ^ side) * 4 + yh * 2 + yl
                out_ref[goal, :GROUP] = keys
                for n, tile in enumerate(flipped):
                    out_ref[goal, GROUP + n * HD : GROUP + n * HD + HD] = tile
                out_ref[goal, 2 * GROUP :] = queries[:, yl].reshape(ASKED, HD)


def project(at, blocks, own, sib, before=None):
    share = (2, GROUP, 6 * HD)
    final = before is not None
    out = jax.ShapeDtypeStruct((8, MESSAGE, HD), BF) if final else jax.ShapeDtypeStruct(share, F32)
    return pl.pallas_call(
        functools.partial(project_kernel, final),
        out_shape=out,
        in_specs=[pl.BlockSpec(memory_space=pltpu.SMEM)]
        + [whole((GROUP, WIDE))] * 8
        + [pl.BlockSpec(memory_space=pl.ANY)] * 2
        + [whole(share)] * final,
        out_specs=whole(out.shape),
        scratch_shapes=[pltpu.VMEM((2, 8 * WIDE, 6 * HD), BF), pltpu.SemaphoreType.DMA((8, 2))],
        cost_estimate=pl.CostEstimate(
            flops=GROUP * CHANS * 12 * HD, bytes_accessed=CHANS * 12 * HD, transcendentals=0
        ),
        compiler_params=params(),
        name="project_last" if final else "project_first",
    )(at, *blocks, own, sib, *([before] * final))


SCALE = math.log2(math.e) / math.sqrt(HD)
EXTRA = 16
KEYS = 2 * GROUP
QUERIES = ASKED


PAIR = 2 * QUERIES
ROOM = 80.0
REACH = 170.0


def attend_kernel(at_ref, *refs):
    own_hbm, sib_hbm, out_ref, k_s, v_s, q_s, acc_s, sems = refs
    my_yl, my_c = at_ref[2], at_ref[5]

    def fetch(group):
        copies = []

        def add(source, target):
            copies.append(pltpu.make_async_copy(source, target, sems.at[group, len(copies)]))

        for n, source in enumerate((own_hbm, sib_hbm)):
            add(source.at[group, pl.ds(0, GROUP)], k_s.at[group, pl.ds(n * GROUP, GROUP)])
            for tile in range(GROUP // HD):
                add(
                    source.at[group, pl.ds(GROUP + tile * HD, HD)],
                    v_s.at[group, pl.ds(0, HD), pl.ds(n * GROUP + tile * HD, HD)],
                )
            if n == 0:
                add(source.at[group, pl.ds(2 * GROUP, ASKED)], q_s.at[group])
        return copies

    for group in range(8):
        for copy in fetch(group):
            copy.start()
    for group in range(8):
        v_s[group, HD:] = jnp.ones((EXTRA, KEYS), BF)

    row = lax.broadcasted_iota(jnp.int32, (KEYS, 1), 0)
    col = lax.broadcasted_iota(jnp.int32, (1, PAIR), 1)
    key_pos = ((row >> 6) & 7) * 128 + (my_c ^ (row >> 9)) * ROWS + (row & 63)
    query_pos = (col >> 8) * 1024 + ((col >> 5) & 7) * 128 + my_c * ROWS + my_yl * PART + (col & 31)

    def nt(a, b):
        return lax.dot_general(a, b, (((1,), (1,)), ((), ())), preferred_element_type=F32)

    def score(group, queries, which):
        s = nt(k_s[group], queries)
        if which is not None:
            s = jnp.where(key_pos + which * 1024 <= query_pos, s, -1e30)
        return s

    def pair(k, tallest):
        groups = (2 * k, 2 * k + 1)
        for group in groups:
            for copy in fetch(group):
                copy.wait()
        queries = jnp.concatenate([q_s[group] for group in groups], axis=0)
        itself = jnp.concatenate(
            [
                k_s[group, pl.ds(pl.multiple_of(shard * ROWS + my_yl * PART, PART), PART)]
                for group in groups
                for shard in range(8)
            ],
            axis=0,
        )
        ones = jnp.ones((16, HD), BF)
        for group in groups:
            square = nt(ones, jnp.square(k_s[group].astype(F32)).astype(BF))
            tallest = jnp.maximum(tallest, jnp.max(square[:8], axis=1, keepdims=True))
        size = nt(ones, jnp.square(queries.astype(F32)).astype(BF))[:1]
        bound = jnp.sqrt(size * tallest[:1]) * (SCALE * 1.02)
        product = (queries.astype(F32) * itself.astype(F32)).astype(BF)
        own = nt(ones, product)[:1] * SCALE
        safe = jnp.max(bound * 1.01 - own) <= REACH
        acc_s[...] = jnp.zeros(acc_s.shape, F32)

        @pl.when(safe)
        def _():
            offset = bound - ROOM

            def visit(group, which=None):
                weight = jnp.exp2(score(group, queries, which) * SCALE - offset).astype(BF)
                acc_s[...] += dot(v_s[group], weight)

            visit(groups[0], 0)
            visit(groups[1], 1)

            @pl.loop(0, 2 * k)
            def _(group):
                visit(group)

        @pl.when(jnp.logical_not(safe))
        def _():
            def visit(group, best, which=None):
                s = score(group, queries, which)
                new = jnp.maximum(best, jnp.max(s, axis=0, keepdims=True))
                weight = jnp.exp2((s - new) * SCALE).astype(BF)
                acc_s[...] = acc_s[...] * jnp.exp2((best - new) * SCALE) + dot(v_s[group], weight)
                return new

            best = visit(groups[0], jnp.full((1, PAIR), -1e30, F32), 0)
            best = visit(groups[1], best, 1)
            lax.fori_loop(0, 2 * k, visit, best)

        out = (acc_s[:HD] / acc_s[HD : HD + 1]).T.astype(BF)
        for n, group in enumerate(groups):
            for shard in range(8):
                first = n * QUERIES + shard * PART
                out_ref[group * 8 + shard] = out[first : first + PART]
        return tallest

    lax.fori_loop(0, 4, pair, jnp.zeros((8, 1), F32))


def attend(at, own, sib):
    return pl.pallas_call(
        attend_kernel,
        out_shape=jax.ShapeDtypeStruct((64, PART, HD), BF),
        in_specs=[pl.BlockSpec(memory_space=pltpu.SMEM)] + [pl.BlockSpec(memory_space=pl.ANY)] * 2,
        out_specs=whole((64, PART, HD)),
        scratch_shapes=[
            pltpu.VMEM((8, KEYS, HD), BF),
            pltpu.VMEM((8, HD + EXTRA, KEYS), BF),
            pltpu.VMEM((8, QUERIES, HD), BF),
            pltpu.VMEM((HD + EXTRA, PAIR), F32),
            pltpu.SemaphoreType.DMA((8, 11)),
        ],
        compiler_params=params(),
        name="attend",
    )(at, own, sib)


def shift(x, move):
    pairs = []
    for spot in itertools.product(*[range(n) for n in SIZES]):
        target = dict(zip(NAMES, spot))
        move(target)
        goal = [target[n] % size for n, size in zip(NAMES, SIZES)]
        pairs.append((int(np.ravel_multi_index(spot, SIZES)), int(np.ravel_multi_index(goal, SIZES))))
    return lax.ppermute(x, NAMES, pairs)


def along_z(x, step):
    def move(t):
        t["z"] = (t["z"] + step) % 4

    return shift(x, move)


def flip(x, **bits):
    def move(t):
        for name, bit in bits.items():
            t[name] ^= bit

    return shift(x, move)


def per_device(gate_signal, key_signal, value_signal, long_filter, skip_gain, head_weight):
    at = jnp.stack([lax.axis_index(name) for name in NAMES]).astype(jnp.int32)
    device = lax.axis_index(NAMES)

    packed, gate = pack(key_signal, value_signal, long_filter, gate_signal)
    packed = packed.reshape(DEVS, 2, 16, 128)
    recv = lax.all_to_all(packed, NAMES, split_axis=0, concat_axis=0, tiled=True)

    own_weight = head_weight.reshape(CHANS, 6 * HD)
    sib_weight = flip(head_weight, c=1).reshape(CHANS, 6 * HD)

    inner, outer = device % 16, device // 16
    gain = skip_gain.reshape(16, 2, 8, 16)[inner, :, outer]
    gain = jnp.repeat(gain.T, ROWS, axis=1)
    recv, own_weight, sib_weight, gate, at, gain = lax.optimization_barrier(
        (recv, own_weight, sib_weight, gate, at, gain)
    )
    gate = lax.all_to_all(gate, ("z", "xh", "c"), split_axis=0, concat_axis=0, tiled=True)
    filtered, gate = lax.optimization_barrier((convolve(recv, gain), gate))
    returned = lax.all_to_all(filtered, ("xl", "yh", "yl"), split_axis=0, concat_axis=0, tiled=True)
    kept, sent = apply_gate(at, returned.reshape(8, 16, 16, 128), gate)
    given = flip(sent, c=1)

    def round_z(part, way):
        near, far = along_z(part, -way), along_z(part, way)
        return {0: part, way % 4: near, -way % 4: far, 2: along_z(near, -way)}

    kept_z = round_z(kept, 1)
    given_z = [round_z(given, -1), round_z(flip(given, xh=1), 1)]
    blocks = {}
    for half, z, xh in SPOTS:
        if half == 1:
            blocks[half, z, xh] = given_z[xh][z]
        else:
            blocks[half, z, xh] = flip(kept_z[z], xh=1) if xh else kept_z[z]

    share = project(at, [blocks[spot] for spot in EARLY], own_weight, sib_weight)
    messages = project(at, [blocks[spot] for spot in LATE], own_weight, sib_weight, share)
    mixed = collect(at, [blocks[spot] for spot in SPOTS])

    own = lax.all_to_all(messages, ("xl", "yh", "yl"), split_axis=0, concat_axis=0, tiled=True)
    sib = flip(own, c=1)
    heads = attend(at, own, sib)

    out = lax.all_to_all(heads, ("xl", "yh", "yl", "z", "xh"), split_axis=0, concat_axis=0, tiled=True)
    out = out.reshape(2, 2, 2, 4, 2, PART, HD).transpose(2, 5, 3, 4, 0, 1, 6)
    return mixed, out.reshape(ROWS, CHANS)


def solution(mesh):
    fine = Mesh(mesh.devices.reshape(SIZES), NAMES)
    rows = P(NAMES, None)
    return jax.shard_map(
        per_device,
        mesh=fine,
        in_specs=(rows, rows, rows, rows, P(), P(None, ("z", "xh", "c"), None)),
        out_specs=(rows, rows),
        check_vma=False,
    )
```

time: 219 us -> 208 us (0.950)
  blocking collectives: 74.2 us -> 49.2 us
  Pallas kernels: 60.1 us -> 65.4 us
  starting transfers between devices: 34.4 us -> 39.7 us
  waiting for transfers between devices: 29.2 us -> 33.5 us
    all_to_all x2 -> x1, blocking collectives: 37.7 us -> 13.9 us  [per_device(): lax.all_to_all(filtered, ('xl', 'yh', 'yl'), split_axis=0, concat_axis=0,...]
    all_to_all x0 -> x2, waiting for transfers between devices: none -> 13.6 us  [the longest x1 10.9 us: per_device(): lax.all_to_all(heads, ('xl', 'yh', 'yl', 'z', 'xh'), split_axis=0, concat...]
    all_to_all x0 -> x2, starting transfers between devices: none -> 9.58 us  [the longest x1 5.42 us: per_device(): lax.all_to_all(heads, ('xl', 'yh', 'yl', 'z', 'xh'), split_axis=0, concat...]
    ppermute x16 -> x17, waiting for transfers between devices: 25 us -> 17 us  [shift(): return lax.ppermute(x, NAMES, pairs)]
    pallas_call x4 -> x6, Pallas kernels: 33.5 us -> 39 us  [the longest x2 20.1 us: project(): pl.pallas_call(functools.partial(project_kernel, final), out_shape=out, i...]
    ppermute x16 -> x17, starting transfers between devices: 23.1 us -> 18.9 us  [shift(): return lax.ppermute(x, NAMES, pairs)]
  transfers between devices with their start and end apart: 17 -> 20, of which waited for: 9 -> 9; matrix products, arithmetic and copies ran while one was open for 7% -> 7% of each run, Pallas kernels for 1% -> 12%
where the time goes in v3:
time: 208 us; the launch traced here: 207 us
  Pallas kernels  65.4 us (31%)
  blocking collectives  49.2 us (24%)
  starting transfers between devices  39.7 us (19%)
  waiting for transfers between devices  33.5 us (16%)
  local copies, waits for them, and re-layouts  18.7 us (9%)
    all_to_all x1, blocking collectives, per_device(): lax.all_to_all(messages, ('xl', 'yh', 'yl'), split_axis=0, concat_axis=0,...  35.2 us
    pallas_call x1, Pallas kernels, attend(): pl.pallas_call(attend_kernel, out_shape=jax.ShapeDtypeStruct((64, PART, H...  26.4 us
    pallas_call x2, Pallas kernels, project(): pl.pallas_call(functools.partial(project_kernel, final), out_shape=out, i...  20.1 us
    ppermute x17, starting transfers between devices, shift(): return lax.ppermute(x, NAMES, pairs)  18.9 us
    ppermute x17, waiting for transfers between devices, shift(): return lax.ppermute(x, NAMES, pairs)  17 us
    unnamed x38, local copies, waits for them, and re-layouts  14.7 us
    all_to_all x1, blocking collectives, per_device(): lax.all_to_all(filtered, ('xl', 'yh', 'yl'), split_axis=0, concat_axis=0,...  13.9 us
    all_to_all x1, starting transfers between devices, per_device(): lax.all_to_all(packed, NAMES, split_axis=0, concat_axis=0, tiled=True)  11.2 us
  transfers between devices with their start and end apart: 20, of which 9 were waited for; matrix products, arithmetic and copies ran while one was open for 7% of the time, Pallas kernels for 12%

profile of v3, /device:TPU:0, one launch (start us, length us, event | category | flops | bytes accessed | tf_op | source)
XLA Modules:
  0.0 207.4 jit_solution(9755259690131386904)
XLA Ops:
  0.6 0.1 collective-permute-start
  0.7 3.0 %pack.1 = (bf16[8,16,2,16,128]{4,3,2,1,0:T(8,128)(2,1)}, bf16[16,64,256]{2,1,0:T(8,128)(2,1)}) custom-call(bf16[64,4096]{1,0:T(8,128)(2,1)} %key_ref.1, bf16[64,4096]{1,0:T(8,128)(2,1)} %value_ref.1, bf16[64,4096]{1,0:T(8,128)(2,1)} %taps_ref.1, bf16[64,4096]{1,0:T(8,128)(2,1)} %gate_ref.1), custom_call_target="tpu_custom_call" | custom-call | tf_op jit(solution)/shard_map/pack/pallas_call | solution.py:79
  3.7 11.2 %all-to-all-start = ((bf16[128,2,16,128]{3,2,1,0:T(8,128)(2,1)}), bf16[128,2,16,128]{3,2,1,0:T(8,128)(2,1)S(1)}, u32[]{:S(2)}, u32[]{:S(2)}) async-start(bf16[128,2,16,128]{3,2,1,0:T(8,128)(2,1)} %bitcast.25), calls=%async_computation | async-start | bytes 2097152 | tf_op jit(solution)/shard_map/all_to_all | solution.py:454
  15.0 0.8 reshape.31
  15.9 0.1 copy.20
  16.0 0.1 broadcast_in_dim.3
  16.0 0.7 reshape.32.gain_ref
  16.7 6.5 %copy.22 = bf16[512,8,2,384]{3,1,2,0:T(8,128)(2,1)} copy(bf16[512,8,2,384]{3,2,1,0:T(2,128)(2,1)} %bitcast.22) | data formatting | bytes 12582912
  23.2 0.6 stack.27.at_ref
  23.9 6.5 %copy.23 = bf16[512,8,2,384]{3,1,2,0:T(8,128)(2,1)} copy(bf16[512,8,2,384]{3,2,1,0:T(2,128)(2,1)} %bitcast.16) | data formatting | bytes 12582912
  30.4 2.8 %all-to-all-done.recv_ref = bf16[128,2,16,128]{3,2,1,0:T(8,128)(2,1)S(1)} async-done(((bf16[128,2,16,128]{3,2,1,0:T(8,128)(2,1)}), bf16[128,2,16,128]{3,2,1,0:T(8,128)(2,1)S(1)}, u32[]{:S(2)}, u32[]{:S(2)}) %all-to-all-start) | async-done | bytes 1048608 | tf_op jit(solution)/shard_map/all_to_all | solution.py:454
  33.2 4.2 %all-to-all-start.1 = ((bf16[16,64,256]{2,1,0:T(8,128)(2,1)}), bf16[16,64,256]{2,1,0:T(8,128)(2,1)S(1)}, u32[]{:S(2)}, u32[]{:S(2)}) async-start(bf16[16,64,256]{2,1,0:T(8,128)(2,1)} %get-tuple-element.19), calls=%async_computation.1 | async-start | bytes 1048576 | tf_op jit(solution)/shard_map/all_to_all | solution.py:465
  37.4 9.6 %convolve.1 = bf16[128,16,128]{2,1,0:T(8,128)(2,1)} custom-call(bf16[128,2,16,128]{3,2,1,0:T(8,128)(2,1)} %copy-done.1, f32[16,128]{1,0:T(8,128)} %reshape.32.gain_ref, bf16[256,128]{1,0:T(8,128)(2,1)} %constant.79.clone.w1h, bf16[256,128]{1,0:T(8,128)(2,1)} %constant.80.clone.w1l, f32[128,128]{1,0:T(8,128)} %constant.81.clone.tc_ref, ...), custom_call_target="tpu_custom_call" | custom-call | tf_op jit(solution)/shard_map/convolve/pallas_call | solution.py:148
  47.0 2.8 %all-to-all-done.1.gate_ref = bf16[16,64,256]{2,1,0:T(8,128)(2,1)S(1)} async-done(((bf16[16,64,256]{2,1,0:T(8,128)(2,1)}), bf16[16,64,256]{2,1,0:T(8,128)(2,1)S(1)}, u32[]{:S(2)}, u32[]{:S(2)}) %all-to-all-start.1) | async-done | bytes 524320 | tf_op jit(solution)/shard_map/all_to_all | solution.py:465
  49.8 13.9 %all_to_all.25 = bf16[128,16,128]{2,1,0:T(8,128)(2,1)} all-to-all(bf16[128,16,128]{2,1,0:T(8,128)(2,1)} %convolve.1), channel_id=1, replica_groups=mesh['xl'=2,'yh'=2,'yl'=2,'z'=4,'xh'=2,'c'=2] {'xl','yh','yl'}, dimensions={0} | all-to-all | bytes 1048576 | tf_op jit(solution)/shard_map/all_to_all | solution.py:467
  63.7 3.7 %apply_gate.1 = (bf16[512,256]{1,0:T(8,128)(2,1)}, bf16[512,256]{1,0:T(8,128)(2,1)}) custom-call(s32[6]{0:T(128)} %stack.27.at_ref, bf16[8,16,16,128]{3,2,1,0:T(8,128)(2,1)} %bitcast.24, bf16[16,64,256]{2,1,0:T(8,128)(2,1)} %copy-done.2), custom_call_target="tpu_custom_call" | custom-call | tf_op jit(solution)/shard_map/apply_gate/pallas_call | solution.py:192
  67.4 0.1 collective-permute-start.13
  67.4 3.2 %collective-permute-start.4 = (bf16[512,256]{1,0:T(8,128)(2,1)}, bf16[512,256]{1,0:T(8,128)(2,1)S(1)}, u32[]{:S(2)}, u32[]{:S(2)}) collective-permute-start(bf16[512,256]{1,0:T(8,128)(2,1)} %get-tuple-element.22.refs_0_), channel_id=1, source_target_pairs={{0,12},{1,13},{2,14},{3,15},{4,0},{5,1},{6,2},{7,3},{8,4},{9,5},{1... | collective-permute-start | bytes 786440 | tf_op jit(solution)/shard_map/ppermute | solution.py:430
  70.6 1.9 collective-permute-start.2
  72.6 1.6 collective-permute-start.3
  74.2 3.5 %collective-permute-done.13.refs_12_.refs_4_ = bf16[512,256]{1,0:T(8,128)(2,1)S(1)} collective-permute-done((bf16[512,256]{1,0:T(8,128)(2,1)}, bf16[512,256]{1,0:T(8,128)(2,1)S(1)}, u32[]{:S(2)}, u32[]{:S(2)}) %collective-permute-start.13) | collective-permute-done | bytes 262176 | tf_op jit(solution)/shard_map/ppermute | solution.py:430
  77.6 0.3 collective-permute-start.5
  77.9 3.3 %collective-permute-start.14 = (bf16[512,256]{1,0:T(8,128)(2,1)S(1)}, bf16[512,256]{1,0:T(8,128)(2,1)S(1)}, u32[]{:S(2)}, u32[]{:S(2)}) collective-permute-start(bf16[512,256]{1,0:T(8,128)(2,1)S(1)} %collective-permute-done.13.refs_12_.refs_4_), channel_id=1, source_target_pairs={{0,2},{1,3},{2,0},{3,1},{4,6},{5,7},{6,4},{7,5},{8,10},{9,11},{10,... | collective-permute-start | bytes 786440 | tf_op jit(solution)/shard_map/ppermute | solution.py:430
  81.2 0.3 collective-permute-done.2.refs_2_
  81.5 0.9 collective-permute-start.8
  82.4 4.7 %collective-permute-done.3.refs_3_.refs_6_ = bf16[512,256]{1,0:T(8,128)(2,1)S(1)} collective-permute-done((bf16[512,256]{1,0:T(8,128)(2,1)S(1)}, bf16[512,256]{1,0:T(8,128)(2,1)S(1)}, u32[]{:S(2)}, u32[]{:S(2)}) %collective-permute-start.3) | collective-permute-done | bytes 262176 | tf_op jit(solution)/shard_map/ppermute | solution.py:430
  87.1 0.0 collective-permute-start.7
  87.1 3.3 %collective-permute-start.6 = (bf16[512,256]{1,0:T(8,128)(2,1)S(1)}, bf16[512,256]{1,0:T(8,128)(2,1)S(1)}, u32[]{:S(2)}, u32[]{:S(2)}) collective-permute-start(bf16[512,256]{1,0:T(8,128)(2,1)S(1)} %collective-permute-done.4.refs_4_.refs_3_), channel_id=1, source_target_pairs={{0,2},{1,3},{2,0},{3,1},{4,6},{5,7},{6,4},{7,5},{8,10},{9,11},{10,... | collective-permute-start | bytes 786440 | tf_op jit(solution)/shard_map/ppermute | solution.py:430
  90.5 0.6 collective-permute-start.15
  91.1 1.6 collective-permute-done.14.refs_14_.refs_6_
  92.8 2.0 collective-permute-start.11
  94.8 1.9 collective-permute-done.7.refs_7_.refs_1_
  96.7 1.5 collective-permute-start.12
  98.2 9.5 %project_first.1.refs_10_ = f32[2,512,768]{2,1,0:T(8,128)} custom-call(s32[6]{0:T(128)} %stack.27.at_ref, bf16[512,256]{1,0:T(8,128)(2,1)} %get-tuple-element.22.refs_0_, bf16[512,256]{1,0:T(8,128)(2,1)} %copy-done.3, bf16[512,256]{1,0:T(8,128)(2,1)} %copy-done.6, bf16[512,256]{1,0:T(8,128)(2,1)} %copy-done.5, bf16[512,256]{1,0:T(8,128)(2,1)} %copy-done.4, ...), custom_call_target="tpu_custom_call" | custom-call | flops 3221225472 | bytes 6291456 | tf_op jit(solution)/shard_map/project_first/pallas_call | solution.py:273
  107.8 0.6 copy-done.13
  108.5 0.1 copy-done.15
  108.6 0.1 copy-done.14
  108.7 0.1 copy-done.16
  108.8 0.7 copy-done.17
  109.5 10.6 %project_last.1 = bf16[8,1280,128]{2,1,0:T(8,128)(2,1)} custom-call(s32[6]{0:T(128)} %stack.27.at_ref, bf16[512,256]{1,0:T(8,128)(2,1)} %copy-done.13, bf16[512,256]{1,0:T(8,128)(2,1)} %copy-done.12, bf16[512,256]{1,0:T(8,128)(2,1)} %copy-done.15, bf16[512,256]{1,0:T(8,128)(2,1)} %copy-done.16, bf16[512,256]{1,0:T(8,128)(2,1)} %copy-done.17, ...), custom_call_target="tpu_custom_call" | custom-call | flops 3221225472 | bytes 6291456 | tf_op jit(solution)/shard_map/project_last/pallas_call | solution.py:273
  120.0 35.2 %all_to_all.26.refs_0_ = bf16[8,1280,128]{2,1,0:T(8,128)(2,1)S(1)} all-to-all(bf16[8,1280,128]{2,1,0:T(8,128)(2,1)} %project_last.1), channel_id=1, replica_groups=mesh['xl'=2,'yh'=2,'yl'=2,'z'=4,'xh'=2,'c'=2] {'xl','yh','yl'}, dimensions={0} | all-to-all | bytes 5242880 | tf_op jit(solution)/shard_map/all_to_all | solution.py:488
  155.3 5.0 %collective-permute-done.16.refs_1_ = bf16[8,1280,128]{2,1,0:T(8,128)(2,1)} collective-permute-done((bf16[8,1280,128]{2,1,0:T(8,128)(2,1)S(1)}, bf16[8,1280,128]{2,1,0:T(8,128)(2,1)}, u32[]{:S(2)}, u32[]{:S(2)}) %collective-permute-start.16) | collective-permute-done | bytes 2621472 | tf_op jit(solution)/shard_map/ppermute | solution.py:430
  160.3 26.4 %attend.1 = bf16[64,32,128]{2,1,0:T(8,128)(2,1)} custom-call(s32[6]{0:T(128)} %stack.27.at_ref, bf16[8,1280,128]{2,1,0:T(8,128)(2,1)} %copy-done, bf16[8,1280,128]{2,1,0:T(8,128)(2,1)} %collective-permute-done.16.refs_1_), custom_call_target="tpu_custom_call" | custom-call | tf_op jit(solution)/shard_map/attend/pallas_call | solution.py:406
  186.7 5.4 %all-to-all-start.4 = ((bf16[64,32,128]{2,1,0:T(8,128)(2,1)}), bf16[64,32,128]{2,1,0:T(8,128)(2,1)S(1)}, u32[]{:S(2)}, u32[]{:S(2)}) async-start(bf16[64,32,128]{2,1,0:T(8,128)(2,1)} %attend.1), calls=%async_computation.4 | async-start | bytes 1048576 | tf_op jit(solution)/shard_map/all_to_all | solution.py:492
  192.2 2.6 %collect.1 = bf16[64,4096]{1,0:T(8,128)(2,1)} custom-call(s32[6]{0:T(128)} %stack.27.at_ref, bf16[512,256]{1,0:T(8,128)(2,1)} %get-tuple-element.22.refs_0_, bf16[512,256]{1,0:T(8,128)(2,1)} %copy-done.3, bf16[512,256]{1,0:T(8,128)(2,1)} %copy-done.6, bf16[512,256]{1,0:T(8,128)(2,1)} %copy-done.7, bf16[512,256]{1,0:T(8,128)(2,1)} %copy-done.5, ...), custom_call_target="tpu_custom_call" | custom-call | tf_op jit(solution)/shard_map/collect/pallas_call | solution.py:216
  194.8 10.9 %all-to-all-done.4 = bf16[64,32,128]{2,1,0:T(8,128)(2,1)S(1)} async-done(((bf16[64,32,128]{2,1,0:T(8,128)(2,1)}), bf16[64,32,128]{2,1,0:T(8,128)(2,1)S(1)}, u32[]{:S(2)}, u32[]{:S(2)}) %all-to-all-start.4) | async-done | bytes 524320 | tf_op jit(solution)/shard_map/all_to_all | solution.py:492
  205.7 0.5 copy.21
  206.2 1.2 reshape.35
  (47 shorter events, 0.1 us)
Async XLA Ops:
  0.6 23.2 %collective-permute-start = (bf16[4096,2,384]{2,1,0:T(2,128)(2,1)}, bf16[4096,2,384]{2,1,0:T(2,128)(2,1)}, u32[]{:S(2)}, u32[]{:S(2)}) collective-permute-start(bf16[4096,2,384]{2,1,0:T(2,128)(2,1)} %param.21), channel_id=1, source_target_pairs={{0,1},{1,0},{2,3},{3,2},{4,5},{5,4},{6,7},{7,6},{8,9},{9,8},{10,11... | collective-permute-start | bytes 18874376 | tf_op jit(solution)/shard_map/ppermute | solution.py:430
  3.7 29.5 %all-to-all-start = ((bf16[128,2,16,128]{3,2,1,0:T(8,128)(2,1)}), bf16[128,2,16,128]{3,2,1,0:T(8,128)(2,1)S(1)}, u32[]{:S(2)}, u32[]{:S(2)}) async-start(bf16[128,2,16,128]{3,2,1,0:T(8,128)(2,1)} %bitcast.25), calls=%async_computation | async-start | bytes 2097152 | tf_op jit(solution)/shard_map/all_to_all | solution.py:454
  33.2 4.2 %copy-start.1 = (bf16[128,2,16,128]{3,2,1,0:T(8,128)(2,1)}, bf16[128,2,16,128]{3,2,1,0:T(8,128)(2,1)S(1)}, u32[]{:S(2)}) copy-start(bf16[128,2,16,128]{3,2,1,0:T(8,128)(2,1)S(1)} %all-to-all-done.recv_ref) | copy-start | bytes 3145732
  33.2 16.5 %all-to-all-start.1 = ((bf16[16,64,256]{2,1,0:T(8,128)(2,1)}), bf16[16,64,256]{2,1,0:T(8,128)(2,1)S(1)}, u32[]{:S(2)}, u32[]{:S(2)}) async-start(bf16[16,64,256]{2,1,0:T(8,128)(2,1)} %get-tuple-element.19), calls=%async_computation.1 | async-start | bytes 1048576 | tf_op jit(solution)/shard_map/all_to_all | solution.py:465
  49.8 13.9 %copy-start.2 = (bf16[16,64,256]{2,1,0:T(8,128)(2,1)}, bf16[16,64,256]{2,1,0:T(8,128)(2,1)S(1)}, u32[]{:S(2)}) copy-start(bf16[16,64,256]{2,1,0:T(8,128)(2,1)S(1)} %all-to-all-done.1.gate_ref) | copy-start | bytes 1572868
  67.4 5.2 %collective-permute-start.1 = (bf16[512,256]{1,0:T(8,128)(2,1)}, bf16[512,256]{1,0:T(8,128)(2,1)S(1)}, u32[]{:S(2)}, u32[]{:S(2)}) collective-permute-start(bf16[512,256]{1,0:T(8,128)(2,1)} %get-tuple-element.23), channel_id=1, source_target_pairs={{0,1},{1,0},{2,3},{3,2},{4,5},{5,4},{6,7},{7,6},{8,9},{9,8},{10,11... | collective-permute-start | bytes 786440 | tf_op jit(solution)/shard_map/ppermute | solution.py:430
  67.4 10.2 %collective-permute-start.13 = (bf16[512,256]{1,0:T(8,128)(2,1)}, bf16[512,256]{1,0:T(8,128)(2,1)S(1)}, u32[]{:S(2)}, u32[]{:S(2)}) collective-permute-start(bf16[512,256]{1,0:T(8,128)(2,1)} %get-tuple-element.22.refs_0_), channel_id=1, source_target_pairs={{0,4},{1,5},{2,6},{3,7},{4,8},{5,9},{6,10},{7,11},{8,12},{9,13},{1... | collective-permute-start | bytes 786440 | tf_op jit(solution)/shard_map/ppermute | solution.py:430
  67.4 10.5 %collective-permute-start.4 = (bf16[512,256]{1,0:T(8,128)(2,1)}, bf16[512,256]{1,0:T(8,128)(2,1)S(1)}, u32[]{:S(2)}, u32[]{:S(2)}) collective-permute-start(bf16[512,256]{1,0:T(8,128)(2,1)} %get-tuple-element.22.refs_0_), channel_id=1, source_target_pairs={{0,12},{1,13},{2,14},{3,15},{4,0},{5,1},{6,2},{7,3},{8,4},{9,5},{1... | collective-permute-start | bytes 786440 | tf_op jit(solution)/shard_map/ppermute | solution.py:430
  70.6 10.9 %collective-permute-start.2 = (bf16[512,256]{1,0:T(8,128)(2,1)}, bf16[512,256]{1,0:T(8,128)(2,1)S(1)}, u32[]{:S(2)}, u32[]{:S(2)}) collective-permute-start(bf16[512,256]{1,0:T(8,128)(2,1)} %get-tuple-element.22.refs_0_), channel_id=1, source_target_pairs={{0,2},{1,3},{2,0},{3,1},{4,6},{5,7},{6,4},{7,5},{8,10},{9,11},{10,... | collective-permute-start | bytes 786440 | tf_op jit(solution)/shard_map/ppermute | solution.py:430
  72.6 25.6 %copy-start.3 = (bf16[512,256]{1,0:T(8,128)(2,1)}, bf16[512,256]{1,0:T(8,128)(2,1)S(1)}, u32[]{:S(2)}) copy-start(bf16[512,256]{1,0:T(8,128)(2,1)S(1)} %collective-permute-done.1.refs_1_) | copy-start | bytes 786436
  72.6 14.6 %collective-permute-start.3 = (bf16[512,256]{1,0:T(8,128)(2,1)S(1)}, bf16[512,256]{1,0:T(8,128)(2,1)S(1)}, u32[]{:S(2)}, u32[]{:S(2)}) collective-permute-start(bf16[512,256]{1,0:T(8,128)(2,1)S(1)} %collective-permute-done.1.refs_1_), channel_id=1, source_target_pairs={{0,2},{1,3},{2,0},{3,1},{4,6},{5,7},{6,4},{7,5},{8,10},{9,11},{10,... | collective-permute-start | bytes 786440 | tf_op jit(solution)/shard_map/ppermute | solution.py:430
  74.1 13.0 %collective-permute-start.9 = (bf16[512,256]{1,0:T(8,128)(2,1)S(1)}, bf16[512,256]{1,0:T(8,128)(2,1)S(1)}, u32[]{:S(2)}, u32[]{:S(2)}) collective-permute-start(bf16[512,256]{1,0:T(8,128)(2,1)S(1)} %collective-permute-done.1.refs_1_), channel_id=1, source_target_pairs={{0,4},{1,5},{2,6},{3,7},{4,8},{5,9},{6,10},{7,11},{8,12},{9,13},{1... | collective-permute-start | bytes 786440 | tf_op jit(solution)/shard_map/ppermute | solution.py:430
  77.6 20.6 %copy-start.4 = (bf16[512,256]{1,0:T(8,128)(2,1)}, bf16[512,256]{1,0:T(8,128)(2,1)S(1)}, u32[]{:S(2)}) copy-start(bf16[512,256]{1,0:T(8,128)(2,1)S(1)} %collective-permute-done.13.refs_12_.refs_4_) | copy-start | bytes 786436
  77.6 12.8 %collective-permute-start.5 = (bf16[512,256]{1,0:T(8,128)(2,1)S(1)}, bf16[512,256]{1,0:T(8,128)(2,1)S(1)}, u32[]{:S(2)}, u32[]{:S(2)}) collective-permute-start(bf16[512,256]{1,0:T(8,128)(2,1)S(1)} %collective-permute-done.1.refs_1_), channel_id=1, source_target_pairs={{0,12},{1,13},{2,14},{3,15},{4,0},{5,1},{6,2},{7,3},{8,4},{9,5},{1... | collective-permute-start | bytes 786440 | tf_op jit(solution)/shard_map/ppermute | solution.py:430
  77.9 20.2 %copy-start.5 = (bf16[512,256]{1,0:T(8,128)(2,1)}, bf16[512,256]{1,0:T(8,128)(2,1)S(1)}, u32[]{:S(2)}) copy-start(bf16[512,256]{1,0:T(8,128)(2,1)S(1)} %collective-permute-done.4.refs_4_.refs_3_) | copy-start | bytes 786436
  77.9 14.8 %collective-permute-start.14 = (bf16[512,256]{1,0:T(8,128)(2,1)S(1)}, bf16[512,256]{1,0:T(8,128)(2,1)S(1)}, u32[]{:S(2)}, u32[]{:S(2)}) collective-permute-start(bf16[512,256]{1,0:T(8,128)(2,1)S(1)} %collective-permute-done.13.refs_12_.refs_4_), channel_id=1, source_target_pairs={{0,2},{1,3},{2,0},{3,1},{4,6},{5,7},{6,4},{7,5},{8,10},{9,11},{10,... | collective-permute-start | bytes 786440 | tf_op jit(solution)/shard_map/ppermute | solution.py:430
  81.5 16.7 %copy-start.6 = (bf16[512,256]{1,0:T(8,128)(2,1)}, bf16[512,256]{1,0:T(8,128)(2,1)S(1)}, u32[]{:S(2)}) copy-start(bf16[512,256]{1,0:T(8,128)(2,1)S(1)} %collective-permute-done.2.refs_2_) | copy-start | bytes 786436
  81.5 11.2 %collective-permute-start.8 = (bf16[512,256]{1,0:T(8,128)(2,1)S(1)}, bf16[512,256]{1,0:T(8,128)(2,1)S(1)}, u32[]{:S(2)}, u32[]{:S(2)}) collective-permute-start(bf16[512,256]{1,0:T(8,128)(2,1)S(1)} %collective-permute-done.4.refs_4_.refs_3_), channel_id=1, source_target_pairs={{0,12},{1,13},{2,14},{3,15},{4,0},{5,1},{6,2},{7,3},{8,4},{9,5},{1... | collective-permute-start | bytes 786440 | tf_op jit(solution)/shard_map/ppermute | solution.py:430
  87.1 11.1 %copy-start.7 = (bf16[512,256]{1,0:T(8,128)(2,1)}, bf16[512,256]{1,0:T(8,128)(2,1)S(1)}, u32[]{:S(2)}) copy-start(bf16[512,256]{1,0:T(8,128)(2,1)S(1)} %collective-permute-done.3.refs_3_.refs_6_) | copy-start | bytes 786436
  87.1 9.6 %collective-permute-start.7 = (bf16[512,256]{1,0:T(8,128)(2,1)S(1)}, bf16[512,256]{1,0:T(8,128)(2,1)S(1)}, u32[]{:S(2)}, u32[]{:S(2)}) collective-permute-start(bf16[512,256]{1,0:T(8,128)(2,1)S(1)} %collective-permute-done.3.refs_3_.refs_6_), channel_id=1, source_target_pairs={{0,12},{1,13},{2,14},{3,15},{4,0},{5,1},{6,2},{7,3},{8,4},{9,5},{1... | collective-permute-start | bytes 786440 | tf_op jit(solution)/shard_map/ppermute | solution.py:430
  87.1 20.6 %copy-start.8 = (bf16[512,256]{1,0:T(8,128)(2,1)}, bf16[512,256]{1,0:T(8,128)(2,1)S(1)}, u32[]{:S(2)}) copy-start(bf16[512,256]{1,0:T(8,128)(2,1)S(1)} %collective-permute-done.9.refs_13_.refs_5_) | copy-start | bytes 786436
  87.1 20.6 %collective-permute-start.6 = (bf16[512,256]{1,0:T(8,128)(2,1)S(1)}, bf16[512,256]{1,0:T(8,128)(2,1)S(1)}, u32[]{:S(2)}, u32[]{:S(2)}) collective-permute-start(bf16[512,256]{1,0:T(8,128)(2,1)S(1)} %collective-permute-done.4.refs_4_.refs_3_), channel_id=1, source_target_pairs={{0,2},{1,3},{2,0},{3,1},{4,6},{5,7},{6,4},{7,5},{8,10},{9,11},{10,... | collective-permute-start | bytes 786440 | tf_op jit(solution)/shard_map/ppermute | solution.py:430
  90.5 7.7 %copy-start.9 = (bf16[512,256]{1,0:T(8,128)(2,1)}, bf16[512,256]{1,0:T(8,128)(2,1)S(1)}, u32[]{:S(2)}) copy-start(bf16[512,256]{1,0:T(8,128)(2,1)S(1)} %collective-permute-done.5.refs_5_.refs_7_) | copy-start | bytes 786436
  90.5 17.3 %collective-permute-start.15 = (bf16[512,256]{1,0:T(8,128)(2,1)S(1)}, bf16[512,256]{1,0:T(8,128)(2,1)S(1)}, u32[]{:S(2)}, u32[]{:S(2)}) collective-permute-start(bf16[512,256]{1,0:T(8,128)(2,1)S(1)} %collective-permute-done.3.refs_3_.refs_6_), channel_id=1, source_target_pairs={{0,4},{1,5},{2,6},{3,7},{4,8},{5,9},{6,10},{7,11},{8,12},{9,13},{1... | collective-permute-start | bytes 786440 | tf_op jit(solution)/shard_map/ppermute | solution.py:430
  92.7 15.0 %copy-start.10 = (bf16[512,256]{1,0:T(8,128)(2,1)}, bf16[512,256]{1,0:T(8,128)(2,1)S(1)}, u32[]{:S(2)}) copy-start(bf16[512,256]{1,0:T(8,128)(2,1)S(1)} %collective-permute-done.14.refs_14_.refs_6_) | copy-start | bytes 786436
  92.7 15.0 %collective-permute-start.10 = (bf16[512,256]{1,0:T(8,128)(2,1)S(1)}, bf16[512,256]{1,0:T(8,128)(2,1)S(1)}, u32[]{:S(2)}, u32[]{:S(2)}) collective-permute-start(bf16[512,256]{1,0:T(8,128)(2,1)S(1)} %collective-permute-done.9.refs_13_.refs_5_), channel_id=1, source_target_pairs={{0,4},{1,5},{2,6},{3,7},{4,8},{5,9},{6,10},{7,11},{8,12},{9,13},{1... | collective-permute-start | bytes 786440 | tf_op jit(solution)/shard_map/ppermute | solution.py:430
  92.8 5.5 %copy-start.11 = (bf16[512,256]{1,0:T(8,128)(2,1)}, bf16[512,256]{1,0:T(8,128)(2,1)S(1)}, u32[]{:S(2)}) copy-start(bf16[512,256]{1,0:T(8,128)(2,1)S(1)} %collective-permute-done.8.refs_8_.refs_5_) | copy-start | bytes 786436
  92.8 15.0 %collective-permute-start.11 = (bf16[512,256]{1,0:T(8,128)(2,1)S(1)}, bf16[512,256]{1,0:T(8,128)(2,1)S(1)}, u32[]{:S(2)}, u32[]{:S(2)}) collective-permute-start(bf16[512,256]{1,0:T(8,128)(2,1)S(1)} %collective-permute-done.8.refs_8_.refs_5_), channel_id=1, source_target_pairs={{0,2},{1,3},{2,0},{3,1},{4,6},{5,7},{6,4},{7,5},{8,10},{9,11},{10,... | collective-permute-start | bytes 786440 | tf_op jit(solution)/shard_map/ppermute | solution.py:430
  96.7 11.0 %copy-start.12 = (bf16[512,256]{1,0:T(8,128)(2,1)}, bf16[512,256]{1,0:T(8,128)(2,1)S(1)}, u32[]{:S(2)}) copy-start(bf16[512,256]{1,0:T(8,128)(2,1)S(1)} %collective-permute-done.7.refs_7_.refs_1_) | copy-start | bytes 786436
  96.7 11.1 %collective-permute-start.12 = (bf16[512,256]{1,0:T(8,128)(2,1)S(1)}, bf16[512,256]{1,0:T(8,128)(2,1)S(1)}, u32[]{:S(2)}, u32[]{:S(2)}) collective-permute-start(bf16[512,256]{1,0:T(8,128)(2,1)S(1)} %collective-permute-done.7.refs_7_.refs_1_), channel_id=1, source_target_pairs={{0,12},{1,13},{2,14},{3,15},{4,0},{5,1},{6,2},{7,3},{8,4},{9,5},{1... | collective-permute-start | bytes 786440 | tf_op jit(solution)/shard_map/ppermute | solution.py:430
  107.8 0.7 copy-start.13
  107.8 0.8 copy-start.15
  107.8 0.9 copy-start.14
  107.8 0.9 copy-start.16
  108.8 0.7 copy-start.17
  155.3 5.0 %copy-start = (bf16[8,1280,128]{2,1,0:T(8,128)(2,1)}, bf16[8,1280,128]{2,1,0:T(8,128)(2,1)S(1)}, u32[]{:S(2)}) copy-start(bf16[8,1280,128]{2,1,0:T(8,128)(2,1)S(1)} %all_to_all.26.refs_0_) | copy-start | bytes 7864324
  155.3 5.0 %collective-permute-start.16 = (bf16[8,1280,128]{2,1,0:T(8,128)(2,1)S(1)}, bf16[8,1280,128]{2,1,0:T(8,128)(2,1)}, u32[]{:S(2)}, u32[]{:S(2)}) collective-permute-start(bf16[8,1280,128]{2,1,0:T(8,128)(2,1)S(1)} %all_to_all.26.refs_0_), channel_id=1, source_target_pairs={{0,1},{1,0},{2,3},{3,2},{4,5},{5,4},{6,7},{7,6},{8,9},{9,8},{10,11... | collective-permute-start | bytes 7864328 | tf_op jit(solution)/shard_map/ppermute | solution.py:430
  186.7 18.9 %all-to-all-start.4 = ((bf16[64,32,128]{2,1,0:T(8,128)(2,1)}), bf16[64,32,128]{2,1,0:T(8,128)(2,1)S(1)}, u32[]{:S(2)}, u32[]{:S(2)}) async-start(bf16[64,32,128]{2,1,0:T(8,128)(2,1)} %attend.1), calls=%async_computation.4 | async-start | bytes 1048576 | tf_op jit(solution)/shard_map/all_to_all | solution.py:492

commit v4 on v3

--- a/solution.py
+++ b/solution.py
@@ -46,7 +46,15 @@
     second = np.block([[cos, -sin], [sin, cos]])
     third = np.block([[cos, sin], [-sin, cos]])
     last = np.concatenate([np.cos(outer).T, -np.sin(outer).T], axis=1) / SEQ
-    return (*split16(first), twist_cos, twist_sin, *split16(second), *split16(third), *split16(last))
+    first, second, third, last = [split16(table) for table in (first, second, third, last)]
+    return (
+        np.concatenate(first, axis=1),
+        twist_cos,
+        twist_sin,
+        np.concatenate([second[0], second[0], second[1]], axis=0),
+        np.concatenate([third[0], third[0], third[1]], axis=0),
+        np.concatenate([last[0], last[1], last[0]], axis=1),
+    )
 
 
 def whole(shape):
@@ -96,43 +104,43 @@
 
 
 def conv_kernel(
-    batch, recv_ref, gain_ref, w1h, w1l, tc_ref, ts_ref, m2h, m2l, m3h, m3l, w3h, w3l, out_ref, x_s, h_s, y_s
+    batch, recv_ref, gain_ref, w1, tc_ref, ts_ref, m2, m3, w3, out_ref, x_s, h_s, y_s
 ):
     x_s[...] = recv_ref[:, 0].astype(F32).reshape(DEVS * 16, 128)
     h_s[...] = recv_ref[:, 1].astype(F32).reshape(DEVS * 16, 128)
     tc = tc_ref[...]
     ts = ts_ref[...]
 
-    def three(a, bh, bl):
+    def three(a, b):
         ah, al = cut(a)
-        return dot(ah, bh) + (dot(al, bh) + dot(ah, bl))
+        return dot(jnp.concatenate([ah, al, ah], axis=1), b)
 
     def step(it, carry):
         rows = [pl.ds(it * batch + u, DEVS, stride=16) for u in range(batch)]
         xs = [x_s[row, :] for row in rows]
         hs = [h_s[row, :] for row in rows]
         signal = jnp.concatenate([v.astype(BF) for v in xs + hs], axis=1)
-        first = dot(w1h[...], signal) + dot(w1l[...], signal)
+        first = dot(w1[...], jnp.concatenate([signal, signal], axis=0))
         stacked = []
         for u in range(2 * batch):
             re = first[:DEVS, u * 128 : u * 128 + 128]
             im = first[DEVS:, u * 128 : u * 128 + 128]
             stacked.append(jnp.concatenate([re * tc + im * ts, im * tc - re * ts], axis=1))
-        spectrum = three(jnp.concatenate(stacked, axis=0), m2h[...], m2l[...])
+        spectrum = three(jnp.concatenate(stacked, axis=0), m2[...])
         prods = []
         for u in range(batch):
             s = spectrum[u * 128 : u * 128 + 128]
             h = spectrum[(batch + u) * 128 : (batch + u) * 128 + 128]
             sr, si, hr, hi = s[:, :128], s[:, 128:], h[:, :128], h[:, 128:]
             prods.append(jnp.concatenate([sr * hr - si * hi, sr * hi + si * hr], axis=1))
-        back = three(jnp.concatenate(prods, axis=0), m3h[...], m3l[...])
+        back = three(jnp.concatenate(prods, axis=0), m3[...])
         outs = []
         for u in range(batch):
             re = back[u * 128 : u * 128 + 128, :128]
             im = back[u * 128 : u * 128 + 128, 128:]
             outs.append(jnp.concatenate([re * tc - im * ts, im * tc + re * ts], axis=0))
         vh, vl = cut(jnp.concatenate(outs, axis=1))
-        conv = dot(w3h[...], vh) + (dot(w3l[...], vh) + dot(w3h[...], vl))
+        conv = dot(w3[...], jnp.concatenate([vh, vh, vl], axis=0))
         for u in range(batch):
             gain = gain_ref[pl.ds(it * batch + u, 1), :]
             y_s[rows[u], :] = conv[:, u * 128 : u * 128 + 128] + gain * xs[u]
@@ -164,7 +172,7 @@
 
 SPOTS = [(half, z, xh) for z in range(4) for xh in range(2) for half in range(2)]
 EARLY = [(0, 0, 0), (1, 0, 0), (0, 0, 1), (0, 1, 0), (0, 3, 0), (0, 2, 0), (1, 0, 1), (1, 1, 0)]
-LATE = [spot for spot in SPOTS if spot not in EARLY]
+STAGES = [EARLY, [spot for spot in SPOTS if spot not in EARLY]]
 
 
 def place(at_ref, spot):
@@ -173,19 +181,12 @@
 
 
 def gate_kernel(at_ref, recv_ref, gate_ref, keep_ref, send_ref):
-    for spot in range(16):
-        tile = recv_ref[:, spot].astype(F32).reshape(128, 128).T
-        wide = jnp.concatenate([tile[:ROWS], tile[ROWS:]], axis=1)
-        mixed = (gate_ref[spot].astype(F32) * wide).astype(BF)
-        first = spot // 2 * ROWS
-
-        @pl.when(at_ref[5] == spot % 2)
-        def _():
-            keep_ref[first : first + ROWS] = mixed
-
-        @pl.when(at_ref[5] != spot % 2)
-        def _():
-            send_ref[first : first + ROWS] = mixed
+    for side, ref in enumerate((keep_ref, send_ref)):
+        for pair in range(8):
+            spot = pair * 2 + (at_ref[5] ^ side)
+            tile = recv_ref[:, spot].astype(F32).reshape(128, 128).T
+            wide = jnp.concatenate([tile[:ROWS], tile[ROWS:]], axis=1)
+            ref[pair * ROWS : pair * ROWS + ROWS] = (gate_ref[spot].astype(F32) * wide).astype(BF)
 
 
 def apply_gate(at, recv, gate):
@@ -224,34 +225,47 @@
     )(at, *blocks)
 
 
-def project_kernel(final, at_ref, *refs):
-    blocks = refs[:8]
-    weights = refs[8:10]
-    before = refs[10] if final else None
-    out_ref, w_s, sems = refs[-3:]
-    copies = []
-    for n in range(8):
-        for side in range(2):
-            first = place(at_ref, (LATE if final else EARLY)[n]) * WIDE
-            source = weights[side].at[pl.ds(pl.multiple_of(first, WIDE), WIDE), :]
-            target = w_s.at[side, pl.ds(n * WIDE, WIDE), :]
-            copies.append(pltpu.make_async_copy(source, target, sems.at[n, side]))
-    for copy in copies:
-        copy.start()
-    total = [None, None]
-    for chunk in range(2):
-        x = jnp.concatenate([block[...] for block in blocks[chunk * 4 : chunk * 4 + 4]], axis=1)
-        for copy in copies[chunk * 8 : chunk * 8 + 8]:
+def project_kernel(stage, at_ref, *refs):
+    spots = STAGES[stage]
+    first, last = stage == 0, stage == len(STAGES) - 1
+    blocks, refs = refs[: len(spots)], refs[len(spots) :]
+    weights, refs = refs[:2], refs[2:]
+    before, refs = (None, refs) if first else (refs[0], refs[1:])
+    out_ref, x_s, w_s, acc, goal_s, load_sems, save_sems = refs
+    loads = []
+
+    def load(source, target):
+        loads.append(pltpu.make_async_copy(source, target, load_sems.at[len(loads)]))
+        loads[-1].start()
+
+    for n, block in enumerate(blocks):
+        load(block, x_s.at[:, pl.ds(n * WIDE, WIDE)])
+    for side in range(2):
+        for n, spot in enumerate(spots):
+            rows = pl.ds(pl.multiple_of(place(at_ref, spot) * WIDE, WIDE), WIDE)
+            load(weights[side].at[rows, :], w_s.at[side, pl.ds(n * WIDE, WIDE)])
+        if not first:
+            load(before.at[side], acc.at[side])
+    per_side = len(spots) + (not first)
+    for copy in loads[: len(spots)]:
+        copy.wait()
+
+    saves = []
+
+    def save(source, target):
+        saves.append(pltpu.make_async_copy(source, target, save_sems.at[len(saves)]))
+        saves[-1].start()
+
+    for side in range(2):
+        for copy in loads[len(spots) + side * per_side : len(spots) + (side + 1) * per_side]:
             copy.wait()
-        for side in range(2):
-            part = dot(x, w_s[side, chunk * 4 * WIDE : chunk * 4 * WIDE + 4 * WIDE])
-            total[side] = part if chunk == 0 else total[side] + part
-    if not final:
-        for side in range(2):
-            out_ref[side] = total[side]
-        return
-    for side in range(2):
-        done = total[side] + before[side]
+        done = dot(x_s[...], w_s[side])
+        if not first:
+            done = done + acc[side]
+        if not last:
+            acc[side] = done
+            save(acc.at[side], out_ref.at[side])
+            continue
         for yh in range(2):
             start = yh * 3 * HD
             queries = done[:, start : start + HD].astype(BF).reshape(8, 2, PART, HD)
@@ -259,41 +273,48 @@
             values = done[:, start + 2 * HD : start + 3 * HD]
             flipped = [values[n * HD : n * HD + HD].T.astype(BF) for n in range(GROUP // HD)]
             for yl in range(2):
-                goal = (at_ref[5] ^ side) * 4 + yh * 2 + yl
-                out_ref[goal, :GROUP] = keys
+                slot = side * 4 + yh * 2 + yl
+                goal_s[slot, :GROUP] = keys
                 for n, tile in enumerate(flipped):
-                    out_ref[goal, GROUP + n * HD : GROUP + n * HD + HD] = tile
-                out_ref[goal, 2 * GROUP :] = queries[:, yl].reshape(ASKED, HD)
-
-
-def project(at, blocks, own, sib, before=None):
+                    goal_s[slot, GROUP + n * HD : GROUP + n * HD + HD] = tile
+                goal_s[slot, 2 * GROUP :] = queries[:, yl].reshape(ASKED, HD)
+                save(goal_s.at[slot], out_ref.at[(at_ref[5] ^ side) * 4 + yh * 2 + yl])
+    for copy in saves:
+        copy.wait()
+
+
+def project(stage, at, blocks, own, sib, before=None):
     share = (2, GROUP, 6 * HD)
-    final = before is not None
-    out = jax.ShapeDtypeStruct((8, MESSAGE, HD), BF) if final else jax.ShapeDtypeStruct(share, F32)
+    message = (8, MESSAGE, HD)
+    last = stage == len(STAGES) - 1
+    count = len(blocks)
     return pl.pallas_call(
-        functools.partial(project_kernel, final),
-        out_shape=out,
+        functools.partial(project_kernel, stage),
+        out_shape=jax.ShapeDtypeStruct(message, BF) if last else jax.ShapeDtypeStruct(share, F32),
         in_specs=[pl.BlockSpec(memory_space=pltpu.SMEM)]
-        + [whole((GROUP, WIDE))] * 8
-        + [pl.BlockSpec(memory_space=pl.ANY)] * 2
-        + [whole(share)] * final,
-        out_specs=whole(out.shape),
-        scratch_shapes=[pltpu.VMEM((2, 8 * WIDE, 6 * HD), BF), pltpu.SemaphoreType.DMA((8, 2))],
+        + [pl.BlockSpec(memory_space=pl.ANY)] * (count + 2 + (stage > 0)),
+        out_specs=pl.BlockSpec(memory_space=pl.ANY),
+        scratch_shapes=[
+            pltpu.VMEM((GROUP, count * WIDE), BF),
+            pltpu.VMEM((2, count * WIDE, 6 * HD), BF),
+            pltpu.VMEM(share, F32),
+            pltpu.VMEM(message if last else (8, 16, HD), BF),
+            pltpu.SemaphoreType.DMA((3 * count + 2,)),
+            pltpu.SemaphoreType.DMA((8,)),
+        ],
         cost_estimate=pl.CostEstimate(
-            flops=GROUP * CHANS * 12 * HD, bytes_accessed=CHANS * 12 * HD, transcendentals=0
+            flops=2 * GROUP * count * WIDE * 12 * HD, bytes_accessed=count * WIDE * 24 * HD, transcendentals=0
         ),
         compiler_params=params(),
-        name="project_last" if final else "project_first",
-    )(at, *blocks, own, sib, *([before] * final))
+        name="project_%d" % stage,
+    )(at, *blocks, own, sib, *([before] if stage else []))
 
 
 SCALE = math.log2(math.e) / math.sqrt(HD)
 EXTRA = 16
-KEYS = 2 * GROUP
-QUERIES = ASKED
-
-
-PAIR = 2 * QUERIES
+SPAN = 2 * GROUP
+KEYS = 2 * SPAN
+PAIR = 2 * ASKED
 ROOM = 80.0
 REACH = 170.0
 
@@ -302,101 +323,99 @@
     own_hbm, sib_hbm, out_ref, k_s, v_s, q_s, acc_s, sems = refs
     my_yl, my_c = at_ref[2], at_ref[5]
 
-    def fetch(group):
+    def fetch(k):
         copies = []
 
         def add(source, target):
-            copies.append(pltpu.make_async_copy(source, target, sems.at[group, len(copies)]))
-
-        for n, source in enumerate((own_hbm, sib_hbm)):
-            add(source.at[group, pl.ds(0, GROUP)], k_s.at[group, pl.ds(n * GROUP, GROUP)])
-            for tile in range(GROUP // HD):
-                add(
-                    source.at[group, pl.ds(GROUP + tile * HD, HD)],
-                    v_s.at[group, pl.ds(0, HD), pl.ds(n * GROUP + tile * HD, HD)],
-                )
-            if n == 0:
-                add(source.at[group, pl.ds(2 * GROUP, ASKED)], q_s.at[group])
+            copies.append(pltpu.make_async_copy(source, target, sems.at[k, len(copies)]))
+
+        for n in range(2):
+            for side, source in enumerate((own_hbm, sib_hbm)):
+                here = source.at[2 * k + n]
+                first = n * SPAN + side * GROUP
+                add(here.at[pl.ds(0, GROUP)], k_s.at[k, pl.ds(first, GROUP)])
+                for tile in range(GROUP // HD):
+                    add(
+                        here.at[pl.ds(GROUP + tile * HD, HD)],
+                        v_s.at[k, pl.ds(0, HD), pl.ds(first + tile * HD, HD)],
+                    )
+                if side == 0:
+                    add(here.at[pl.ds(2 * GROUP, ASKED)], q_s.at[k, pl.ds(n * ASKED, ASKED)])
         return copies
 
-    for group in range(8):
-        for copy in fetch(group):
+    for k in range(4):
+        for copy in fetch(k):
             copy.start()
-    for group in range(8):
-        v_s[group, HD:] = jnp.ones((EXTRA, KEYS), BF)
+    for k in range(4):
+        v_s[k, HD:] = jnp.ones((EXTRA, KEYS), BF)
 
     row = lax.broadcasted_iota(jnp.int32, (KEYS, 1), 0)
     col = lax.broadcasted_iota(jnp.int32, (1, PAIR), 1)
-    key_pos = ((row >> 6) & 7) * 128 + (my_c ^ (row >> 9)) * ROWS + (row & 63)
+    key_pos = (
+        (row >> 10) * 1024 + ((row >> 6) & 7) * 128 + (my_c ^ ((row >> 9) & 1)) * ROWS + (row & 63)
+    )
     query_pos = (col >> 8) * 1024 + ((col >> 5) & 7) * 128 + my_c * ROWS + my_yl * PART + (col & 31)
 
     def nt(a, b):
         return lax.dot_general(a, b, (((1,), (1,)), ((), ())), preferred_element_type=F32)
 
-    def score(group, queries, which):
-        s = nt(k_s[group], queries)
-        if which is not None:
-            s = jnp.where(key_pos + which * 1024 <= query_pos, s, -1e30)
-        return s
-
     def pair(k, tallest):
-        groups = (2 * k, 2 * k + 1)
-        for group in groups:
-            for copy in fetch(group):
-                copy.wait()
-        queries = jnp.concatenate([q_s[group] for group in groups], axis=0)
+        for copy in fetch(k):
+            copy.wait()
+        queries = q_s[k]
         itself = jnp.concatenate(
             [
-                k_s[group, pl.ds(pl.multiple_of(shard * ROWS + my_yl * PART, PART), PART)]
-                for group in groups
+                k_s[k, pl.ds(pl.multiple_of(n * SPAN + shard * ROWS + my_yl * PART, PART), PART)]
+                for n in range(2)
                 for shard in range(8)
             ],
             axis=0,
         )
         ones = jnp.ones((16, HD), BF)
-        for group in groups:
-            square = nt(ones, jnp.square(k_s[group].astype(F32)).astype(BF))
-            tallest = jnp.maximum(tallest, jnp.max(square[:8], axis=1, keepdims=True))
+        square = nt(ones, jnp.square(k_s[k].astype(F32)).astype(BF))
+        tallest = jnp.maximum(tallest, jnp.max(square[:8], axis=1, keepdims=True))
         size = nt(ones, jnp.square(queries.astype(F32)).astype(BF))[:1]
         bound = jnp.sqrt(size * tallest[:1]) * (SCALE * 1.02)
         product = (queries.astype(F32) * itself.astype(F32)).astype(BF)
         own = nt(ones, product)[:1] * SCALE
         safe = jnp.max(bound * 1.01 - own) <= REACH
-        acc_s[...] = jnp.zeros(acc_s.shape, F32)
+
+        def score(j, masked):
+            s = nt(k_s[j], queries)
+            return jnp.where(key_pos <= query_pos, s, -1e30) if masked else s
 
         @pl.when(safe)
         def _():
             offset = bound - ROOM
 
-            def visit(group, which=None):
-                weight = jnp.exp2(score(group, queries, which) * SCALE - offset).astype(BF)
-                acc_s[...] += dot(v_s[group], weight)
-
-            visit(groups[0], 0)
-            visit(groups[1], 1)
-
-            @pl.loop(0, 2 * k)
-            def _(group):
-                visit(group)
+            def visit(j, masked=False):
+                weight = jnp.exp2(score(j, masked) * SCALE - offset).astype(BF)
+                return dot(v_s[j], weight)
+
+            acc_s[...] = visit(k, True)
+
+            @pl.loop(0, k)
+            def _(j):
+                acc_s[...] += visit(j)
 
         @pl.when(jnp.logical_not(safe))
         def _():
-            def visit(group, best, which=None):
-                s = score(group, queries, which)
+            def visit(j, best, masked=False):
+                s = score(j, masked)
                 new = jnp.maximum(best, jnp.max(s, axis=0, keepdims=True))
                 weight = jnp.exp2((s - new) * SCALE).astype(BF)
-                acc_s[...] = acc_s[...] * jnp.exp2((best - new) * SCALE) + dot(v_s[group], weight)
+                acc_s[...] = acc_s[...] * jnp.exp2((best - new) * SCALE) + dot(v_s[j], weight)
                 return new
 
-            best = visit(groups[0], jnp.full((1, PAIR), -1e30, F32), 0)
-            best = visit(groups[1], best, 1)
-            lax.fori_loop(0, 2 * k, visit, best)
+            acc_s[...] = jnp.zeros(acc_s.shape, F32)
+            best = visit(k, jnp.full((1, PAIR), -1e30, F32), True)
+            lax.fori_loop(0, k, visit, best)
 
         out = (acc_s[:HD] / acc_s[HD : HD + 1]).T.astype(BF)
-        for n, group in enumerate(groups):
+        for n in range(2):
             for shard in range(8):
-                first = n * QUERIES + shard * PART
-                out_ref[group * 8 + shard] = out[first : first + PART]
+                first = n * ASKED + shard * PART
+                out_ref[(2 * k + n) * 8 + shard] = out[first : first + PART]
         return tallest
 
     lax.fori_loop(0, 4, pair, jnp.zeros((8, 1), F32))
@@ -409,11 +428,11 @@
         in_specs=[pl.BlockSpec(memory_space=pltpu.SMEM)] + [pl.BlockSpec(memory_space=pl.ANY)] * 2,
         out_specs=whole((64, PART, HD)),
         scratch_shapes=[
-            pltpu.VMEM((8, KEYS, HD), BF),
-            pltpu.VMEM((8, HD + EXTRA, KEYS), BF),
-            pltpu.VMEM((8, QUERIES, HD), BF),
+            pltpu.VMEM((4, KEYS, HD), BF),
+            pltpu.VMEM((4, HD + EXTRA, KEYS), BF),
+            pltpu.VMEM((4, PAIR, HD), BF),
             pltpu.VMEM((HD + EXTRA, PAIR), F32),
-            pltpu.SemaphoreType.DMA((8, 11)),
+            pltpu.SemaphoreType.DMA((4, 22)),
         ],
         compiler_params=params(),
         name="attend",
@@ -481,11 +500,12 @@
         else:
             blocks[half, z, xh] = flip(kept_z[z], xh=1) if xh else kept_z[z]
 
-    share = project(at, [blocks[spot] for spot in EARLY], own_weight, sib_weight)
-    messages = project(at, [blocks[spot] for spot in LATE], own_weight, sib_weight, share)
+    share = None
+    for stage, spots in enumerate(STAGES):
+        share = project(stage, at, [blocks[spot] for spot in spots], own_weight, sib_weight, share)
     mixed = collect(at, [blocks[spot] for spot in SPOTS])
 
-    own = lax.all_to_all(messages, ("xl", "yh", "yl"), split_axis=0, concat_axis=0, tiled=True)
+    own = lax.all_to_all(share, ("xl", "yh", "yl"), split_axis=0, concat_axis=0, tiled=True)
     sib = flip(own, c=1)
     heads = attend(at, own, sib)
 

time: 208 us -> 203 us (0.976)
  Pallas kernels: 65.4 us -> 59.5 us
    pallas_call x1, Pallas kernels: 26.4 us -> 23.7 us  [attend(): pl.pallas_call(attend_kernel, out_shape=jax.ShapeDtypeStruct((64, PART, H...]
  transfers between devices with their start and end apart: 20 -> 20, of which waited for: 9 -> 9; matrix products, arithmetic and copies ran while one was open for 7% -> 8% of each run, Pallas kernels for 12% -> 12%
where the time goes in v4:
time: 203 us; the launch traced here: 202 us
  Pallas kernels  59.5 us (29%)
  blocking collectives  49.2 us (24%)
  starting transfers between devices  38.9 us (19%)
  waiting for transfers between devices  34.4 us (17%)
  local copies, waits for them, and re-layouts  18.7 us (9%)
    all_to_all x1, blocking collectives, per_device(): lax.all_to_all(share, ('xl', 'yh', 'yl'), split_axis=0, concat_axis=0, ti...  35.2 us
    pallas_call x1, Pallas kernels, attend(): pl.pallas_call(attend_kernel, out_shape=jax.ShapeDtypeStruct((64, PART, H...  23.7 us
    pallas_call x2, Pallas kernels, project(): pl.pallas_call(functools.partial(project_kernel, stage), out_shape=jax.Sh...  18.9 us
    ppermute x17, starting transfers between devices, shift(): return lax.ppermute(x, NAMES, pairs)  18.4 us
    ppermute x17, waiting for transfers between devices, shift(): return lax.ppermute(x, NAMES, pairs)  17.5 us
    unnamed x38, local copies, waits for them, and re-layouts  14.7 us
    all_to_all x1, blocking collectives, per_device(): lax.all_to_all(filtered, ('xl', 'yh', 'yl'), split_axis=0, concat_axis=0,...  13.9 us
    all_to_all x1, starting transfers between devices, per_device(): lax.all_to_all(packed, NAMES, split_axis=0, concat_axis=0, tiled=True)  11.2 us
  transfers between devices with their start and end apart: 20, of which 9 were waited for; matrix products, arithmetic and copies ran while one was open for 8% of the time, Pallas kernels for 12%

profile of v4, /device:TPU:0, one launch (start us, length us, event | category | flops | bytes accessed | tf_op | source)
XLA Modules:
  0.0 201.7 jit_solution(9246406181025361780)
XLA Ops:
  0.6 0.1 collective-permute-start
  0.7 3.0 %pack.1 = (bf16[8,16,2,16,128]{4,3,2,1,0:T(8,128)(2,1)}, bf16[16,64,256]{2,1,0:T(8,128)(2,1)}) custom-call(bf16[64,4096]{1,0:T(8,128)(2,1)} %key_ref.1, bf16[64,4096]{1,0:T(8,128)(2,1)} %value_ref.1, bf16[64,4096]{1,0:T(8,128)(2,1)} %taps_ref.1, bf16[64,4096]{1,0:T(8,128)(2,1)} %gate_ref.1), custom_call_target="tpu_custom_call" | custom-call | tf_op jit(solution)/shard_map/pack/pallas_call | solution.py:87
  3.7 11.2 %all-to-all-start = ((bf16[128,2,16,128]{3,2,1,0:T(8,128)(2,1)}), bf16[128,2,16,128]{3,2,1,0:T(8,128)(2,1)S(1)}, u32[]{:S(2)}, u32[]{:S(2)}) async-start(bf16[128,2,16,128]{3,2,1,0:T(8,128)(2,1)} %bitcast.25), calls=%async_computation | async-start | bytes 2097152 | tf_op jit(solution)/shard_map/all_to_all | solution.py:473
  15.0 0.8 reshape.31
  15.9 0.1 copy.16
  16.0 0.1 broadcast_in_dim.3
  16.0 0.7 reshape.32.gain_ref
  16.7 6.5 %copy.18 = bf16[512,8,2,384]{3,1,2,0:T(8,128)(2,1)} copy(bf16[512,8,2,384]{3,2,1,0:T(2,128)(2,1)} %bitcast.22) | data formatting | bytes 12582912
  23.2 0.6 stack.27.at_ref
  23.9 0.0 collective-permute-done
  23.9 6.5 %copy.19 = bf16[512,8,2,384]{3,1,2,0:T(8,128)(2,1)} copy(bf16[512,8,2,384]{3,2,1,0:T(2,128)(2,1)} %bitcast.16) | data formatting | bytes 12582912
  30.4 2.8 %all-to-all-done.recv_ref = bf16[128,2,16,128]{3,2,1,0:T(8,128)(2,1)S(1)} async-done(((bf16[128,2,16,128]{3,2,1,0:T(8,128)(2,1)}), bf16[128,2,16,128]{3,2,1,0:T(8,128)(2,1)S(1)}, u32[]{:S(2)}, u32[]{:S(2)}) %all-to-all-start) | async-done | bytes 1048608 | tf_op jit(solution)/shard_map/all_to_all | solution.py:473
  33.2 4.2 %all-to-all-start.1 = ((bf16[16,64,256]{2,1,0:T(8,128)(2,1)}), bf16[16,64,256]{2,1,0:T(8,128)(2,1)S(1)}, u32[]{:S(2)}, u32[]{:S(2)}) async-start(bf16[16,64,256]{2,1,0:T(8,128)(2,1)} %get-tuple-element.19), calls=%async_computation.1 | async-start | bytes 1048576 | tf_op jit(solution)/shard_map/all_to_all | solution.py:484
  37.4 9.2 %convolve.1 = bf16[128,16,128]{2,1,0:T(8,128)(2,1)} custom-call(bf16[128,2,16,128]{3,2,1,0:T(8,128)(2,1)} %copy-done.1, f32[16,128]{1,0:T(8,128)} %reshape.32.gain_ref, bf16[256,256]{1,0:T(8,128)(2,1)} %constant.71.clone.w1, f32[128,128]{1,0:T(8,128)} %constant.72.clone.tc_ref, f32[128,128]{1,0:T(8,128)} %constant.73.clone.ts_ref, ...), custom_call_target="tpu_custom_call" | custom-call | tf_op jit(solution)/shard_map/convolve/pallas_call | solution.py:156
  46.6 3.2 %all-to-all-done.1.gate_ref = bf16[16,64,256]{2,1,0:T(8,128)(2,1)S(1)} async-done(((bf16[16,64,256]{2,1,0:T(8,128)(2,1)}), bf16[16,64,256]{2,1,0:T(8,128)(2,1)S(1)}, u32[]{:S(2)}, u32[]{:S(2)}) %all-to-all-start.1) | async-done | bytes 524320 | tf_op jit(solution)/shard_map/all_to_all | solution.py:484
  49.8 13.9 %all_to_all.25 = bf16[128,16,128]{2,1,0:T(8,128)(2,1)} all-to-all(bf16[128,16,128]{2,1,0:T(8,128)(2,1)} %convolve.1), channel_id=1, replica_groups=mesh['xl'=2,'yh'=2,'yl'=2,'z'=4,'xh'=2,'c'=2] {'xl','yh','yl'}, dimensions={0} | all-to-all | bytes 1048576 | tf_op jit(solution)/shard_map/all_to_all | solution.py:486
  63.7 2.2 %apply_gate.1 = (bf16[512,256]{1,0:T(8,128)(2,1)}, bf16[512,256]{1,0:T(8,128)(2,1)}) custom-call(s32[6]{0:T(128)} %stack.27.at_ref, bf16[8,16,16,128]{3,2,1,0:T(8,128)(2,1)} %bitcast.24, bf16[16,64,256]{2,1,0:T(8,128)(2,1)} %copy-done.2), custom_call_target="tpu_custom_call" | custom-call | tf_op jit(solution)/shard_map/apply_gate/pallas_call | solution.py:193
  65.9 0.1 collective-permute-start.13
  65.9 3.2 %collective-permute-start.4 = (bf16[512,256]{1,0:T(8,128)(2,1)}, bf16[512,256]{1,0:T(8,128)(2,1)S(1)}, u32[]{:S(2)}, u32[]{:S(2)}) collective-permute-start(bf16[512,256]{1,0:T(8,128)(2,1)} %get-tuple-element.22.refs_0_), channel_id=1, source_target_pairs={{0,12},{1,13},{2,14},{3,15},{4,0},{5,1},{6,2},{7,3},{8,4},{9,5},{1... | collective-permute-start | bytes 786440 | tf_op jit(solution)/shard_map/ppermute | solution.py:449
  69.1 1.9 collective-permute-start.2
  71.1 1.6 collective-permute-start.3
  72.6 3.5 %collective-permute-done.13.refs_12_.refs_4_ = bf16[512,256]{1,0:T(8,128)(2,1)S(1)} collective-permute-done((bf16[512,256]{1,0:T(8,128)(2,1)}, bf16[512,256]{1,0:T(8,128)(2,1)S(1)}, u32[]{:S(2)}, u32[]{:S(2)}) %collective-permute-start.13) | collective-permute-done | bytes 262176 | tf_op jit(solution)/shard_map/ppermute | solution.py:449
  76.1 3.2 %collective-permute-start.14 = (bf16[512,256]{1,0:T(8,128)(2,1)S(1)}, bf16[512,256]{1,0:T(8,128)(2,1)S(1)}, u32[]{:S(2)}, u32[]{:S(2)}) collective-permute-start(bf16[512,256]{1,0:T(8,128)(2,1)S(1)} %collective-permute-done.13.refs_12_.refs_4_), channel_id=1, source_target_pairs={{0,2},{1,3},{2,0},{3,1},{4,6},{5,7},{6,4},{7,5},{8,10},{9,11},{10,... | collective-permute-start | bytes 786440 | tf_op jit(solution)/shard_map/ppermute | solution.py:449
  79.3 0.7 collective-permute-done.2.refs_2_
  80.0 0.9 collective-permute-start.8
  80.9 4.7 %collective-permute-done.3.refs_3_.refs_6_ = bf16[512,256]{1,0:T(8,128)(2,1)S(1)} collective-permute-done((bf16[512,256]{1,0:T(8,128)(2,1)S(1)}, bf16[512,256]{1,0:T(8,128)(2,1)S(1)}, u32[]{:S(2)}, u32[]{:S(2)}) %collective-permute-start.3) | collective-permute-done | bytes 262176 | tf_op jit(solution)/shard_map/ppermute | solution.py:449
  85.6 2.9 %collective-permute-start.6 = (bf16[512,256]{1,0:T(8,128)(2,1)S(1)}, bf16[512,256]{1,0:T(8,128)(2,1)S(1)}, u32[]{:S(2)}, u32[]{:S(2)}) collective-permute-start(bf16[512,256]{1,0:T(8,128)(2,1)S(1)} %collective-permute-done.4.refs_4_.refs_3_), channel_id=1, source_target_pairs={{0,2},{1,3},{2,0},{3,1},{4,6},{5,7},{6,4},{7,5},{8,10},{9,11},{10,... | collective-permute-start | bytes 786440 | tf_op jit(solution)/shard_map/ppermute | solution.py:449
  88.5 1.1 collective-permute-start.15
  89.6 1.6 collective-permute-done.14.refs_14_.refs_6_
  91.3 2.0 %collective-permute-start.11 = (bf16[512,256]{1,0:T(8,128)(2,1)S(1)}, bf16[512,256]{1,0:T(8,128)(2,1)S(1)}, u32[]{:S(2)}, u32[]{:S(2)}) collective-permute-start(bf16[512,256]{1,0:T(8,128)(2,1)S(1)} %collective-permute-done.8.refs_8_.refs_5_), channel_id=1, source_target_pairs={{0,2},{1,3},{2,0},{3,1},{4,6},{5,7},{6,4},{7,5},{8,10},{9,11},{10,... | collective-permute-start | bytes 786440 | tf_op jit(solution)/shard_map/ppermute | solution.py:449
  93.3 1.9 collective-permute-done.7.refs_7_.refs_1_
  95.2 1.5 collective-permute-start.12
  96.7 9.2 %project_0.1.refs_10_ = f32[2,512,768]{2,1,0:T(8,128)} custom-call(s32[6]{0:T(128)} %stack.27.at_ref, bf16[512,256]{1,0:T(8,128)(2,1)} %get-tuple-element.22.refs_0_, bf16[512,256]{1,0:T(8,128)(2,1)} %copy-done.3, bf16[512,256]{1,0:T(8,128)(2,1)} %copy-done.6, bf16[512,256]{1,0:T(8,128)(2,1)} %copy-done.5, bf16[512,256]{1,0:T(8,128)(2,1)} %copy-done.4, ...), custom_call_target="tpu_custom_call" | custom-call | flops 3221225472 | bytes 6291456 | tf_op jit(solution)/shard_map/project_0/pallas_call | solution.py:291
  106.1 0.6 copy-done.13
  106.7 0.1 copy-done.15
  106.8 0.1 copy-done.14
  106.9 0.1 copy-done.16
  107.0 0.7 copy-done.17
  107.7 9.7 %project_1.1 = bf16[8,1280,128]{2,1,0:T(8,128)(2,1)} custom-call(s32[6]{0:T(128)} %stack.27.at_ref, bf16[512,256]{1,0:T(8,128)(2,1)} %copy-done.13, bf16[512,256]{1,0:T(8,128)(2,1)} %copy-done.12, bf16[512,256]{1,0:T(8,128)(2,1)} %copy-done.15, bf16[512,256]{1,0:T(8,128)(2,1)} %copy-done.16, bf16[512,256]{1,0:T(8,128)(2,1)} %copy-done.17, ...), custom_call_target="tpu_custom_call" | custom-call | flops 3221225472 | bytes 6291456 | tf_op jit(solution)/shard_map/project_1/pallas_call | solution.py:291
  117.4 35.2 %all_to_all.26.refs_0_ = bf16[8,1280,128]{2,1,0:T(8,128)(2,1)S(1)} all-to-all(bf16[8,1280,128]{2,1,0:T(8,128)(2,1)} %project_1.1), channel_id=1, replica_groups=mesh['xl'=2,'yh'=2,'yl'=2,'z'=4,'xh'=2,'c'=2] {'xl','yh','yl'}, dimensions={0} | all-to-all | bytes 5242880 | tf_op jit(solution)/shard_map/all_to_all | solution.py:508
  152.6 0.0 collective-permute-start.16
  152.6 5.0 %collective-permute-done.16.refs_1_ = bf16[8,1280,128]{2,1,0:T(8,128)(2,1)} collective-permute-done((bf16[8,1280,128]{2,1,0:T(8,128)(2,1)S(1)}, bf16[8,1280,128]{2,1,0:T(8,128)(2,1)}, u32[]{:S(2)}, u32[]{:S(2)}) %collective-permute-start.16) | collective-permute-done | bytes 2621472 | tf_op jit(solution)/shard_map/ppermute | solution.py:449
  157.7 23.7 %attend.1 = bf16[64,32,128]{2,1,0:T(8,128)(2,1)} custom-call(s32[6]{0:T(128)} %stack.27.at_ref, bf16[8,1280,128]{2,1,0:T(8,128)(2,1)} %copy-done, bf16[8,1280,128]{2,1,0:T(8,128)(2,1)} %collective-permute-done.16.refs_1_), custom_call_target="tpu_custom_call" | custom-call | tf_op jit(solution)/shard_map/attend/pallas_call | solution.py:425
  181.3 5.0 %all-to-all-start.4 = ((bf16[64,32,128]{2,1,0:T(8,128)(2,1)}), bf16[64,32,128]{2,1,0:T(8,128)(2,1)S(1)}, u32[]{:S(2)}, u32[]{:S(2)}) async-start(bf16[64,32,128]{2,1,0:T(8,128)(2,1)} %attend.1), calls=%async_computation.4 | async-start | bytes 1048576 | tf_op jit(solution)/shard_map/all_to_all | solution.py:512
  186.4 2.6 %collect.1 = bf16[64,4096]{1,0:T(8,128)(2,1)} custom-call(s32[6]{0:T(128)} %stack.27.at_ref, bf16[512,256]{1,0:T(8,128)(2,1)} %get-tuple-element.22.refs_0_, bf16[512,256]{1,0:T(8,128)(2,1)} %copy-done.3, bf16[512,256]{1,0:T(8,128)(2,1)} %copy-done.6, bf16[512,256]{1,0:T(8,128)(2,1)} %copy-done.7, bf16[512,256]{1,0:T(8,128)(2,1)} %copy-done.5, ...), custom_call_target="tpu_custom_call" | custom-call | tf_op jit(solution)/shard_map/collect/pallas_call | solution.py:217
  189.0 10.9 %all-to-all-done.4 = bf16[64,32,128]{2,1,0:T(8,128)(2,1)S(1)} async-done(((bf16[64,32,128]{2,1,0:T(8,128)(2,1)}), bf16[64,32,128]{2,1,0:T(8,128)(2,1)S(1)}, u32[]{:S(2)}, u32[]{:S(2)}) %all-to-all-start.4) | async-done | bytes 524320 | tf_op jit(solution)/shard_map/all_to_all | solution.py:512
  199.9 0.5 copy.17
  200.5 1.2 reshape.35
  (47 shorter events, 0.1 us)
Async XLA Ops:
  0.6 23.2 %collective-permute-start = (bf16[4096,2,384]{2,1,0:T(2,128)(2,1)}, bf16[4096,2,384]{2,1,0:T(2,128)(2,1)}, u32[]{:S(2)}, u32[]{:S(2)}) collective-permute-start(bf16[4096,2,384]{2,1,0:T(2,128)(2,1)} %param.17), channel_id=1, source_target_pairs={{0,1},{1,0},{2,3},{3,2},{4,5},{5,4},{6,7},{7,6},{8,9},{9,8},{10,11... | collective-permute-start | bytes 18874376 | tf_op jit(solution)/shard_map/ppermute | solution.py:449
  3.7 29.5 %all-to-all-start = ((bf16[128,2,16,128]{3,2,1,0:T(8,128)(2,1)}), bf16[128,2,16,128]{3,2,1,0:T(8,128)(2,1)S(1)}, u32[]{:S(2)}, u32[]{:S(2)}) async-start(bf16[128,2,16,128]{3,2,1,0:T(8,128)(2,1)} %bitcast.25), calls=%async_computation | async-start | bytes 2097152 | tf_op jit(solution)/shard_map/all_to_all | solution.py:473
  33.2 4.2 %copy-start.1 = (bf16[128,2,16,128]{3,2,1,0:T(8,128)(2,1)}, bf16[128,2,16,128]{3,2,1,0:T(8,128)(2,1)S(1)}, u32[]{:S(2)}) copy-start(bf16[128,2,16,128]{3,2,1,0:T(8,128)(2,1)S(1)} %all-to-all-done.recv_ref) | copy-start | bytes 3145732
  33.2 16.5 %all-to-all-start.1 = ((bf16[16,64,256]{2,1,0:T(8,128)(2,1)}), bf16[16,64,256]{2,1,0:T(8,128)(2,1)S(1)}, u32[]{:S(2)}, u32[]{:S(2)}) async-start(bf16[16,64,256]{2,1,0:T(8,128)(2,1)} %get-tuple-element.19), calls=%async_computation.1 | async-start | bytes 1048576 | tf_op jit(solution)/shard_map/all_to_all | solution.py:484
  49.8 13.9 %copy-start.2 = (bf16[16,64,256]{2,1,0:T(8,128)(2,1)}, bf16[16,64,256]{2,1,0:T(8,128)(2,1)S(1)}, u32[]{:S(2)}) copy-start(bf16[16,64,256]{2,1,0:T(8,128)(2,1)S(1)} %all-to-all-done.1.gate_ref) | copy-start | bytes 1572868
  65.9 5.2 %collective-permute-start.1 = (bf16[512,256]{1,0:T(8,128)(2,1)}, bf16[512,256]{1,0:T(8,128)(2,1)S(1)}, u32[]{:S(2)}, u32[]{:S(2)}) collective-permute-start(bf16[512,256]{1,0:T(8,128)(2,1)} %get-tuple-element.23), channel_id=1, source_target_pairs={{0,1},{1,0},{2,3},{3,2},{4,5},{5,4},{6,7},{7,6},{8,9},{9,8},{10,11... | collective-permute-start | bytes 786440 | tf_op jit(solution)/shard_map/ppermute | solution.py:449
  65.9 10.2 %collective-permute-start.13 = (bf16[512,256]{1,0:T(8,128)(2,1)}, bf16[512,256]{1,0:T(8,128)(2,1)S(1)}, u32[]{:S(2)}, u32[]{:S(2)}) collective-permute-start(bf16[512,256]{1,0:T(8,128)(2,1)} %get-tuple-element.22.refs_0_), channel_id=1, source_target_pairs={{0,4},{1,5},{2,6},{3,7},{4,8},{5,9},{6,10},{7,11},{8,12},{9,13},{1... | collective-permute-start | bytes 786440 | tf_op jit(solution)/shard_map/ppermute | solution.py:449
  65.9 10.2 %collective-permute-start.4 = (bf16[512,256]{1,0:T(8,128)(2,1)}, bf16[512,256]{1,0:T(8,128)(2,1)S(1)}, u32[]{:S(2)}, u32[]{:S(2)}) collective-permute-start(bf16[512,256]{1,0:T(8,128)(2,1)} %get-tuple-element.22.refs_0_), channel_id=1, source_target_pairs={{0,12},{1,13},{2,14},{3,15},{4,0},{5,1},{6,2},{7,3},{8,4},{9,5},{1... | collective-permute-start | bytes 786440 | tf_op jit(solution)/shard_map/ppermute | solution.py:449
  69.1 10.9 %collective-permute-start.2 = (bf16[512,256]{1,0:T(8,128)(2,1)}, bf16[512,256]{1,0:T(8,128)(2,1)S(1)}, u32[]{:S(2)}, u32[]{:S(2)}) collective-permute-start(bf16[512,256]{1,0:T(8,128)(2,1)} %get-tuple-element.22.refs_0_), channel_id=1, source_target_pairs={{0,2},{1,3},{2,0},{3,1},{4,6},{5,7},{6,4},{7,5},{8,10},{9,11},{10,... | collective-permute-start | bytes 786440 | tf_op jit(solution)/shard_map/ppermute | solution.py:449
  71.1 25.6 %copy-start.3 = (bf16[512,256]{1,0:T(8,128)(2,1)}, bf16[512,256]{1,0:T(8,128)(2,1)S(1)}, u32[]{:S(2)}) copy-start(bf16[512,256]{1,0:T(8,128)(2,1)S(1)} %collective-permute-done.1.refs_1_) | copy-start | bytes 786436
  71.1 14.6 %collective-permute-start.3 = (bf16[512,256]{1,0:T(8,128)(2,1)S(1)}, bf16[512,256]{1,0:T(8,128)(2,1)S(1)}, u32[]{:S(2)}, u32[]{:S(2)}) collective-permute-start(bf16[512,256]{1,0:T(8,128)(2,1)S(1)} %collective-permute-done.1.refs_1_), channel_id=1, source_target_pairs={{0,2},{1,3},{2,0},{3,1},{4,6},{5,7},{6,4},{7,5},{8,10},{9,11},{10,... | collective-permute-start | bytes 786440 | tf_op jit(solution)/shard_map/ppermute | solution.py:449
  72.6 13.0 %collective-permute-start.9 = (bf16[512,256]{1,0:T(8,128)(2,1)S(1)}, bf16[512,256]{1,0:T(8,128)(2,1)S(1)}, u32[]{:S(2)}, u32[]{:S(2)}) collective-permute-start(bf16[512,256]{1,0:T(8,128)(2,1)S(1)} %collective-permute-done.1.refs_1_), channel_id=1, source_target_pairs={{0,4},{1,5},{2,6},{3,7},{4,8},{5,9},{6,10},{7,11},{8,12},{9,13},{1... | collective-permute-start | bytes 786440 | tf_op jit(solution)/shard_map/ppermute | solution.py:449
  76.1 20.6 %copy-start.4 = (bf16[512,256]{1,0:T(8,128)(2,1)}, bf16[512,256]{1,0:T(8,128)(2,1)S(1)}, u32[]{:S(2)}) copy-start(bf16[512,256]{1,0:T(8,128)(2,1)S(1)} %collective-permute-done.13.refs_12_.refs_4_) | copy-start | bytes 786436
  76.1 12.4 %collective-permute-start.5 = (bf16[512,256]{1,0:T(8,128)(2,1)S(1)}, bf16[512,256]{1,0:T(8,128)(2,1)S(1)}, u32[]{:S(2)}, u32[]{:S(2)}) collective-permute-start(bf16[512,256]{1,0:T(8,128)(2,1)S(1)} %collective-permute-done.1.refs_1_), channel_id=1, source_target_pairs={{0,12},{1,13},{2,14},{3,15},{4,0},{5,1},{6,2},{7,3},{8,4},{9,5},{1... | collective-permute-start | bytes 786440 | tf_op jit(solution)/shard_map/ppermute | solution.py:449
  76.1 20.6 %copy-start.5 = (bf16[512,256]{1,0:T(8,128)(2,1)}, bf16[512,256]{1,0:T(8,128)(2,1)S(1)}, u32[]{:S(2)}) copy-start(bf16[512,256]{1,0:T(8,128)(2,1)S(1)} %collective-permute-done.4.refs_4_.refs_3_) | copy-start | bytes 786436
  76.1 15.1 %collective-permute-start.14 = (bf16[512,256]{1,0:T(8,128)(2,1)S(1)}, bf16[512,256]{1,0:T(8,128)(2,1)S(1)}, u32[]{:S(2)}, u32[]{:S(2)}) collective-permute-start(bf16[512,256]{1,0:T(8,128)(2,1)S(1)} %collective-permute-done.13.refs_12_.refs_4_), channel_id=1, source_target_pairs={{0,2},{1,3},{2,0},{3,1},{4,6},{5,7},{6,4},{7,5},{8,10},{9,11},{10,... | collective-permute-start | bytes 786440 | tf_op jit(solution)/shard_map/ppermute | solution.py:449
  80.0 16.7 %copy-start.6 = (bf16[512,256]{1,0:T(8,128)(2,1)}, bf16[512,256]{1,0:T(8,128)(2,1)S(1)}, u32[]{:S(2)}) copy-start(bf16[512,256]{1,0:T(8,128)(2,1)S(1)} %collective-permute-done.2.refs_2_) | copy-start | bytes 786436
  80.0 11.2 %collective-permute-start.8 = (bf16[512,256]{1,0:T(8,128)(2,1)S(1)}, bf16[512,256]{1,0:T(8,128)(2,1)S(1)}, u32[]{:S(2)}, u32[]{:S(2)}) collective-permute-start(bf16[512,256]{1,0:T(8,128)(2,1)S(1)} %collective-permute-done.4.refs_4_.refs_3_), channel_id=1, source_target_pairs={{0,12},{1,13},{2,14},{3,15},{4,0},{5,1},{6,2},{7,3},{8,4},{9,5},{1... | collective-permute-start | bytes 786440 | tf_op jit(solution)/shard_map/ppermute | solution.py:449
  85.6 11.1 %copy-start.7 = (bf16[512,256]{1,0:T(8,128)(2,1)}, bf16[512,256]{1,0:T(8,128)(2,1)S(1)}, u32[]{:S(2)}) copy-start(bf16[512,256]{1,0:T(8,128)(2,1)S(1)} %collective-permute-done.3.refs_3_.refs_6_) | copy-start | bytes 786436
  85.6 9.6 %collective-permute-start.7 = (bf16[512,256]{1,0:T(8,128)(2,1)S(1)}, bf16[512,256]{1,0:T(8,128)(2,1)S(1)}, u32[]{:S(2)}, u32[]{:S(2)}) collective-permute-start(bf16[512,256]{1,0:T(8,128)(2,1)S(1)} %collective-permute-done.3.refs_3_.refs_6_), channel_id=1, source_target_pairs={{0,12},{1,13},{2,14},{3,15},{4,0},{5,1},{6,2},{7,3},{8,4},{9,5},{1... | collective-permute-start | bytes 786440 | tf_op jit(solution)/shard_map/ppermute | solution.py:449
  85.6 20.3 %copy-start.8 = (bf16[512,256]{1,0:T(8,128)(2,1)}, bf16[512,256]{1,0:T(8,128)(2,1)S(1)}, u32[]{:S(2)}) copy-start(bf16[512,256]{1,0:T(8,128)(2,1)S(1)} %collective-permute-done.9.refs_13_.refs_5_) | copy-start | bytes 786436
  85.6 20.4 %collective-permute-start.6 = (bf16[512,256]{1,0:T(8,128)(2,1)S(1)}, bf16[512,256]{1,0:T(8,128)(2,1)S(1)}, u32[]{:S(2)}, u32[]{:S(2)}) collective-permute-start(bf16[512,256]{1,0:T(8,128)(2,1)S(1)} %collective-permute-done.4.refs_4_.refs_3_), channel_id=1, source_target_pairs={{0,2},{1,3},{2,0},{3,1},{4,6},{5,7},{6,4},{7,5},{8,10},{9,11},{10,... | collective-permute-start | bytes 786440 | tf_op jit(solution)/shard_map/ppermute | solution.py:449
  88.5 8.2 %copy-start.9 = (bf16[512,256]{1,0:T(8,128)(2,1)}, bf16[512,256]{1,0:T(8,128)(2,1)S(1)}, u32[]{:S(2)}) copy-start(bf16[512,256]{1,0:T(8,128)(2,1)S(1)} %collective-permute-done.5.refs_5_.refs_7_) | copy-start | bytes 786436
  88.5 17.5 %collective-permute-start.15 = (bf16[512,256]{1,0:T(8,128)(2,1)S(1)}, bf16[512,256]{1,0:T(8,128)(2,1)S(1)}, u32[]{:S(2)}, u32[]{:S(2)}) collective-permute-start(bf16[512,256]{1,0:T(8,128)(2,1)S(1)} %collective-permute-done.3.refs_3_.refs_6_), channel_id=1, source_target_pairs={{0,4},{1,5},{2,6},{3,7},{4,8},{5,9},{6,10},{7,11},{8,12},{9,13},{1... | collective-permute-start | bytes 786440 | tf_op jit(solution)/shard_map/ppermute | solution.py:449
  91.2 14.7 %copy-start.10 = (bf16[512,256]{1,0:T(8,128)(2,1)}, bf16[512,256]{1,0:T(8,128)(2,1)S(1)}, u32[]{:S(2)}) copy-start(bf16[512,256]{1,0:T(8,128)(2,1)S(1)} %collective-permute-done.14.refs_14_.refs_6_) | copy-start | bytes 786436
  91.2 14.8 %collective-permute-start.10 = (bf16[512,256]{1,0:T(8,128)(2,1)S(1)}, bf16[512,256]{1,0:T(8,128)(2,1)S(1)}, u32[]{:S(2)}, u32[]{:S(2)}) collective-permute-start(bf16[512,256]{1,0:T(8,128)(2,1)S(1)} %collective-permute-done.9.refs_13_.refs_5_), channel_id=1, source_target_pairs={{0,4},{1,5},{2,6},{3,7},{4,8},{5,9},{6,10},{7,11},{8,12},{9,13},{1... | collective-permute-start | bytes 786440 | tf_op jit(solution)/shard_map/ppermute | solution.py:449
  91.2 5.5 %copy-start.11 = (bf16[512,256]{1,0:T(8,128)(2,1)}, bf16[512,256]{1,0:T(8,128)(2,1)S(1)}, u32[]{:S(2)}) copy-start(bf16[512,256]{1,0:T(8,128)(2,1)S(1)} %collective-permute-done.8.refs_8_.refs_5_) | copy-start | bytes 786436
  91.3 14.8 %collective-permute-start.11 = (bf16[512,256]{1,0:T(8,128)(2,1)S(1)}, bf16[512,256]{1,0:T(8,128)(2,1)S(1)}, u32[]{:S(2)}, u32[]{:S(2)}) collective-permute-start(bf16[512,256]{1,0:T(8,128)(2,1)S(1)} %collective-permute-done.8.refs_8_.refs_5_), channel_id=1, source_target_pairs={{0,2},{1,3},{2,0},{3,1},{4,6},{5,7},{6,4},{7,5},{8,10},{9,11},{10,... | collective-permute-start | bytes 786440 | tf_op jit(solution)/shard_map/ppermute | solution.py:449
  95.2 10.8 %copy-start.12 = (bf16[512,256]{1,0:T(8,128)(2,1)}, bf16[512,256]{1,0:T(8,128)(2,1)S(1)}, u32[]{:S(2)}) copy-start(bf16[512,256]{1,0:T(8,128)(2,1)S(1)} %collective-permute-done.7.refs_7_.refs_1_) | copy-start | bytes 786436
  95.2 10.9 %collective-permute-start.12 = (bf16[512,256]{1,0:T(8,128)(2,1)S(1)}, bf16[512,256]{1,0:T(8,128)(2,1)S(1)}, u32[]{:S(2)}, u32[]{:S(2)}) collective-permute-start(bf16[512,256]{1,0:T(8,128)(2,1)S(1)} %collective-permute-done.7.refs_7_.refs_1_), channel_id=1, source_target_pairs={{0,12},{1,13},{2,14},{3,15},{4,0},{5,1},{6,2},{7,3},{8,4},{9,5},{1... | collective-permute-start | bytes 786440 | tf_op jit(solution)/shard_map/ppermute | solution.py:449
  106.0 0.7 copy-start.13
  106.0 0.8 copy-start.15
  106.0 0.9 copy-start.14
  106.1 0.9 copy-start.16
  107.0 0.7 copy-start.17
  152.6 5.0 %copy-start = (bf16[8,1280,128]{2,1,0:T(8,128)(2,1)}, bf16[8,1280,128]{2,1,0:T(8,128)(2,1)S(1)}, u32[]{:S(2)}) copy-start(bf16[8,1280,128]{2,1,0:T(8,128)(2,1)S(1)} %all_to_all.26.refs_0_) | copy-start | bytes 7864324
  152.6 5.0 %collective-permute-start.16 = (bf16[8,1280,128]{2,1,0:T(8,128)(2,1)S(1)}, bf16[8,1280,128]{2,1,0:T(8,128)(2,1)}, u32[]{:S(2)}, u32[]{:S(2)}) collective-permute-start(bf16[8,1280,128]{2,1,0:T(8,128)(2,1)S(1)} %all_to_all.26.refs_0_), channel_id=1, source_target_pairs={{0,1},{1,0},{2,3},{3,2},{4,5},{5,4},{6,7},{7,6},{8,9},{9,8},{10,11... | collective-permute-start | bytes 7864328 | tf_op jit(solution)/shard_map/ppermute | solution.py:449
  181.3 18.6 %all-to-all-start.4 = ((bf16[64,32,128]{2,1,0:T(8,128)(2,1)}), bf16[64,32,128]{2,1,0:T(8,128)(2,1)S(1)}, u32[]{:S(2)}, u32[]{:S(2)}) async-start(bf16[64,32,128]{2,1,0:T(8,128)(2,1)} %attend.1), calls=%async_computation.4 | async-start | bytes 1048576 | tf_op jit(solution)/shard_map/all_to_all | solution.py:512

commit v5 on v4

--- a/solution.py
+++ b/solution.py
@@ -171,7 +171,7 @@
 
 
 SPOTS = [(half, z, xh) for z in range(4) for xh in range(2) for half in range(2)]
-EARLY = [(0, 0, 0), (1, 0, 0), (0, 0, 1), (0, 1, 0), (0, 3, 0), (0, 2, 0), (1, 0, 1), (1, 1, 0)]
+EARLY = [(0, 0, 0), (1, 0, 0), (0, 0, 1), (0, 1, 0), (0, 3, 0), (0, 2, 0), (1, 0, 1), (1, 1, 0), (1, 3, 0), (0, 1, 1)]
 STAGES = [EARLY, [spot for spot in SPOTS if spot not in EARLY]]
 
 

time: 203 us -> 200 us (0.985)
  waiting for transfers between devices: 34.4 us -> 29.9 us
  starting transfers between devices: 38.9 us -> 42.2 us
    ppermute x17, waiting for transfers between devices: 17.5 us -> 12.3 us  [shift(): return lax.ppermute(x, NAMES, pairs)]
    ppermute x17, starting transfers between devices: 18.4 us -> 21.9 us  [shift(): return lax.ppermute(x, NAMES, pairs)]
    unnamed x38 -> x40, local copies, waits for them, and re-layouts: 14.7 us -> 14.7 us
  transfers between devices with their start and end apart: 20 -> 20, of which waited for: 9 -> 9; matrix products, arithmetic and copies ran while one was open for 8% -> 7% of each run, Pallas kernels for 12% -> 13%
where the time goes in v5:
time: 200 us; the launch traced here: 199 us
  Pallas kernels  59.6 us (30%)
  blocking collectives  48.3 us (24%)
  starting transfers between devices  42.2 us (21%)
  waiting for transfers between devices  29.9 us (15%)
  local copies, waits for them, and re-layouts  18 us (9%)
    all_to_all x1, blocking collectives, per_device(): lax.all_to_all(share, ('xl', 'yh', 'yl'), split_axis=0, concat_axis=0, ti...  34.4 us
    pallas_call x1, Pallas kernels, attend(): pl.pallas_call(attend_kernel, out_shape=jax.ShapeDtypeStruct((64, PART, H...  23.6 us
    ppermute x17, starting transfers between devices, shift(): return lax.ppermute(x, NAMES, pairs)  21.9 us
    pallas_call x2, Pallas kernels, project(): pl.pallas_call(functools.partial(project_kernel, stage), out_shape=jax.Sh...  18.9 us
    unnamed x40, local copies, waits for them, and re-layouts  14.7 us
    all_to_all x1, blocking collectives, per_device(): lax.all_to_all(filtered, ('xl', 'yh', 'yl'), split_axis=0, concat_axis=0,...  13.9 us
    ppermute x17, waiting for transfers between devices, shift(): return lax.ppermute(x, NAMES, pairs)  12.3 us
    all_to_all x1, starting transfers between devices, per_device(): lax.all_to_all(packed, NAMES, split_axis=0, concat_axis=0, tiled=True)  11.2 us
  transfers between devices with their start and end apart: 20, of which 9 were waited for; matrix products, arithmetic and copies ran while one was open for 7% of the time, Pallas kernels for 13%

profile of v5, /device:TPU:0, one launch (start us, length us, event | category | flops | bytes accessed | tf_op | source)
XLA Modules:
  0.0 199.0 jit_solution(8898123520172003518)
XLA Ops:
  0.6 0.1 collective-permute-start
  0.7 3.0 %pack.1 = (bf16[8,16,2,16,128]{4,3,2,1,0:T(8,128)(2,1)}, bf16[16,64,256]{2,1,0:T(8,128)(2,1)}) custom-call(bf16[64,4096]{1,0:T(8,128)(2,1)} %key_ref.1, bf16[64,4096]{1,0:T(8,128)(2,1)} %value_ref.1, bf16[64,4096]{1,0:T(8,128)(2,1)} %taps_ref.1, bf16[64,4096]{1,0:T(8,128)(2,1)} %gate_ref.1), custom_call_target="tpu_custom_call" | custom-call | tf_op jit(solution)/shard_map/pack/pallas_call | solution.py:87
  3.7 11.2 %all-to-all-start = ((bf16[128,2,16,128]{3,2,1,0:T(8,128)(2,1)}), bf16[128,2,16,128]{3,2,1,0:T(8,128)(2,1)S(1)}, u32[]{:S(2)}, u32[]{:S(2)}) async-start(bf16[128,2,16,128]{3,2,1,0:T(8,128)(2,1)} %bitcast.25), calls=%async_computation | async-start | bytes 2097152 | tf_op jit(solution)/shard_map/all_to_all | solution.py:473
  15.0 6.5 %copy.18 = bf16[512,8,2,384]{3,1,2,0:T(8,128)(2,1)} copy(bf16[512,8,2,384]{3,2,1,0:T(2,128)(2,1)} %bitcast.22) | data formatting | bytes 12582912
  21.6 0.1 reshape.31
  21.7 0.1 copy.16
  21.9 0.7 reshape.32.gain_ref
  22.6 0.7 stack.27.at_ref
  23.2 6.5 %copy.19 = bf16[512,8,2,384]{3,1,2,0:T(8,128)(2,1)} copy(bf16[512,8,2,384]{3,2,1,0:T(2,128)(2,1)} %bitcast.16) | data formatting | bytes 12582912
  29.7 3.5 %all-to-all-done.recv_ref = bf16[128,2,16,128]{3,2,1,0:T(8,128)(2,1)S(1)} async-done(((bf16[128,2,16,128]{3,2,1,0:T(8,128)(2,1)}), bf16[128,2,16,128]{3,2,1,0:T(8,128)(2,1)S(1)}, u32[]{:S(2)}, u32[]{:S(2)}) %all-to-all-start) | async-done | bytes 1048608 | tf_op jit(solution)/shard_map/all_to_all | solution.py:473
  33.2 4.2 %all-to-all-start.1 = ((bf16[16,64,256]{2,1,0:T(8,128)(2,1)}), bf16[16,64,256]{2,1,0:T(8,128)(2,1)S(1)}, u32[]{:S(2)}, u32[]{:S(2)}) async-start(bf16[16,64,256]{2,1,0:T(8,128)(2,1)} %get-tuple-element.19), calls=%async_computation.1 | async-start | bytes 1048576 | tf_op jit(solution)/shard_map/all_to_all | solution.py:484
  37.4 9.2 %convolve.1 = bf16[128,16,128]{2,1,0:T(8,128)(2,1)} custom-call(bf16[128,2,16,128]{3,2,1,0:T(8,128)(2,1)} %copy-done.1, f32[16,128]{1,0:T(8,128)} %reshape.32.gain_ref, bf16[256,256]{1,0:T(8,128)(2,1)} %constant.71.clone.w1, f32[128,128]{1,0:T(8,128)} %constant.72.clone.tc_ref, f32[128,128]{1,0:T(8,128)} %constant.73.clone.ts_ref, ...), custom_call_target="tpu_custom_call" | custom-call | tf_op jit(solution)/shard_map/convolve/pallas_call | solution.py:156
  46.6 3.2 %all-to-all-done.1.gate_ref = bf16[16,64,256]{2,1,0:T(8,128)(2,1)S(1)} async-done(((bf16[16,64,256]{2,1,0:T(8,128)(2,1)}), bf16[16,64,256]{2,1,0:T(8,128)(2,1)S(1)}, u32[]{:S(2)}, u32[]{:S(2)}) %all-to-all-start.1) | async-done | bytes 524320 | tf_op jit(solution)/shard_map/all_to_all | solution.py:484
  49.8 13.9 %all_to_all.25 = bf16[128,16,128]{2,1,0:T(8,128)(2,1)} all-to-all(bf16[128,16,128]{2,1,0:T(8,128)(2,1)} %convolve.1), channel_id=1, replica_groups=mesh['xl'=2,'yh'=2,'yl'=2,'z'=4,'xh'=2,'c'=2] {'xl','yh','yl'}, dimensions={0} | all-to-all | bytes 1048576 | tf_op jit(solution)/shard_map/all_to_all | solution.py:486
  63.7 2.2 %apply_gate.1 = (bf16[512,256]{1,0:T(8,128)(2,1)}, bf16[512,256]{1,0:T(8,128)(2,1)}) custom-call(s32[6]{0:T(128)} %stack.27.at_ref, bf16[8,16,16,128]{3,2,1,0:T(8,128)(2,1)} %bitcast.24, bf16[16,64,256]{2,1,0:T(8,128)(2,1)} %copy-done.2), custom_call_target="tpu_custom_call" | custom-call | tf_op jit(solution)/shard_map/apply_gate/pallas_call | solution.py:193
  65.9 0.9 collective-permute-start.4
  66.7 2.8 %collective-permute-start.2 = (bf16[512,256]{1,0:T(8,128)(2,1)}, bf16[512,256]{1,0:T(8,128)(2,1)S(1)}, u32[]{:S(2)}, u32[]{:S(2)}) collective-permute-start(bf16[512,256]{1,0:T(8,128)(2,1)} %get-tuple-element.22.refs_0_), channel_id=1, source_target_pairs={{0,2},{1,3},{2,0},{3,1},{4,6},{5,7},{6,4},{7,5},{8,10},{9,11},{10,... | collective-permute-start | bytes 786440 | tf_op jit(solution)/shard_map/ppermute | solution.py:449
  69.5 1.9 collective-permute-start.3
  71.4 2.1 %collective-permute-start.5 = (bf16[512,256]{1,0:T(8,128)(2,1)S(1)}, bf16[512,256]{1,0:T(8,128)(2,1)S(1)}, u32[]{:S(2)}, u32[]{:S(2)}) collective-permute-start(bf16[512,256]{1,0:T(8,128)(2,1)S(1)} %collective-permute-done.1.refs_1_), channel_id=1, source_target_pairs={{0,12},{1,13},{2,14},{3,15},{4,0},{5,1},{6,2},{7,3},{8,4},{9,5},{1... | collective-permute-start | bytes 786440 | tf_op jit(solution)/shard_map/ppermute | solution.py:449
  73.5 1.7 collective-permute-done.4.refs_4_.refs_3_
  75.2 1.5 collective-permute-start.6
  76.7 0.9 collective-permute-done.2.refs_2_
  77.6 1.2 collective-permute-start.9
  78.7 0.4 collective-permute-done.13.refs_12_.refs_4_
  79.1 1.7 collective-permute-start.8
  80.8 2.4 %collective-permute-done.3.refs_3_.refs_6_ = bf16[512,256]{1,0:T(8,128)(2,1)S(1)} collective-permute-done((bf16[512,256]{1,0:T(8,128)(2,1)S(1)}, bf16[512,256]{1,0:T(8,128)(2,1)S(1)}, u32[]{:S(2)}, u32[]{:S(2)}) %collective-permute-start.3) | collective-permute-done | bytes 262176 | tf_op jit(solution)/shard_map/ppermute | solution.py:449
  83.2 1.1 collective-permute-start.7
  84.3 2.6 %collective-permute-start.14 = (bf16[512,256]{1,0:T(8,128)(2,1)S(1)}, bf16[512,256]{1,0:T(8,128)(2,1)S(1)}, u32[]{:S(2)}, u32[]{:S(2)}) collective-permute-start(bf16[512,256]{1,0:T(8,128)(2,1)S(1)} %collective-permute-done.13.refs_12_.refs_4_), channel_id=1, source_target_pairs={{0,2},{1,3},{2,0},{3,1},{4,6},{5,7},{6,4},{7,5},{8,10},{9,11},{10,... | collective-permute-start | bytes 786440 | tf_op jit(solution)/shard_map/ppermute | solution.py:449
  86.9 1.9 collective-permute-done.6.refs_6_.refs_9_
  88.8 1.2 collective-permute-start.15
  90.0 0.1 collective-permute-start.10
  90.1 2.4 %collective-permute-start.11 = (bf16[512,256]{1,0:T(8,128)(2,1)S(1)}, bf16[512,256]{1,0:T(8,128)(2,1)S(1)}, u32[]{:S(2)}, u32[]{:S(2)}) collective-permute-start(bf16[512,256]{1,0:T(8,128)(2,1)S(1)} %collective-permute-done.8.refs_8_.refs_5_), channel_id=1, source_target_pairs={{0,2},{1,3},{2,0},{3,1},{4,6},{5,7},{6,4},{7,5},{8,10},{9,11},{10,... | collective-permute-start | bytes 786440 | tf_op jit(solution)/shard_map/ppermute | solution.py:449
  92.4 2.5 %collective-permute-start.12 = (bf16[512,256]{1,0:T(8,128)(2,1)S(1)}, bf16[512,256]{1,0:T(8,128)(2,1)S(1)}, u32[]{:S(2)}, u32[]{:S(2)}) collective-permute-start(bf16[512,256]{1,0:T(8,128)(2,1)S(1)} %collective-permute-done.7.refs_7_.refs_0_), channel_id=1, source_target_pairs={{0,12},{1,13},{2,14},{3,15},{4,0},{5,1},{6,2},{7,3},{8,4},{9,5},{1... | collective-permute-start | bytes 786440 | tf_op jit(solution)/shard_map/ppermute | solution.py:449
  95.0 10.8 %project_0.1.refs_8_ = f32[2,512,768]{2,1,0:T(8,128)} custom-call(s32[6]{0:T(128)} %stack.27.at_ref, bf16[512,256]{1,0:T(8,128)(2,1)} %get-tuple-element.22.refs_0_, bf16[512,256]{1,0:T(8,128)(2,1)} %copy-done.3, bf16[512,256]{1,0:T(8,128)(2,1)} %copy-done.5, bf16[512,256]{1,0:T(8,128)(2,1)} %copy-done.4, bf16[512,256]{1,0:T(8,128)(2,1)} %copy-done.6, ...), custom_call_target="tpu_custom_call" | custom-call | flops 4026531840 | bytes 7864320 | tf_op jit(solution)/shard_map/project_0/pallas_call | solution.py:291
  105.9 0.6 copy-done.13
  106.5 0.1 copy-done.15
  106.6 0.1 copy-done.16
  106.7 0.1 copy-done.14
  106.8 0.7 copy-done.17
  107.5 8.2 %project_1.1 = bf16[8,1280,128]{2,1,0:T(8,128)(2,1)} custom-call(s32[6]{0:T(128)} %stack.27.at_ref, bf16[512,256]{1,0:T(8,128)(2,1)} %copy-done.12, bf16[512,256]{1,0:T(8,128)(2,1)} %copy-done.15, bf16[512,256]{1,0:T(8,128)(2,1)} %copy-done.16, bf16[512,256]{1,0:T(8,128)(2,1)} %copy-done.17, bf16[512,256]{1,0:T(8,128)(2,1)} %copy-done.13, ...), custom_call_target="tpu_custom_call" | custom-call | flops 2415919104 | bytes 4718592 | tf_op jit(solution)/shard_map/project_1/pallas_call | solution.py:291
  115.7 34.4 %all_to_all.26.refs_0_ = bf16[8,1280,128]{2,1,0:T(8,128)(2,1)S(1)} all-to-all(bf16[8,1280,128]{2,1,0:T(8,128)(2,1)} %project_1.1), channel_id=1, replica_groups=mesh['xl'=2,'yh'=2,'yl'=2,'z'=4,'xh'=2,'c'=2] {'xl','yh','yl'}, dimensions={0} | all-to-all | bytes 5242880 | tf_op jit(solution)/shard_map/all_to_all | solution.py:508
  150.0 5.0 %collective-permute-done.16.refs_1_ = bf16[8,1280,128]{2,1,0:T(8,128)(2,1)} collective-permute-done((bf16[8,1280,128]{2,1,0:T(8,128)(2,1)S(1)}, bf16[8,1280,128]{2,1,0:T(8,128)(2,1)}, u32[]{:S(2)}, u32[]{:S(2)}) %collective-permute-start.16) | collective-permute-done | bytes 2621472 | tf_op jit(solution)/shard_map/ppermute | solution.py:449
  155.1 23.6 %attend.1 = bf16[64,32,128]{2,1,0:T(8,128)(2,1)} custom-call(s32[6]{0:T(128)} %stack.27.at_ref, bf16[8,1280,128]{2,1,0:T(8,128)(2,1)} %copy-done, bf16[8,1280,128]{2,1,0:T(8,128)(2,1)} %collective-permute-done.16.refs_1_), custom_call_target="tpu_custom_call" | custom-call | tf_op jit(solution)/shard_map/attend/pallas_call | solution.py:425
  178.7 4.9 %all-to-all-start.4 = ((bf16[64,32,128]{2,1,0:T(8,128)(2,1)}), bf16[64,32,128]{2,1,0:T(8,128)(2,1)S(1)}, u32[]{:S(2)}, u32[]{:S(2)}) async-start(bf16[64,32,128]{2,1,0:T(8,128)(2,1)} %attend.1), calls=%async_computation.4 | async-start | bytes 1048576 | tf_op jit(solution)/shard_map/all_to_all | solution.py:512
  183.6 2.6 %collect.1 = bf16[64,4096]{1,0:T(8,128)(2,1)} custom-call(s32[6]{0:T(128)} %stack.27.at_ref, bf16[512,256]{1,0:T(8,128)(2,1)} %get-tuple-element.22.refs_0_, bf16[512,256]{1,0:T(8,128)(2,1)} %copy-done.3, bf16[512,256]{1,0:T(8,128)(2,1)} %copy-done.5, bf16[512,256]{1,0:T(8,128)(2,1)} %copy-done.7, bf16[512,256]{1,0:T(8,128)(2,1)} %copy-done.4, ...), custom_call_target="tpu_custom_call" | custom-call | tf_op jit(solution)/shard_map/collect/pallas_call | solution.py:217
  186.3 11.0 %all-to-all-done.4 = bf16[64,32,128]{2,1,0:T(8,128)(2,1)S(1)} async-done(((bf16[64,32,128]{2,1,0:T(8,128)(2,1)}), bf16[64,32,128]{2,1,0:T(8,128)(2,1)S(1)}, u32[]{:S(2)}, u32[]{:S(2)}) %all-to-all-start.4) | async-done | bytes 524320 | tf_op jit(solution)/shard_map/all_to_all | solution.py:512
  197.2 0.5 copy.17
  197.8 1.2 reshape.35
  (49 shorter events, 0.2 us)
Async XLA Ops:
  0.6 22.6 %collective-permute-start = (bf16[4096,2,384]{2,1,0:T(2,128)(2,1)}, bf16[4096,2,384]{2,1,0:T(2,128)(2,1)}, u32[]{:S(2)}, u32[]{:S(2)}) collective-permute-start(bf16[4096,2,384]{2,1,0:T(2,128)(2,1)} %param.17), channel_id=1, source_target_pairs={{0,1},{1,0},{2,3},{3,2},{4,5},{5,4},{6,7},{7,6},{8,9},{9,8},{10,11... | collective-permute-start | bytes 18874376 | tf_op jit(solution)/shard_map/ppermute | solution.py:449
  3.7 29.5 %all-to-all-start = ((bf16[128,2,16,128]{3,2,1,0:T(8,128)(2,1)}), bf16[128,2,16,128]{3,2,1,0:T(8,128)(2,1)S(1)}, u32[]{:S(2)}, u32[]{:S(2)}) async-start(bf16[128,2,16,128]{3,2,1,0:T(8,128)(2,1)} %bitcast.25), calls=%async_computation | async-start | bytes 2097152 | tf_op jit(solution)/shard_map/all_to_all | solution.py:473
  15.0 6.6 %copy-start.18 = (f32[4096]{0:T(1024)S(1)}, f32[4096]{0:T(1024)}, u32[]{:S(2)}) copy-start(f32[4096]{0:T(1024)} %param.16) | copy-start | bytes 49156
  33.2 4.2 %copy-start.1 = (bf16[128,2,16,128]{3,2,1,0:T(8,128)(2,1)}, bf16[128,2,16,128]{3,2,1,0:T(8,128)(2,1)S(1)}, u32[]{:S(2)}) copy-start(bf16[128,2,16,128]{3,2,1,0:T(8,128)(2,1)S(1)} %all-to-all-done.recv_ref) | copy-start | bytes 3145732
  33.2 16.5 %all-to-all-start.1 = ((bf16[16,64,256]{2,1,0:T(8,128)(2,1)}), bf16[16,64,256]{2,1,0:T(8,128)(2,1)S(1)}, u32[]{:S(2)}, u32[]{:S(2)}) async-start(bf16[16,64,256]{2,1,0:T(8,128)(2,1)} %get-tuple-element.19), calls=%async_computation.1 | async-start | bytes 1048576 | tf_op jit(solution)/shard_map/all_to_all | solution.py:484
  49.8 13.9 %copy-start.2 = (bf16[16,64,256]{2,1,0:T(8,128)(2,1)}, bf16[16,64,256]{2,1,0:T(8,128)(2,1)S(1)}, u32[]{:S(2)}) copy-start(bf16[16,64,256]{2,1,0:T(8,128)(2,1)S(1)} %all-to-all-done.1.gate_ref) | copy-start | bytes 1572868
  65.9 3.7 %collective-permute-start.1 = (bf16[512,256]{1,0:T(8,128)(2,1)}, bf16[512,256]{1,0:T(8,128)(2,1)S(1)}, u32[]{:S(2)}, u32[]{:S(2)}) collective-permute-start(bf16[512,256]{1,0:T(8,128)(2,1)} %get-tuple-element.23), channel_id=1, source_target_pairs={{0,1},{1,0},{2,3},{3,2},{4,5},{5,4},{6,7},{7,6},{8,9},{9,8},{10,11... | collective-permute-start | bytes 786440 | tf_op jit(solution)/shard_map/ppermute | solution.py:449
  65.9 9.3 %collective-permute-start.4 = (bf16[512,256]{1,0:T(8,128)(2,1)}, bf16[512,256]{1,0:T(8,128)(2,1)S(1)}, u32[]{:S(2)}, u32[]{:S(2)}) collective-permute-start(bf16[512,256]{1,0:T(8,128)(2,1)} %get-tuple-element.22.refs_0_), channel_id=1, source_target_pairs={{0,12},{1,13},{2,14},{3,15},{4,0},{5,1},{6,2},{7,3},{8,4},{9,5},{1... | collective-permute-start | bytes 786440 | tf_op jit(solution)/shard_map/ppermute | solution.py:449
  66.7 10.9 %collective-permute-start.2 = (bf16[512,256]{1,0:T(8,128)(2,1)}, bf16[512,256]{1,0:T(8,128)(2,1)S(1)}, u32[]{:S(2)}, u32[]{:S(2)}) collective-permute-start(bf16[512,256]{1,0:T(8,128)(2,1)} %get-tuple-element.22.refs_0_), channel_id=1, source_target_pairs={{0,2},{1,3},{2,0},{3,1},{4,6},{5,7},{6,4},{7,5},{8,10},{9,11},{10,... | collective-permute-start | bytes 786440 | tf_op jit(solution)/shard_map/ppermute | solution.py:449
  69.5 9.6 %collective-permute-start.13 = (bf16[512,256]{1,0:T(8,128)(2,1)}, bf16[512,256]{1,0:T(8,128)(2,1)S(1)}, u32[]{:S(2)}, u32[]{:S(2)}) collective-permute-start(bf16[512,256]{1,0:T(8,128)(2,1)} %get-tuple-element.22.refs_0_), channel_id=1, source_target_pairs={{0,4},{1,5},{2,6},{3,7},{4,8},{5,9},{6,10},{7,11},{8,12},{9,13},{1... | collective-permute-start | bytes 786440 | tf_op jit(solution)/shard_map/ppermute | solution.py:449
  69.5 25.4 %copy-start.3 = (bf16[512,256]{1,0:T(8,128)(2,1)}, bf16[512,256]{1,0:T(8,128)(2,1)S(1)}, u32[]{:S(2)}) copy-start(bf16[512,256]{1,0:T(8,128)(2,1)S(1)} %collective-permute-done.1.refs_1_) | copy-start | bytes 786436
  69.5 13.7 %collective-permute-start.3 = (bf16[512,256]{1,0:T(8,128)(2,1)S(1)}, bf16[512,256]{1,0:T(8,128)(2,1)S(1)}, u32[]{:S(2)}, u32[]{:S(2)}) collective-permute-start(bf16[512,256]{1,0:T(8,128)(2,1)S(1)} %collective-permute-done.1.refs_1_), channel_id=1, source_target_pairs={{0,2},{1,3},{2,0},{3,1},{4,6},{5,7},{6,4},{7,5},{8,10},{9,11},{10,... | collective-permute-start | bytes 786440 | tf_op jit(solution)/shard_map/ppermute | solution.py:449
  71.4 12.8 %collective-permute-start.5 = (bf16[512,256]{1,0:T(8,128)(2,1)S(1)}, bf16[512,256]{1,0:T(8,128)(2,1)S(1)}, u32[]{:S(2)}, u32[]{:S(2)}) collective-permute-start(bf16[512,256]{1,0:T(8,128)(2,1)S(1)} %collective-permute-done.1.refs_1_), channel_id=1, source_target_pairs={{0,12},{1,13},{2,14},{3,15},{4,0},{5,1},{6,2},{7,3},{8,4},{9,5},{1... | collective-permute-start | bytes 786440 | tf_op jit(solution)/shard_map/ppermute | solution.py:449
  75.2 19.8 %copy-start.4 = (bf16[512,256]{1,0:T(8,128)(2,1)}, bf16[512,256]{1,0:T(8,128)(2,1)S(1)}, u32[]{:S(2)}) copy-start(bf16[512,256]{1,0:T(8,128)(2,1)S(1)} %collective-permute-done.4.refs_4_.refs_3_) | copy-start | bytes 786436
  75.2 13.6 %collective-permute-start.6 = (bf16[512,256]{1,0:T(8,128)(2,1)S(1)}, bf16[512,256]{1,0:T(8,128)(2,1)S(1)}, u32[]{:S(2)}, u32[]{:S(2)}) collective-permute-start(bf16[512,256]{1,0:T(8,128)(2,1)S(1)} %collective-permute-done.4.refs_4_.refs_3_), channel_id=1, source_target_pairs={{0,2},{1,3},{2,0},{3,1},{4,6},{5,7},{6,4},{7,5},{8,10},{9,11},{10,... | collective-permute-start | bytes 786440 | tf_op jit(solution)/shard_map/ppermute | solution.py:449
  77.6 17.4 %copy-start.5 = (bf16[512,256]{1,0:T(8,128)(2,1)}, bf16[512,256]{1,0:T(8,128)(2,1)S(1)}, u32[]{:S(2)}) copy-start(bf16[512,256]{1,0:T(8,128)(2,1)S(1)} %collective-permute-done.2.refs_2_) | copy-start | bytes 786436
  77.6 12.4 %collective-permute-start.9 = (bf16[512,256]{1,0:T(8,128)(2,1)S(1)}, bf16[512,256]{1,0:T(8,128)(2,1)S(1)}, u32[]{:S(2)}, u32[]{:S(2)}) collective-permute-start(bf16[512,256]{1,0:T(8,128)(2,1)S(1)} %collective-permute-done.1.refs_1_), channel_id=1, source_target_pairs={{0,4},{1,5},{2,6},{3,7},{4,8},{5,9},{6,10},{7,11},{8,12},{9,13},{1... | collective-permute-start | bytes 786440 | tf_op jit(solution)/shard_map/ppermute | solution.py:449
  79.1 15.9 %copy-start.6 = (bf16[512,256]{1,0:T(8,128)(2,1)}, bf16[512,256]{1,0:T(8,128)(2,1)S(1)}, u32[]{:S(2)}) copy-start(bf16[512,256]{1,0:T(8,128)(2,1)S(1)} %collective-permute-done.13.refs_12_.refs_4_) | copy-start | bytes 786436
  79.1 11.0 %collective-permute-start.8 = (bf16[512,256]{1,0:T(8,128)(2,1)S(1)}, bf16[512,256]{1,0:T(8,128)(2,1)S(1)}, u32[]{:S(2)}, u32[]{:S(2)}) collective-permute-start(bf16[512,256]{1,0:T(8,128)(2,1)S(1)} %collective-permute-done.4.refs_4_.refs_3_), channel_id=1, source_target_pairs={{0,12},{1,13},{2,14},{3,15},{4,0},{5,1},{6,2},{7,3},{8,4},{9,5},{1... | collective-permute-start | bytes 786440 | tf_op jit(solution)/shard_map/ppermute | solution.py:449
  83.2 11.8 %copy-start.7 = (bf16[512,256]{1,0:T(8,128)(2,1)}, bf16[512,256]{1,0:T(8,128)(2,1)S(1)}, u32[]{:S(2)}) copy-start(bf16[512,256]{1,0:T(8,128)(2,1)S(1)} %collective-permute-done.3.refs_3_.refs_6_) | copy-start | bytes 786436
  83.2 9.3 %collective-permute-start.7 = (bf16[512,256]{1,0:T(8,128)(2,1)S(1)}, bf16[512,256]{1,0:T(8,128)(2,1)S(1)}, u32[]{:S(2)}, u32[]{:S(2)}) collective-permute-start(bf16[512,256]{1,0:T(8,128)(2,1)S(1)} %collective-permute-done.3.refs_3_.refs_6_), channel_id=1, source_target_pairs={{0,12},{1,13},{2,14},{3,15},{4,0},{5,1},{6,2},{7,3},{8,4},{9,5},{1... | collective-permute-start | bytes 786440 | tf_op jit(solution)/shard_map/ppermute | solution.py:449
  84.2 10.7 %copy-start.8 = (bf16[512,256]{1,0:T(8,128)(2,1)}, bf16[512,256]{1,0:T(8,128)(2,1)S(1)}, u32[]{:S(2)}) copy-start(bf16[512,256]{1,0:T(8,128)(2,1)S(1)} %collective-permute-done.5.refs_5_.refs_7_) | copy-start | bytes 786436
  84.3 21.6 %collective-permute-start.14 = (bf16[512,256]{1,0:T(8,128)(2,1)S(1)}, bf16[512,256]{1,0:T(8,128)(2,1)S(1)}, u32[]{:S(2)}, u32[]{:S(2)}) collective-permute-start(bf16[512,256]{1,0:T(8,128)(2,1)S(1)} %collective-permute-done.13.refs_12_.refs_4_), channel_id=1, source_target_pairs={{0,2},{1,3},{2,0},{3,1},{4,6},{5,7},{6,4},{7,5},{8,10},{9,11},{10,... | collective-permute-start | bytes 786440 | tf_op jit(solution)/shard_map/ppermute | solution.py:449
  88.8 6.2 %copy-start.9 = (bf16[512,256]{1,0:T(8,128)(2,1)}, bf16[512,256]{1,0:T(8,128)(2,1)S(1)}, u32[]{:S(2)}) copy-start(bf16[512,256]{1,0:T(8,128)(2,1)S(1)} %collective-permute-done.6.refs_6_.refs_9_) | copy-start | bytes 786436
  88.8 17.1 %collective-permute-start.15 = (bf16[512,256]{1,0:T(8,128)(2,1)S(1)}, bf16[512,256]{1,0:T(8,128)(2,1)S(1)}, u32[]{:S(2)}, u32[]{:S(2)}) collective-permute-start(bf16[512,256]{1,0:T(8,128)(2,1)S(1)} %collective-permute-done.3.refs_3_.refs_6_), channel_id=1, source_target_pairs={{0,4},{1,5},{2,6},{3,7},{4,8},{5,9},{6,10},{7,11},{8,12},{9,13},{1... | collective-permute-start | bytes 786440 | tf_op jit(solution)/shard_map/ppermute | solution.py:449
  90.0 5.0 %copy-start.10 = (bf16[512,256]{1,0:T(8,128)(2,1)}, bf16[512,256]{1,0:T(8,128)(2,1)S(1)}, u32[]{:S(2)}) copy-start(bf16[512,256]{1,0:T(8,128)(2,1)S(1)} %collective-permute-done.9.refs_13_.refs_8_) | copy-start | bytes 786436
  90.0 15.9 %collective-permute-start.10 = (bf16[512,256]{1,0:T(8,128)(2,1)S(1)}, bf16[512,256]{1,0:T(8,128)(2,1)S(1)}, u32[]{:S(2)}, u32[]{:S(2)}) collective-permute-start(bf16[512,256]{1,0:T(8,128)(2,1)S(1)} %collective-permute-done.9.refs_13_.refs_8_), channel_id=1, source_target_pairs={{0,4},{1,5},{2,6},{3,7},{4,8},{5,9},{6,10},{7,11},{8,12},{9,13},{1... | collective-permute-start | bytes 786440 | tf_op jit(solution)/shard_map/ppermute | solution.py:449
  90.1 5.0 %copy-start.11 = (bf16[512,256]{1,0:T(8,128)(2,1)}, bf16[512,256]{1,0:T(8,128)(2,1)S(1)}, u32[]{:S(2)}) copy-start(bf16[512,256]{1,0:T(8,128)(2,1)S(1)} %collective-permute-done.8.refs_8_.refs_5_) | copy-start | bytes 786436
  90.1 15.8 %collective-permute-start.11 = (bf16[512,256]{1,0:T(8,128)(2,1)S(1)}, bf16[512,256]{1,0:T(8,128)(2,1)S(1)}, u32[]{:S(2)}, u32[]{:S(2)}) collective-permute-start(bf16[512,256]{1,0:T(8,128)(2,1)S(1)} %collective-permute-done.8.refs_8_.refs_5_), channel_id=1, source_target_pairs={{0,2},{1,3},{2,0},{3,1},{4,6},{5,7},{6,4},{7,5},{8,10},{9,11},{10,... | collective-permute-start | bytes 786440 | tf_op jit(solution)/shard_map/ppermute | solution.py:449
  92.4 13.4 %copy-start.12 = (bf16[512,256]{1,0:T(8,128)(2,1)}, bf16[512,256]{1,0:T(8,128)(2,1)S(1)}, u32[]{:S(2)}) copy-start(bf16[512,256]{1,0:T(8,128)(2,1)S(1)} %collective-permute-done.7.refs_7_.refs_0_) | copy-start | bytes 786436
  92.4 13.5 %collective-permute-start.12 = (bf16[512,256]{1,0:T(8,128)(2,1)S(1)}, bf16[512,256]{1,0:T(8,128)(2,1)S(1)}, u32[]{:S(2)}, u32[]{:S(2)}) collective-permute-start(bf16[512,256]{1,0:T(8,128)(2,1)S(1)} %collective-permute-done.7.refs_7_.refs_0_), channel_id=1, source_target_pairs={{0,12},{1,13},{2,14},{3,15},{4,0},{5,1},{6,2},{7,3},{8,4},{9,5},{1... | collective-permute-start | bytes 786440 | tf_op jit(solution)/shard_map/ppermute | solution.py:449
  105.8 0.7 copy-start.13
  105.8 0.8 copy-start.15
  105.9 0.8 copy-start.16
  105.9 0.9 copy-start.14
  106.8 0.7 copy-start.17
  150.0 5.0 %copy-start = (bf16[8,1280,128]{2,1,0:T(8,128)(2,1)}, bf16[8,1280,128]{2,1,0:T(8,128)(2,1)S(1)}, u32[]{:S(2)}) copy-start(bf16[8,1280,128]{2,1,0:T(8,128)(2,1)S(1)} %all_to_all.26.refs_0_) | copy-start | bytes 7864324
  150.0 5.0 %collective-permute-start.16 = (bf16[8,1280,128]{2,1,0:T(8,128)(2,1)S(1)}, bf16[8,1280,128]{2,1,0:T(8,128)(2,1)}, u32[]{:S(2)}, u32[]{:S(2)}) collective-permute-start(bf16[8,1280,128]{2,1,0:T(8,128)(2,1)S(1)} %all_to_all.26.refs_0_), channel_id=1, source_target_pairs={{0,1},{1,0},{2,3},{3,2},{4,5},{5,4},{6,7},{7,6},{8,9},{9,8},{10,11... | collective-permute-start | bytes 7864328 | tf_op jit(solution)/shard_map/ppermute | solution.py:449
  178.7 18.5 %all-to-all-start.4 = ((bf16[64,32,128]{2,1,0:T(8,128)(2,1)}), bf16[64,32,128]{2,1,0:T(8,128)(2,1)S(1)}, u32[]{:S(2)}, u32[]{:S(2)}) async-start(bf16[64,32,128]{2,1,0:T(8,128)(2,1)} %attend.1), calls=%async_computation.4 | async-start | bytes 1048576 | tf_op jit(solution)/shard_map/all_to_all | solution.py:512

commit v6 on v5

--- a/solution.py
+++ b/solution.py
@@ -244,9 +244,9 @@
         for n, spot in enumerate(spots):
             rows = pl.ds(pl.multiple_of(place(at_ref, spot) * WIDE, WIDE), WIDE)
             load(weights[side].at[rows, :], w_s.at[side, pl.ds(n * WIDE, WIDE)])
-        if not first:
-            load(before.at[side], acc.at[side])
-    per_side = len(spots) + (not first)
+    for side in range(0 if first else 2):
+        load(before.at[side], acc.at[side])
+    count = len(spots)
     for copy in loads[: len(spots)]:
         copy.wait()
 
@@ -257,10 +257,11 @@
         saves[-1].start()
 
     for side in range(2):
-        for copy in loads[len(spots) + side * per_side : len(spots) + (side + 1) * per_side]:
+        for copy in loads[(side + 1) * count : (side + 2) * count]:
             copy.wait()
         done = dot(x_s[...], w_s[side])
         if not first:
+            loads[3 * count + side].wait()
             done = done + acc[side]
         if not last:
             acc[side] = done

time: 200 us -> 201 us (level)
  no operation moved by 1% of the time
where the time goes in v6:
time: 201 us; the launch traced here: 200 us
  Pallas kernels  60.5 us (30%)
  blocking collectives  48.3 us (24%)
  starting transfers between devices  42.2 us (21%)
  waiting for transfers between devices  29.9 us (15%)
  local copies, waits for them, and re-layouts  18 us (9%)
    all_to_all x1, blocking collectives, per_device(): lax.all_to_all(share, ('xl', 'yh', 'yl'), split_axis=0, concat_axis=0, ti...  34.4 us
    pallas_call x1, Pallas kernels, attend(): pl.pallas_call(attend_kernel, out_shape=jax.ShapeDtypeStruct((64, PART, H...  23.7 us
    ppermute x17, starting transfers between devices, shift(): return lax.ppermute(x, NAMES, pairs)  21.9 us
    pallas_call x2, Pallas kernels, project(): pl.pallas_call(functools.partial(project_kernel, stage), out_shape=jax.Sh...  19.9 us
    unnamed x40, local copies, waits for them, and re-layouts  14.7 us
    all_to_all x1, blocking collectives, per_device(): lax.all_to_all(filtered, ('xl', 'yh', 'yl'), split_axis=0, concat_axis=0,...  13.9 us
    ppermute x17, waiting for transfers between devices, shift(): return lax.ppermute(x, NAMES, pairs)  12.3 us
    all_to_all x1, starting transfers between devices, per_device(): lax.all_to_all(packed, NAMES, split_axis=0, concat_axis=0, tiled=True)  11.2 us
  transfers between devices with their start and end apart: 20, of which 9 were waited for; matrix products, arithmetic and copies ran while one was open for 7% of the time, Pallas kernels for 13%

profile of v6, /device:TPU:0, one launch (start us, length us, event | category | flops | bytes accessed | tf_op | source)
XLA Modules:
  0.0 199.9 jit_solution(4490207788315623420)
XLA Ops:
  0.6 0.1 collective-permute-start
  0.7 3.0 %pack.1 = (bf16[8,16,2,16,128]{4,3,2,1,0:T(8,128)(2,1)}, bf16[16,64,256]{2,1,0:T(8,128)(2,1)}) custom-call(bf16[64,4096]{1,0:T(8,128)(2,1)} %key_ref.1, bf16[64,4096]{1,0:T(8,128)(2,1)} %value_ref.1, bf16[64,4096]{1,0:T(8,128)(2,1)} %taps_ref.1, bf16[64,4096]{1,0:T(8,128)(2,1)} %gate_ref.1), custom_call_target="tpu_custom_call" | custom-call | tf_op jit(solution)/shard_map/pack/pallas_call | solution.py:87
  3.7 11.2 %all-to-all-start = ((bf16[128,2,16,128]{3,2,1,0:T(8,128)(2,1)}), bf16[128,2,16,128]{3,2,1,0:T(8,128)(2,1)S(1)}, u32[]{:S(2)}, u32[]{:S(2)}) async-start(bf16[128,2,16,128]{3,2,1,0:T(8,128)(2,1)} %bitcast.25), calls=%async_computation | async-start | bytes 2097152 | tf_op jit(solution)/shard_map/all_to_all | solution.py:474
  15.0 6.5 %copy.18 = bf16[512,8,2,384]{3,1,2,0:T(8,128)(2,1)} copy(bf16[512,8,2,384]{3,2,1,0:T(2,128)(2,1)} %bitcast.22) | data formatting | bytes 12582912
  21.6 0.1 reshape.31
  21.7 0.1 copy.16
  21.9 0.7 reshape.32.gain_ref
  22.6 0.7 stack.27.at_ref
  23.2 6.5 %copy.19 = bf16[512,8,2,384]{3,1,2,0:T(8,128)(2,1)} copy(bf16[512,8,2,384]{3,2,1,0:T(2,128)(2,1)} %bitcast.16) | data formatting | bytes 12582912
  29.7 3.5 %all-to-all-done.recv_ref = bf16[128,2,16,128]{3,2,1,0:T(8,128)(2,1)S(1)} async-done(((bf16[128,2,16,128]{3,2,1,0:T(8,128)(2,1)}), bf16[128,2,16,128]{3,2,1,0:T(8,128)(2,1)S(1)}, u32[]{:S(2)}, u32[]{:S(2)}) %all-to-all-start) | async-done | bytes 1048608 | tf_op jit(solution)/shard_map/all_to_all | solution.py:474
  33.2 4.2 %all-to-all-start.1 = ((bf16[16,64,256]{2,1,0:T(8,128)(2,1)}), bf16[16,64,256]{2,1,0:T(8,128)(2,1)S(1)}, u32[]{:S(2)}, u32[]{:S(2)}) async-start(bf16[16,64,256]{2,1,0:T(8,128)(2,1)} %get-tuple-element.19), calls=%async_computation.1 | async-start | bytes 1048576 | tf_op jit(solution)/shard_map/all_to_all | solution.py:485
  37.4 9.2 %convolve.1 = bf16[128,16,128]{2,1,0:T(8,128)(2,1)} custom-call(bf16[128,2,16,128]{3,2,1,0:T(8,128)(2,1)} %copy-done.1, f32[16,128]{1,0:T(8,128)} %reshape.32.gain_ref, bf16[256,256]{1,0:T(8,128)(2,1)} %constant.71.clone.w1, f32[128,128]{1,0:T(8,128)} %constant.72.clone.tc_ref, f32[128,128]{1,0:T(8,128)} %constant.73.clone.ts_ref, ...), custom_call_target="tpu_custom_call" | custom-call | tf_op jit(solution)/shard_map/convolve/pallas_call | solution.py:156
  46.6 3.2 %all-to-all-done.1.gate_ref = bf16[16,64,256]{2,1,0:T(8,128)(2,1)S(1)} async-done(((bf16[16,64,256]{2,1,0:T(8,128)(2,1)}), bf16[16,64,256]{2,1,0:T(8,128)(2,1)S(1)}, u32[]{:S(2)}, u32[]{:S(2)}) %all-to-all-start.1) | async-done | bytes 524320 | tf_op jit(solution)/shard_map/all_to_all | solution.py:485
  49.8 13.9 %all_to_all.25 = bf16[128,16,128]{2,1,0:T(8,128)(2,1)} all-to-all(bf16[128,16,128]{2,1,0:T(8,128)(2,1)} %convolve.1), channel_id=1, replica_groups=mesh['xl'=2,'yh'=2,'yl'=2,'z'=4,'xh'=2,'c'=2] {'xl','yh','yl'}, dimensions={0} | all-to-all | bytes 1048576 | tf_op jit(solution)/shard_map/all_to_all | solution.py:487
  63.7 2.2 %apply_gate.1 = (bf16[512,256]{1,0:T(8,128)(2,1)}, bf16[512,256]{1,0:T(8,128)(2,1)}) custom-call(s32[6]{0:T(128)} %stack.27.at_ref, bf16[8,16,16,128]{3,2,1,0:T(8,128)(2,1)} %bitcast.24, bf16[16,64,256]{2,1,0:T(8,128)(2,1)} %copy-done.2), custom_call_target="tpu_custom_call" | custom-call | tf_op jit(solution)/shard_map/apply_gate/pallas_call | solution.py:193
  65.9 0.9 collective-permute-start.4
  66.7 2.8 %collective-permute-start.2 = (bf16[512,256]{1,0:T(8,128)(2,1)}, bf16[512,256]{1,0:T(8,128)(2,1)S(1)}, u32[]{:S(2)}, u32[]{:S(2)}) collective-permute-start(bf16[512,256]{1,0:T(8,128)(2,1)} %get-tuple-element.22.refs_0_), channel_id=1, source_target_pairs={{0,2},{1,3},{2,0},{3,1},{4,6},{5,7},{6,4},{7,5},{8,10},{9,11},{10,... | collective-permute-start | bytes 786440 | tf_op jit(solution)/shard_map/ppermute | solution.py:450
  69.5 1.9 collective-permute-start.3
  71.4 2.1 %collective-permute-start.5 = (bf16[512,256]{1,0:T(8,128)(2,1)S(1)}, bf16[512,256]{1,0:T(8,128)(2,1)S(1)}, u32[]{:S(2)}, u32[]{:S(2)}) collective-permute-start(bf16[512,256]{1,0:T(8,128)(2,1)S(1)} %collective-permute-done.1.refs_1_), channel_id=1, source_target_pairs={{0,12},{1,13},{2,14},{3,15},{4,0},{5,1},{6,2},{7,3},{8,4},{9,5},{1... | collective-permute-start | bytes 786440 | tf_op jit(solution)/shard_map/ppermute | solution.py:450
  73.5 1.7 collective-permute-done.4.refs_4_.refs_3_
  75.2 1.5 collective-permute-start.6
  76.7 0.9 collective-permute-done.2.refs_2_
  77.6 1.2 collective-permute-start.9
  78.7 0.4 collective-permute-done.13.refs_12_.refs_4_
  79.1 1.7 collective-permute-start.8
  80.8 2.4 %collective-permute-done.3.refs_3_.refs_6_ = bf16[512,256]{1,0:T(8,128)(2,1)S(1)} collective-permute-done((bf16[512,256]{1,0:T(8,128)(2,1)S(1)}, bf16[512,256]{1,0:T(8,128)(2,1)S(1)}, u32[]{:S(2)}, u32[]{:S(2)}) %collective-permute-start.3) | collective-permute-done | bytes 262176 | tf_op jit(solution)/shard_map/ppermute | solution.py:450
  83.2 1.1 collective-permute-start.7
  84.3 2.6 %collective-permute-start.14 = (bf16[512,256]{1,0:T(8,128)(2,1)S(1)}, bf16[512,256]{1,0:T(8,128)(2,1)S(1)}, u32[]{:S(2)}, u32[]{:S(2)}) collective-permute-start(bf16[512,256]{1,0:T(8,128)(2,1)S(1)} %collective-permute-done.13.refs_12_.refs_4_), channel_id=1, source_target_pairs={{0,2},{1,3},{2,0},{3,1},{4,6},{5,7},{6,4},{7,5},{8,10},{9,11},{10,... | collective-permute-start | bytes 786440 | tf_op jit(solution)/shard_map/ppermute | solution.py:450
  86.9 1.9 collective-permute-done.6.refs_6_.refs_9_
  88.8 1.2 collective-permute-start.15
  90.0 0.1 collective-permute-start.10
  90.1 2.4 %collective-permute-start.11 = (bf16[512,256]{1,0:T(8,128)(2,1)S(1)}, bf16[512,256]{1,0:T(8,128)(2,1)S(1)}, u32[]{:S(2)}, u32[]{:S(2)}) collective-permute-start(bf16[512,256]{1,0:T(8,128)(2,1)S(1)} %collective-permute-done.8.refs_8_.refs_5_), channel_id=1, source_target_pairs={{0,2},{1,3},{2,0},{3,1},{4,6},{5,7},{6,4},{7,5},{8,10},{9,11},{10,... | collective-permute-start | bytes 786440 | tf_op jit(solution)/shard_map/ppermute | solution.py:450
  92.4 2.5 %collective-permute-start.12 = (bf16[512,256]{1,0:T(8,128)(2,1)S(1)}, bf16[512,256]{1,0:T(8,128)(2,1)S(1)}, u32[]{:S(2)}, u32[]{:S(2)}) collective-permute-start(bf16[512,256]{1,0:T(8,128)(2,1)S(1)} %collective-permute-done.7.refs_7_.refs_0_), channel_id=1, source_target_pairs={{0,12},{1,13},{2,14},{3,15},{4,0},{5,1},{6,2},{7,3},{8,4},{9,5},{1... | collective-permute-start | bytes 786440 | tf_op jit(solution)/shard_map/ppermute | solution.py:450
  95.0 10.8 %project_0.1.refs_8_ = f32[2,512,768]{2,1,0:T(8,128)} custom-call(s32[6]{0:T(128)} %stack.27.at_ref, bf16[512,256]{1,0:T(8,128)(2,1)} %get-tuple-element.22.refs_0_, bf16[512,256]{1,0:T(8,128)(2,1)} %copy-done.3, bf16[512,256]{1,0:T(8,128)(2,1)} %copy-done.5, bf16[512,256]{1,0:T(8,128)(2,1)} %copy-done.4, bf16[512,256]{1,0:T(8,128)(2,1)} %copy-done.6, ...), custom_call_target="tpu_custom_call" | custom-call | flops 4026531840 | bytes 7864320 | tf_op jit(solution)/shard_map/project_0/pallas_call | solution.py:292
  105.9 0.6 copy-done.13
  106.5 0.1 copy-done.15
  106.6 0.1 copy-done.16
  106.7 0.1 copy-done.14
  106.8 0.7 copy-done.17
  107.5 9.1 %project_1.1 = bf16[8,1280,128]{2,1,0:T(8,128)(2,1)} custom-call(s32[6]{0:T(128)} %stack.27.at_ref, bf16[512,256]{1,0:T(8,128)(2,1)} %copy-done.12, bf16[512,256]{1,0:T(8,128)(2,1)} %copy-done.15, bf16[512,256]{1,0:T(8,128)(2,1)} %copy-done.16, bf16[512,256]{1,0:T(8,128)(2,1)} %copy-done.17, bf16[512,256]{1,0:T(8,128)(2,1)} %copy-done.13, ...), custom_call_target="tpu_custom_call" | custom-call | flops 2415919104 | bytes 4718592 | tf_op jit(solution)/shard_map/project_1/pallas_call | solution.py:292
  116.6 34.4 %all_to_all.26.refs_0_ = bf16[8,1280,128]{2,1,0:T(8,128)(2,1)S(1)} all-to-all(bf16[8,1280,128]{2,1,0:T(8,128)(2,1)} %project_1.1), channel_id=1, replica_groups=mesh['xl'=2,'yh'=2,'yl'=2,'z'=4,'xh'=2,'c'=2] {'xl','yh','yl'}, dimensions={0} | all-to-all | bytes 5242880 | tf_op jit(solution)/shard_map/all_to_all | solution.py:509
  151.0 5.0 %collective-permute-done.16.refs_1_ = bf16[8,1280,128]{2,1,0:T(8,128)(2,1)} collective-permute-done((bf16[8,1280,128]{2,1,0:T(8,128)(2,1)S(1)}, bf16[8,1280,128]{2,1,0:T(8,128)(2,1)}, u32[]{:S(2)}, u32[]{:S(2)}) %collective-permute-start.16) | collective-permute-done | bytes 2621472 | tf_op jit(solution)/shard_map/ppermute | solution.py:450
  156.0 23.7 %attend.1 = bf16[64,32,128]{2,1,0:T(8,128)(2,1)} custom-call(s32[6]{0:T(128)} %stack.27.at_ref, bf16[8,1280,128]{2,1,0:T(8,128)(2,1)} %copy-done, bf16[8,1280,128]{2,1,0:T(8,128)(2,1)} %collective-permute-done.16.refs_1_), custom_call_target="tpu_custom_call" | custom-call | tf_op jit(solution)/shard_map/attend/pallas_call | solution.py:426
  179.7 4.9 %all-to-all-start.4 = ((bf16[64,32,128]{2,1,0:T(8,128)(2,1)}), bf16[64,32,128]{2,1,0:T(8,128)(2,1)S(1)}, u32[]{:S(2)}, u32[]{:S(2)}) async-start(bf16[64,32,128]{2,1,0:T(8,128)(2,1)} %attend.1), calls=%async_computation.4 | async-start | bytes 1048576 | tf_op jit(solution)/shard_map/all_to_all | solution.py:513
  184.6 2.6 %collect.1 = bf16[64,4096]{1,0:T(8,128)(2,1)} custom-call(s32[6]{0:T(128)} %stack.27.at_ref, bf16[512,256]{1,0:T(8,128)(2,1)} %get-tuple-element.22.refs_0_, bf16[512,256]{1,0:T(8,128)(2,1)} %copy-done.3, bf16[512,256]{1,0:T(8,128)(2,1)} %copy-done.5, bf16[512,256]{1,0:T(8,128)(2,1)} %copy-done.7, bf16[512,256]{1,0:T(8,128)(2,1)} %copy-done.4, ...), custom_call_target="tpu_custom_call" | custom-call | tf_op jit(solution)/shard_map/collect/pallas_call | solution.py:217
  187.2 11.0 %all-to-all-done.4 = bf16[64,32,128]{2,1,0:T(8,128)(2,1)S(1)} async-done(((bf16[64,32,128]{2,1,0:T(8,128)(2,1)}), bf16[64,32,128]{2,1,0:T(8,128)(2,1)S(1)}, u32[]{:S(2)}, u32[]{:S(2)}) %all-to-all-start.4) | async-done | bytes 524320 | tf_op jit(solution)/shard_map/all_to_all | solution.py:513
  198.2 0.5 copy.17
  198.7 1.2 reshape.35
  (49 shorter events, 0.2 us)
Async XLA Ops:
  0.6 22.6 %collective-permute-start = (bf16[4096,2,384]{2,1,0:T(2,128)(2,1)}, bf16[4096,2,384]{2,1,0:T(2,128)(2,1)}, u32[]{:S(2)}, u32[]{:S(2)}) collective-permute-start(bf16[4096,2,384]{2,1,0:T(2,128)(2,1)} %param.17), channel_id=1, source_target_pairs={{0,1},{1,0},{2,3},{3,2},{4,5},{5,4},{6,7},{7,6},{8,9},{9,8},{10,11... | collective-permute-start | bytes 18874376 | tf_op jit(solution)/shard_map/ppermute | solution.py:450
  3.7 29.5 %all-to-all-start = ((bf16[128,2,16,128]{3,2,1,0:T(8,128)(2,1)}), bf16[128,2,16,128]{3,2,1,0:T(8,128)(2,1)S(1)}, u32[]{:S(2)}, u32[]{:S(2)}) async-start(bf16[128,2,16,128]{3,2,1,0:T(8,128)(2,1)} %bitcast.25), calls=%async_computation | async-start | bytes 2097152 | tf_op jit(solution)/shard_map/all_to_all | solution.py:474
  15.0 6.6 %copy-start.18 = (f32[4096]{0:T(1024)S(1)}, f32[4096]{0:T(1024)}, u32[]{:S(2)}) copy-start(f32[4096]{0:T(1024)} %param.16) | copy-start | bytes 49156
  33.2 4.2 %copy-start.1 = (bf16[128,2,16,128]{3,2,1,0:T(8,128)(2,1)}, bf16[128,2,16,128]{3,2,1,0:T(8,128)(2,1)S(1)}, u32[]{:S(2)}) copy-start(bf16[128,2,16,128]{3,2,1,0:T(8,128)(2,1)S(1)} %all-to-all-done.recv_ref) | copy-start | bytes 3145732
  33.2 16.5 %all-to-all-start.1 = ((bf16[16,64,256]{2,1,0:T(8,128)(2,1)}), bf16[16,64,256]{2,1,0:T(8,128)(2,1)S(1)}, u32[]{:S(2)}, u32[]{:S(2)}) async-start(bf16[16,64,256]{2,1,0:T(8,128)(2,1)} %get-tuple-element.19), calls=%async_computation.1 | async-start | bytes 1048576 | tf_op jit(solution)/shard_map/all_to_all | solution.py:485
  49.8 13.9 %copy-start.2 = (bf16[16,64,256]{2,1,0:T(8,128)(2,1)}, bf16[16,64,256]{2,1,0:T(8,128)(2,1)S(1)}, u32[]{:S(2)}) copy-start(bf16[16,64,256]{2,1,0:T(8,128)(2,1)S(1)} %all-to-all-done.1.gate_ref) | copy-start | bytes 1572868
  65.9 3.7 %collective-permute-start.1 = (bf16[512,256]{1,0:T(8,128)(2,1)}, bf16[512,256]{1,0:T(8,128)(2,1)S(1)}, u32[]{:S(2)}, u32[]{:S(2)}) collective-permute-start(bf16[512,256]{1,0:T(8,128)(2,1)} %get-tuple-element.23), channel_id=1, source_target_pairs={{0,1},{1,0},{2,3},{3,2},{4,5},{5,4},{6,7},{7,6},{8,9},{9,8},{10,11... | collective-permute-start | bytes 786440 | tf_op jit(solution)/shard_map/ppermute | solution.py:450
  65.9 9.3 %collective-permute-start.4 = (bf16[512,256]{1,0:T(8,128)(2,1)}, bf16[512,256]{1,0:T(8,128)(2,1)S(1)}, u32[]{:S(2)}, u32[]{:S(2)}) collective-permute-start(bf16[512,256]{1,0:T(8,128)(2,1)} %get-tuple-element.22.refs_0_), channel_id=1, source_target_pairs={{0,12},{1,13},{2,14},{3,15},{4,0},{5,1},{6,2},{7,3},{8,4},{9,5},{1... | collective-permute-start | bytes 786440 | tf_op jit(solution)/shard_map/ppermute | solution.py:450
  66.7 10.9 %collective-permute-start.2 = (bf16[512,256]{1,0:T(8,128)(2,1)}, bf16[512,256]{1,0:T(8,128)(2,1)S(1)}, u32[]{:S(2)}, u32[]{:S(2)}) collective-permute-start(bf16[512,256]{1,0:T(8,128)(2,1)} %get-tuple-element.22.refs_0_), channel_id=1, source_target_pairs={{0,2},{1,3},{2,0},{3,1},{4,6},{5,7},{6,4},{7,5},{8,10},{9,11},{10,... | collective-permute-start | bytes 786440 | tf_op jit(solution)/shard_map/ppermute | solution.py:450
  69.5 9.6 %collective-permute-start.13 = (bf16[512,256]{1,0:T(8,128)(2,1)}, bf16[512,256]{1,0:T(8,128)(2,1)S(1)}, u32[]{:S(2)}, u32[]{:S(2)}) collective-permute-start(bf16[512,256]{1,0:T(8,128)(2,1)} %get-tuple-element.22.refs_0_), channel_id=1, source_target_pairs={{0,4},{1,5},{2,6},{3,7},{4,8},{5,9},{6,10},{7,11},{8,12},{9,13},{1... | collective-permute-start | bytes 786440 | tf_op jit(solution)/shard_map/ppermute | solution.py:450
  69.5 25.4 %copy-start.3 = (bf16[512,256]{1,0:T(8,128)(2,1)}, bf16[512,256]{1,0:T(8,128)(2,1)S(1)}, u32[]{:S(2)}) copy-start(bf16[512,256]{1,0:T(8,128)(2,1)S(1)} %collective-permute-done.1.refs_1_) | copy-start | bytes 786436
  69.5 13.7 %collective-permute-start.3 = (bf16[512,256]{1,0:T(8,128)(2,1)S(1)}, bf16[512,256]{1,0:T(8,128)(2,1)S(1)}, u32[]{:S(2)}, u32[]{:S(2)}) collective-permute-start(bf16[512,256]{1,0:T(8,128)(2,1)S(1)} %collective-permute-done.1.refs_1_), channel_id=1, source_target_pairs={{0,2},{1,3},{2,0},{3,1},{4,6},{5,7},{6,4},{7,5},{8,10},{9,11},{10,... | collective-permute-start | bytes 786440 | tf_op jit(solution)/shard_map/ppermute | solution.py:450
  71.4 12.8 %collective-permute-start.5 = (bf16[512,256]{1,0:T(8,128)(2,1)S(1)}, bf16[512,256]{1,0:T(8,128)(2,1)S(1)}, u32[]{:S(2)}, u32[]{:S(2)}) collective-permute-start(bf16[512,256]{1,0:T(8,128)(2,1)S(1)} %collective-permute-done.1.refs_1_), channel_id=1, source_target_pairs={{0,12},{1,13},{2,14},{3,15},{4,0},{5,1},{6,2},{7,3},{8,4},{9,5},{1... | collective-permute-start | bytes 786440 | tf_op jit(solution)/shard_map/ppermute | solution.py:450
  75.2 19.8 %copy-start.4 = (bf16[512,256]{1,0:T(8,128)(2,1)}, bf16[512,256]{1,0:T(8,128)(2,1)S(1)}, u32[]{:S(2)}) copy-start(bf16[512,256]{1,0:T(8,128)(2,1)S(1)} %collective-permute-done.4.refs_4_.refs_3_) | copy-start | bytes 786436
  75.2 13.6 %collective-permute-start.6 = (bf16[512,256]{1,0:T(8,128)(2,1)S(1)}, bf16[512,256]{1,0:T(8,128)(2,1)S(1)}, u32[]{:S(2)}, u32[]{:S(2)}) collective-permute-start(bf16[512,256]{1,0:T(8,128)(2,1)S(1)} %collective-permute-done.4.refs_4_.refs_3_), channel_id=1, source_target_pairs={{0,2},{1,3},{2,0},{3,1},{4,6},{5,7},{6,4},{7,5},{8,10},{9,11},{10,... | collective-permute-start | bytes 786440 | tf_op jit(solution)/shard_map/ppermute | solution.py:450
  77.6 17.4 %copy-start.5 = (bf16[512,256]{1,0:T(8,128)(2,1)}, bf16[512,256]{1,0:T(8,128)(2,1)S(1)}, u32[]{:S(2)}) copy-start(bf16[512,256]{1,0:T(8,128)(2,1)S(1)} %collective-permute-done.2.refs_2_) | copy-start | bytes 786436
  77.6 12.4 %collective-permute-start.9 = (bf16[512,256]{1,0:T(8,128)(2,1)S(1)}, bf16[512,256]{1,0:T(8,128)(2,1)S(1)}, u32[]{:S(2)}, u32[]{:S(2)}) collective-permute-start(bf16[512,256]{1,0:T(8,128)(2,1)S(1)} %collective-permute-done.1.refs_1_), channel_id=1, source_target_pairs={{0,4},{1,5},{2,6},{3,7},{4,8},{5,9},{6,10},{7,11},{8,12},{9,13},{1... | collective-permute-start | bytes 786440 | tf_op jit(solution)/shard_map/ppermute | solution.py:450
  79.1 15.9 %copy-start.6 = (bf16[512,256]{1,0:T(8,128)(2,1)}, bf16[512,256]{1,0:T(8,128)(2,1)S(1)}, u32[]{:S(2)}) copy-start(bf16[512,256]{1,0:T(8,128)(2,1)S(1)} %collective-permute-done.13.refs_12_.refs_4_) | copy-start | bytes 786436
  79.1 11.0 %collective-permute-start.8 = (bf16[512,256]{1,0:T(8,128)(2,1)S(1)}, bf16[512,256]{1,0:T(8,128)(2,1)S(1)}, u32[]{:S(2)}, u32[]{:S(2)}) collective-permute-start(bf16[512,256]{1,0:T(8,128)(2,1)S(1)} %collective-permute-done.4.refs_4_.refs_3_), channel_id=1, source_target_pairs={{0,12},{1,13},{2,14},{3,15},{4,0},{5,1},{6,2},{7,3},{8,4},{9,5},{1... | collective-permute-start | bytes 786440 | tf_op jit(solution)/shard_map/ppermute | solution.py:450
  83.2 11.8 %copy-start.7 = (bf16[512,256]{1,0:T(8,128)(2,1)}, bf16[512,256]{1,0:T(8,128)(2,1)S(1)}, u32[]{:S(2)}) copy-start(bf16[512,256]{1,0:T(8,128)(2,1)S(1)} %collective-permute-done.3.refs_3_.refs_6_) | copy-start | bytes 786436
  83.2 9.3 %collective-permute-start.7 = (bf16[512,256]{1,0:T(8,128)(2,1)S(1)}, bf16[512,256]{1,0:T(8,128)(2,1)S(1)}, u32[]{:S(2)}, u32[]{:S(2)}) collective-permute-start(bf16[512,256]{1,0:T(8,128)(2,1)S(1)} %collective-permute-done.3.refs_3_.refs_6_), channel_id=1, source_target_pairs={{0,12},{1,13},{2,14},{3,15},{4,0},{5,1},{6,2},{7,3},{8,4},{9,5},{1... | collective-permute-start | bytes 786440 | tf_op jit(solution)/shard_map/ppermute | solution.py:450
  84.2 10.7 %copy-start.8 = (bf16[512,256]{1,0:T(8,128)(2,1)}, bf16[512,256]{1,0:T(8,128)(2,1)S(1)}, u32[]{:S(2)}) copy-start(bf16[512,256]{1,0:T(8,128)(2,1)S(1)} %collective-permute-done.5.refs_5_.refs_7_) | copy-start | bytes 786436
  84.3 21.6 %collective-permute-start.14 = (bf16[512,256]{1,0:T(8,128)(2,1)S(1)}, bf16[512,256]{1,0:T(8,128)(2,1)S(1)}, u32[]{:S(2)}, u32[]{:S(2)}) collective-permute-start(bf16[512,256]{1,0:T(8,128)(2,1)S(1)} %collective-permute-done.13.refs_12_.refs_4_), channel_id=1, source_target_pairs={{0,2},{1,3},{2,0},{3,1},{4,6},{5,7},{6,4},{7,5},{8,10},{9,11},{10,... | collective-permute-start | bytes 786440 | tf_op jit(solution)/shard_map/ppermute | solution.py:450
  88.8 6.2 %copy-start.9 = (bf16[512,256]{1,0:T(8,128)(2,1)}, bf16[512,256]{1,0:T(8,128)(2,1)S(1)}, u32[]{:S(2)}) copy-start(bf16[512,256]{1,0:T(8,128)(2,1)S(1)} %collective-permute-done.6.refs_6_.refs_9_) | copy-start | bytes 786436
  88.8 17.1 %collective-permute-start.15 = (bf16[512,256]{1,0:T(8,128)(2,1)S(1)}, bf16[512,256]{1,0:T(8,128)(2,1)S(1)}, u32[]{:S(2)}, u32[]{:S(2)}) collective-permute-start(bf16[512,256]{1,0:T(8,128)(2,1)S(1)} %collective-permute-done.3.refs_3_.refs_6_), channel_id=1, source_target_pairs={{0,4},{1,5},{2,6},{3,7},{4,8},{5,9},{6,10},{7,11},{8,12},{9,13},{1... | collective-permute-start | bytes 786440 | tf_op jit(solution)/shard_map/ppermute | solution.py:450
  90.0 5.0 %copy-start.10 = (bf16[512,256]{1,0:T(8,128)(2,1)}, bf16[512,256]{1,0:T(8,128)(2,1)S(1)}, u32[]{:S(2)}) copy-start(bf16[512,256]{1,0:T(8,128)(2,1)S(1)} %collective-permute-done.9.refs_13_.refs_8_) | copy-start | bytes 786436
  90.0 15.9 %collective-permute-start.10 = (bf16[512,256]{1,0:T(8,128)(2,1)S(1)}, bf16[512,256]{1,0:T(8,128)(2,1)S(1)}, u32[]{:S(2)}, u32[]{:S(2)}) collective-permute-start(bf16[512,256]{1,0:T(8,128)(2,1)S(1)} %collective-permute-done.9.refs_13_.refs_8_), channel_id=1, source_target_pairs={{0,4},{1,5},{2,6},{3,7},{4,8},{5,9},{6,10},{7,11},{8,12},{9,13},{1... | collective-permute-start | bytes 786440 | tf_op jit(solution)/shard_map/ppermute | solution.py:450
  90.1 5.0 %copy-start.11 = (bf16[512,256]{1,0:T(8,128)(2,1)}, bf16[512,256]{1,0:T(8,128)(2,1)S(1)}, u32[]{:S(2)}) copy-start(bf16[512,256]{1,0:T(8,128)(2,1)S(1)} %collective-permute-done.8.refs_8_.refs_5_) | copy-start | bytes 786436
  90.1 15.8 %collective-permute-start.11 = (bf16[512,256]{1,0:T(8,128)(2,1)S(1)}, bf16[512,256]{1,0:T(8,128)(2,1)S(1)}, u32[]{:S(2)}, u32[]{:S(2)}) collective-permute-start(bf16[512,256]{1,0:T(8,128)(2,1)S(1)} %collective-permute-done.8.refs_8_.refs_5_), channel_id=1, source_target_pairs={{0,2},{1,3},{2,0},{3,1},{4,6},{5,7},{6,4},{7,5},{8,10},{9,11},{10,... | collective-permute-start | bytes 786440 | tf_op jit(solution)/shard_map/ppermute | solution.py:450
  92.4 13.4 %copy-start.12 = (bf16[512,256]{1,0:T(8,128)(2,1)}, bf16[512,256]{1,0:T(8,128)(2,1)S(1)}, u32[]{:S(2)}) copy-start(bf16[512,256]{1,0:T(8,128)(2,1)S(1)} %collective-permute-done.7.refs_7_.refs_0_) | copy-start | bytes 786436
  92.4 13.5 %collective-permute-start.12 = (bf16[512,256]{1,0:T(8,128)(2,1)S(1)}, bf16[512,256]{1,0:T(8,128)(2,1)S(1)}, u32[]{:S(2)}, u32[]{:S(2)}) collective-permute-start(bf16[512,256]{1,0:T(8,128)(2,1)S(1)} %collective-permute-done.7.refs_7_.refs_0_), channel_id=1, source_target_pairs={{0,12},{1,13},{2,14},{3,15},{4,0},{5,1},{6,2},{7,3},{8,4},{9,5},{1... | collective-permute-start | bytes 786440 | tf_op jit(solution)/shard_map/ppermute | solution.py:450
  105.8 0.7 copy-start.13
  105.8 0.8 copy-start.15
  105.9 0.8 copy-start.16
  105.9 0.9 copy-start.14
  106.8 0.7 copy-start.17
  151.0 5.0 %copy-start = (bf16[8,1280,128]{2,1,0:T(8,128)(2,1)}, bf16[8,1280,128]{2,1,0:T(8,128)(2,1)S(1)}, u32[]{:S(2)}) copy-start(bf16[8,1280,128]{2,1,0:T(8,128)(2,1)S(1)} %all_to_all.26.refs_0_) | copy-start | bytes 7864324
  151.0 5.0 %collective-permute-start.16 = (bf16[8,1280,128]{2,1,0:T(8,128)(2,1)S(1)}, bf16[8,1280,128]{2,1,0:T(8,128)(2,1)}, u32[]{:S(2)}, u32[]{:S(2)}) collective-permute-start(bf16[8,1280,128]{2,1,0:T(8,128)(2,1)S(1)} %all_to_all.26.refs_0_), channel_id=1, source_target_pairs={{0,1},{1,0},{2,3},{3,2},{4,5},{5,4},{6,7},{7,6},{8,9},{9,8},{10,11... | collective-permute-start | bytes 7864328 | tf_op jit(solution)/shard_map/ppermute | solution.py:450
  179.7 18.5 %all-to-all-start.4 = ((bf16[64,32,128]{2,1,0:T(8,128)(2,1)}), bf16[64,32,128]{2,1,0:T(8,128)(2,1)S(1)}, u32[]{:S(2)}, u32[]{:S(2)}) async-start(bf16[64,32,128]{2,1,0:T(8,128)(2,1)} %attend.1), calls=%async_computation.4 | async-start | bytes 1048576 | tf_op jit(solution)/shard_map/all_to_all | solution.py:513
